TPU v7x, 32 devices: a whole 2x2x4 slice. The times are simulated.
32 devices in a mesh: tx: 4 (over y, x), ty: 2 (over core), ea: 4 (over z).
Axes of the slice: x: 2, y: 2, z: 4, core: 2. Of those that a mesh axis runs over, the one named last changes fastest.
Arguments:
- science: float32 [4, 512, 512], P('ea', 'tx', 'ty'), may hold values from -6 to 6
- inv_variance: float32 [4, 512, 512], P('ea', 'tx', 'ty'), may hold values from 0.25 to 4
- psf_taps: float32 [4, 9], P('ea'), may hold values from 0.05 to 1
- epoch_times: int32 [4], replicated, may hold values from 0 to 256, as said below
- velocities: int32 [24, 2], P('ea'), may hold values from -15 to 15
Outputs:
- likelihood: float32 [24, 512, 512], P('ea', 'tx', 'ty')
Inputs may be any that keep to these rules, and one draw needn't show every extreme that they name: `epoch_times`: the first epoch has time 0 and the last has time 256.
All inputs are finite; a program needn't handle non-finite values.
Results may differ from a plain program's by a relative error of at most 0.0053.
Values may be sent and summed in bfloat16 or wider, within the bound.
No kernel may reach another device: no remote copies, remote signals or barrier semaphores. Data moves between devices by JAX's collectives and lax.ppermute only.
A program may use at most 64 MiB of HBM per device.

v0:
```python
import jax
import jax.numpy as jnp
from jax import lax
from jax.sharding import PartitionSpec as P

REACH = 32
PR = 4


def extended(cells, sides, width):
    for axis, dim in sides:
        count = lax.axis_size(axis)
        ends = count - 1
        head = lax.slice_in_dim(cells, 0, width, axis=dim)
        tail = lax.slice_in_dim(cells, cells.shape[dim] - width, cells.shape[dim], axis=dim)
        cells = jnp.concatenate(
            [
                lax.ppermute(tail, axis, [(i, (i + 1) % count) for i in range(ends)]),
                cells,
                lax.ppermute(head, axis, [((i + 1) % count, i) for i in range(ends)]),
            ],
            axis=dim,
        )
    return cells


def blur(field, kern):
    count = kern.shape[1]
    rows = field.shape[1] - count + 1
    acc = kern[:, 0, None, None] * field[:, 0:rows, :]
    for k in range(1, count):
        acc = acc + kern[:, k, None, None] * field[:, k : k + rows, :]
    cols = acc.shape[2] - count + 1
    out = kern[:, 0, None, None] * acc[:, :, 0:cols]
    for k in range(1, count):
        out = out + kern[:, k, None, None] * acc[:, :, k : k + cols]
    return out


def spline_taps(speed, tvals):
    moved = jnp.floor_divide(speed * tvals, 8)
    whole = jnp.floor_divide(moved, 16)
    frac = (moved - 16 * whole).astype(jnp.float32) / 16.0
    frac2 = frac * frac
    frac3 = frac2 * frac
    weights = jnp.stack(
        [
            (1.0 - frac) ** 3 / 6.0,
            (3.0 * frac3 - 6.0 * frac2 + 4.0) / 6.0,
            (-3.0 * frac3 + 3.0 * frac2 + 3.0 * frac + 1.0) / 6.0,
            frac3 / 6.0,
        ],
        -1,
    )
    return (whole, weights.astype(jnp.bfloat16))


def band_matrix(whole, weights, count, span):
    target = lax.broadcasted_iota(jnp.int32, (1, count, span), 2)
    source = lax.broadcasted_iota(jnp.int32, (1, count, span), 1)
    offset = target - source - (REACH + whole - 1)[:, None, None]
    matrix = jnp.zeros((whole.shape[0], count, span), jnp.bfloat16)
    for a in range(4):
        matrix = matrix + jnp.where(
            offset == a, weights[:, a, None, None], jnp.zeros((), jnp.bfloat16)
        )
    return matrix


def stack_block(padded, tvals, velocities, out_rows, out_cols):
    pad_rows = padded.shape[2]
    pad_cols = padded.shape[3]

    def one_hyp(speed):
        whole_r, w_r = spline_taps(speed[0], tvals)
        whole_c, w_c = spline_taps(speed[1], tvals)
        row_band = band_matrix(whole_r, w_r, out_rows, pad_rows)
        col_band = band_matrix(whole_c, w_c, out_cols, pad_cols)
        moved_rows = jnp.einsum(
            "erp,eipk->eirk", row_band, padded, preferred_element_type=jnp.float32
        ).astype(jnp.bfloat16)
        return jnp.einsum("eirk,eck->irc", moved_rows, col_band, preferred_element_type=jnp.float32)

    return lax.map(one_hyp, velocities)


def shards(science, inv_variance, psf_taps, epoch_times, velocities):
    out_rows = science.shape[1]
    out_cols = science.shape[2]
    kern_p = psf_taps / jnp.sum(psf_taps, axis=1, keepdims=True)
    kern_q = kern_p * kern_p
    raw_pair = jnp.stack([science * inv_variance, inv_variance], 0)
    framed = extended(raw_pair, (("tx", 2), ("ty", 3)), PR)
    psi = blur(framed[0], kern_p).astype(jnp.bfloat16)
    phi = blur(framed[1], kern_q).astype(jnp.bfloat16)
    images = jnp.stack([psi, phi], 1)
    every_epoch = lax.all_gather(images, "ea", axis=0, tiled=True)
    padded = extended(every_epoch, (("tx", 2), ("ty", 3)), REACH)
    stacks = stack_block(padded, epoch_times, velocities, out_rows, out_cols)
    return stacks[:, 0] / jnp.sqrt(stacks[:, 1])


def solution(mesh):
    in_specs = (P("ea", "tx", "ty"), P("ea", "tx", "ty"), P("ea", None), P(), P("ea", None))
    out_specs = P("ea", "tx", "ty")
    return jax.shard_map(shards, mesh=mesh, in_specs=in_specs, out_specs=out_specs, check_vma=False)
```

profile of v0, /device:TPU:0, one launch (start us, length us, event | category | flops | bytes accessed | tf_op | source)
XLA Modules:
  0.0 106.6 jit_solution(10959145824867871440)
XLA Ops:
  1.7 4.8 %collective-permute-start = (f32[2,1,4,256]{3,2,1,0:T(4,128)S(1)}, f32[2,1,4,256]{3,2,1,0:T(4,128)S(1)}, u32[]{:S(2)}, u32[]{:S(2)}) collective-permute-start(f32[2,1,4,256]{3,2,1,0:T(4,128)S(1)} %get-tuple-element.184), channel_id=1, source_target_pairs={{0,8},{8,16},{16,24},{1,9},{9,17},{17,25},{2,10},{10,18},{18,26},{... | collective-permute-start | bytes 24584 | tf_op jit(solution)/shard_map/ppermute | solution.py:18
  6.6 1.3 %collective-permute-start.1 = (f32[2,1,4,256]{3,2,1,0:T(4,128)S(1)}, f32[2,1,4,256]{3,2,1,0:T(4,128)S(1)}, u32[]{:S(2)}, u32[]{:S(2)}) collective-permute-start(f32[2,1,4,256]{3,2,1,0:T(4,128)S(1)} %get-tuple-element.185), channel_id=1, source_target_pairs={{8,0},{16,8},{24,16},{9,1},{17,9},{25,17},{10,2},{18,10},{26,18},{... | collective-permute-start | bytes 24584 | tf_op jit(solution)/shard_map/ppermute | solution.py:20
  9.2 1.3 %fusion.125 = (f32[1,9]{1,0:T(1,128)S(1)}, f32[1,9]{1,0:T(1,128)S(1)}) fusion(f32[1,9]{1,0:T(1,128)} %param.9, f32[]{:T(128)} %reduce_sum.9), kind=kLoop, calls=%fused_computation.202 | loop fusion | flops 18 | bytes 112 | tf_op jit(solution)/shard_map/mul | solution.py:91
  10.5 1.7 %collective-permute-done.1 = f32[2,1,4,256]{3,2,1,0:T(4,128)S(1)} collective-permute-done((f32[2,1,4,256]{3,2,1,0:T(4,128)S(1)}, f32[2,1,4,256]{3,2,1,0:T(4,128)S(1)}, u32[]{:S(2)}, u32[]{:S(2)}) %collective-permute-start.1) | collective-permute-done | bytes 8224 | tf_op jit(solution)/shard_map/ppermute | solution.py:20
  13.2 1.3 %collective-permute-start.2 = (f32[2,1,136,4]{3,2,1,0:T(8,128)S(1)}, f32[2,1,136,4]{3,2,1,0:T(8,128)S(1)}, u32[]{:S(2)}, u32[]{:S(2)}) collective-permute-start(f32[2,1,136,4]{3,2,1,0:T(8,128)S(1)} %get-tuple-element.182), channel_id=1, source_target_pairs={{0,4},{1,5},{2,6},{3,7},{8,12},{9,13},{10,14},{11,15},{16,20},{17,... | collective-permute-start | bytes 13064 | tf_op jit(solution)/shard_map/ppermute | solution.py:18
  14.5 1.3 %collective-permute-start.3 = (f32[2,1,136,4]{3,2,1,0:T(8,128)S(1)}, f32[2,1,136,4]{3,2,1,0:T(8,128)S(1)}, u32[]{:S(2)}, u32[]{:S(2)}) collective-permute-start(f32[2,1,136,4]{3,2,1,0:T(8,128)S(1)} %get-tuple-element.183), channel_id=1, source_target_pairs={{4,0},{5,1},{6,2},{7,3},{12,8},{13,9},{14,10},{15,11},{20,16},{21,... | collective-permute-start | bytes 13064 | tf_op jit(solution)/shard_map/ppermute | solution.py:20
  18.0 6.0 %fusion.97 = f32[1,128,264]{2,1,0:T(8,128)S(1)} fusion(f32[1,136,264]{2,1,0:T(8,128)S(1)} %get-tuple-element.180, f32[]{:T(128)} %bitcast.29, f32[]{:T(128)} %bitcast.28, f32[]{:T(128)} %bitcast.27, f32[]{:T(128)} %bitcast.26, f32[]{:T(128)} %bitcast.25, f32[]{:T(128)} %bitcast.24, f32[]{:T(128)} %bitcast.23, f32[]{:T(128)} %bitcast.22, f32[]{:T(128)} %bitcast.18), kind=kLoop, calls=%fused_computation.140 | loop fusion | flops 574464 | bytes 1351716 | tf_op jit(solution)/shard_map/add | solution.py:32
  24.0 6.1 %fusion.123 = bf16[1,1,128,256]{3,2,1,0:T(8,128)(2,1)S(1)} fusion(f32[1,128,264]{2,1,0:T(8,128)S(1)} %fusion.97, f32[]{:T(128)} %bitcast.29, f32[]{:T(128)} %bitcast.28, f32[]{:T(128)} %bitcast.27, f32[]{:T(128)} %bitcast.26, f32[]{:T(128)} %bitcast.25, f32[]{:T(128)} %bitcast.24, f32[]{:T(128)} %bitcast.23, f32[]{:T(128)} %bitcast.22, f32[]{:T(128)} %bitcast.18), kind=kLoop, calls=%fused_computation.194 | loop fusion | flops 589824 | bytes 1245220 | tf_op jit(solution)/shard_map/stack | solution.py:96
  30.1 5.8 %fusion.89 = f32[1,128,264]{2,1,0:T(8,128)S(1)} fusion(f32[1,136,264]{2,1,0:T(8,128)S(1)} %get-tuple-element.181, f32[]{:T(128)} %bitcast.40, f32[]{:T(128)} %bitcast.39, f32[]{:T(128)} %bitcast.38, f32[]{:T(128)} %bitcast.37, f32[]{:T(128)} %bitcast.36, f32[]{:T(128)} %bitcast.35, f32[]{:T(128)} %bitcast.34, f32[]{:T(128)} %bitcast.33, f32[]{:T(128)} %bitcast.31), kind=kLoop, calls=%fused_computation.123 | loop fusion | flops 574464 | bytes 1351716 | tf_op jit(solution)/shard_map/add | solution.py:32
  35.9 6.0 %fusion.124 = bf16[1,1,128,256]{3,2,1,0:T(8,128)(2,1)S(1)} fusion(f32[1,128,264]{2,1,0:T(8,128)S(1)} %fusion.89, f32[]{:T(128)} %bitcast.40, f32[]{:T(128)} %bitcast.39, f32[]{:T(128)} %bitcast.38, f32[]{:T(128)} %bitcast.37, f32[]{:T(128)} %bitcast.36, f32[]{:T(128)} %bitcast.35, f32[]{:T(128)} %bitcast.34, f32[]{:T(128)} %bitcast.33, f32[]{:T(128)} %bitcast.31), kind=kLoop, calls=%fused_computation.195 | loop fusion | flops 589824 | bytes 1245220 | tf_op jit(solution)/shard_map/stack | solution.py:96
  41.9 16.2 %all_gather.3 = bf16[4,2,128,256]{3,2,1,0:T(8,128)(2,1)S(1)} all-gather(bf16[1,2,128,256]{3,2,1,0:T(8,128)(2,1)S(1)} %pad_maximum_fusion.3), channel_id=1, replica_groups=mesh['tx'=4,'ty'=2,'ea'=4] {'ea'}, dimensions={0}, use_global_device_ids=true | all-gather | bytes 655360 | tf_op jit(solution)/shard_map/all_gather | solution.py:97
  58.1 4.3 %collective-permute-start.4 = (bf16[4,2,32,256]{3,2,1,0:T(8,128)(2,1)S(1)}, bf16[4,2,32,256]{3,2,1,0:T(8,128)(2,1)S(1)}, u32[]{:S(2)}, u32[]{:S(2)}) collective-permute-start(bf16[4,2,32,256]{3,2,1,0:T(8,128)(2,1)S(1)} %get-tuple-element.179), channel_id=1, source_target_pairs={{0,8},{8,16},{16,24},{1,9},{9,17},{17,25},{2,10},{10,18},{18,26},{... | collective-permute-start | bytes 393224 | tf_op jit(solution)/shard_map/ppermute | solution.py:18
  62.4 1.3 %collective-permute-start.5 = (bf16[4,2,32,256]{3,2,1,0:T(8,128)(2,1)S(1)}, bf16[4,2,32,256]{3,2,1,0:T(8,128)(2,1)S(1)}, u32[]{:S(2)}, u32[]{:S(2)}) collective-permute-start(bf16[4,2,32,256]{3,2,1,0:T(8,128)(2,1)S(1)} %get-tuple-element.178), channel_id=1, source_target_pairs={{8,0},{16,8},{24,16},{9,1},{17,9},{25,17},{10,2},{18,10},{26,18},{... | collective-permute-start | bytes 393224 | tf_op jit(solution)/shard_map/ppermute | solution.py:20
  65.0 4.3 %collective-permute-done.5 = bf16[4,2,32,256]{3,2,1,0:T(8,128)(2,1)S(1)} collective-permute-done((bf16[4,2,32,256]{3,2,1,0:T(8,128)(2,1)S(1)}, bf16[4,2,32,256]{3,2,1,0:T(8,128)(2,1)S(1)}, u32[]{:S(2)}, u32[]{:S(2)}) %collective-permute-start.5) | collective-permute-done | bytes 131104 | tf_op jit(solution)/shard_map/ppermute | solution.py:20
  69.5 1.3 %collective-permute-start.6 = (bf16[4,2,192,32]{3,2,1,0:T(8,128)(2,1)S(1)}, bf16[4,2,192,32]{3,2,1,0:T(8,128)(2,1)S(1)}, u32[]{:S(2)}, u32[]{:S(2)}) collective-permute-start(bf16[4,2,192,32]{3,2,1,0:T(8,128)(2,1)S(1)} %get-tuple-element.176), channel_id=1, source_target_pairs={{0,4},{1,5},{2,6},{3,7},{8,12},{9,13},{10,14},{11,15},{16,20},{17,... | collective-permute-start | bytes 294920 | tf_op jit(solution)/shard_map/ppermute | solution.py:18
  70.8 1.3 %collective-permute-start.7 = (bf16[4,2,192,32]{3,2,1,0:T(8,128)(2,1)S(1)}, bf16[4,2,192,32]{3,2,1,0:T(8,128)(2,1)}, u32[]{:S(2)}, u32[]{:S(2)}) collective-permute-start(bf16[4,2,192,32]{3,2,1,0:T(8,128)(2,1)S(1)} %get-tuple-element.177), channel_id=1, source_target_pairs={{4,0},{5,1},{6,2},{7,3},{12,8},{13,9},{14,10},{15,11},{20,16},{21,... | collective-permute-start | bytes 294920 | tf_op jit(solution)/shard_map/ppermute | solution.py:20
  72.9 1.7 %collective-permute-done.7 = bf16[4,2,192,32]{3,2,1,0:T(8,128)(2,1)} collective-permute-done((bf16[4,2,192,32]{3,2,1,0:T(8,128)(2,1)S(1)}, bf16[4,2,192,32]{3,2,1,0:T(8,128)(2,1)}, u32[]{:S(2)}, u32[]{:S(2)}) %collective-permute-start.7) | collective-permute-done | bytes 98336 | tf_op jit(solution)/shard_map/ppermute | solution.py:20
  74.6 1.8 %pad_maximum_fusion = bf16[4,2,192,320]{3,2,1,0:T(8,128)(2,1)S(1)} fusion(bf16[4,2,192,32]{3,2,1,0:T(8,128)(2,1)} %collective-permute-done.7, bf16[4,2,192,256]{3,2,1,0:T(8,128)(2,1)S(1)} %constant_dynamic-update-slice_fusion, bf16[4,2,192,32]{3,2,1,0:T(8,128)(2,1)} %copy-done.1), kind=kLoop, calls=%fused_computation.116 | loop fusion | flops 2949120 | bytes 1966080 | tf_op jit(solution)/shard_map/concatenate | solution.py:16
  76.4 29.2 %while.15 = (s32[]{:T(128)}, f32[6,2,128,256]{3,2,0,1:T(8,128)S(1)}, s32[6,2]{0,1:T(2,128)S(1)}, s32[4]{0:T(128)S(1)}, bf16[4,2,192,320]{3,2,1,0:T(8,128)(2,1)S(1)}, /*index=5*/s32[]{:T(128)}) while((s32[]{:T(128)}, f32[6,2,128,256]{3,2,0,1:T(8,128)S(1)}, s32[6,2]{0,1:T(2,128)S(1)}, s32[4]{0:T(128)S(1)}, ...), condition=%wide.region_2.3_spmd, body=%wide.region_1.2_spmd.sunk | while | flops 299639520 | bytes 2331965 | solution.py:84
  77.0 1.3 %fusion.144 = (bf16[4]{0:T(256)(128)(2,1)S(1)}, s32[4,1]{0,1:T(1,128)S(1)}, bf16[4]{0:T(256)(128)(2,1)S(1)}, s32[4,1]{0,1:T(1,128)S(1)}) fusion(s32[4]{0:T(128)S(1)} %get-tuple-element.287, s32[]{:T(128)} %bitcast.108, s32[]{:T(128)} %bitcast.109), kind=kLoop, calls=%fused_computation.90.clone.1 | loop fusion | flops 320 | bytes 72 | tf_op jit(solution)/shard_map/while/body/eval_jaxpr/jit(_where)/broadcast_in_dim | solution.py:64
  78.3 1.3 %fusion.143 = (s32[4]{0:T(128)S(1)}, s32[4]{0:T(128)S(1)}) fusion(s32[4]{0:T(128)S(1)} %get-tuple-element.287, s32[]{:T(128)} %bitcast.108, s32[]{:T(128)} %bitcast.109), kind=kLoop, calls=%fused_computation.107.clone.1 | loop fusion | flops 256 | bytes 56 | tf_op jit(solution)/shard_map/while/body/eval_jaxpr/sub | solution.py:61
  79.7 1.6 %fusion.145 = f32[6,2,128,256]{3,2,0,1:T(8,128)S(1)} fusion(f32[6,2,128,256]{3,2,0,1:T(8,128)S(1)} %get-tuple-element.279, s32[]{:T(128)} %get-tuple-element.278, bf16[4,2,192,320]{3,2,1,0:T(8,128)(2,1)S(1)} %get-tuple-element.288, s32[4]{0:T(128)S(1)} %get-tuple-element.260, s32[256,320]{0,1:T(8,128)S(1)} %iota_subtract_fusion.4, ...), kind=kOutput, calls=%fused_computation.17.clone.1 | convolution fusion | flops 299532288 | bytes 1905668 | tf_op jit(solution)/shard_map/while/body/eval_jaxpr/eirk,eck->irc/dot_general | solution.py:82
  81.9 1.3 %fusion.144 = (bf16[4]{0:T(256)(128)(2,1)S(1)}, s32[4,1]{0,1:T(1,128)S(1)}, bf16[4]{0:T(256)(128)(2,1)S(1)}, s32[4,1]{0,1:T(1,128)S(1)}) fusion(s32[4]{0:T(128)S(1)} %get-tuple-element.287, s32[]{:T(128)} %bitcast.108, s32[]{:T(128)} %bitcast.109), kind=kLoop, calls=%fused_computation.90.clone.1 | loop fusion | flops 320 | bytes 72 | tf_op jit(solution)/shard_map/while/body/eval_jaxpr/jit(_where)/broadcast_in_dim | solution.py:64
  84.6 1.6 %fusion.145 = f32[6,2,128,256]{3,2,0,1:T(8,128)S(1)} fusion(f32[6,2,128,256]{3,2,0,1:T(8,128)S(1)} %get-tuple-element.279, s32[]{:T(128)} %get-tuple-element.278, bf16[4,2,192,320]{3,2,1,0:T(8,128)(2,1)S(1)} %get-tuple-element.288, s32[4]{0:T(128)S(1)} %get-tuple-element.260, s32[256,320]{0,1:T(8,128)S(1)} %iota_subtract_fusion.4, ...), kind=kOutput, calls=%fused_computation.17.clone.1 | convolution fusion | flops 299532288 | bytes 1905668 | tf_op jit(solution)/shard_map/while/body/eval_jaxpr/eirk,eck->irc/dot_general | solution.py:82
  86.8 1.3 %fusion.144 = (bf16[4]{0:T(256)(128)(2,1)S(1)}, s32[4,1]{0,1:T(1,128)S(1)}, bf16[4]{0:T(256)(128)(2,1)S(1)}, s32[4,1]{0,1:T(1,128)S(1)}) fusion(s32[4]{0:T(128)S(1)} %get-tuple-element.287, s32[]{:T(128)} %bitcast.108, s32[]{:T(128)} %bitcast.109), kind=kLoop, calls=%fused_computation.90.clone.1 | loop fusion | flops 320 | bytes 72 | tf_op jit(solution)/shard_map/while/body/eval_jaxpr/jit(_where)/broadcast_in_dim | solution.py:64
  89.4 1.6 %fusion.145 = f32[6,2,128,256]{3,2,0,1:T(8,128)S(1)} fusion(f32[6,2,128,256]{3,2,0,1:T(8,128)S(1)} %get-tuple-element.279, s32[]{:T(128)} %get-tuple-element.278, bf16[4,2,192,320]{3,2,1,0:T(8,128)(2,1)S(1)} %get-tuple-element.288, s32[4]{0:T(128)S(1)} %get-tuple-element.260, s32[256,320]{0,1:T(8,128)S(1)} %iota_subtract_fusion.4, ...), kind=kOutput, calls=%fused_computation.17.clone.1 | convolution fusion | flops 299532288 | bytes 1905668 | tf_op jit(solution)/shard_map/while/body/eval_jaxpr/eirk,eck->irc/dot_general | solution.py:82
  91.6 1.3 %fusion.144 = (bf16[4]{0:T(256)(128)(2,1)S(1)}, s32[4,1]{0,1:T(1,128)S(1)}, bf16[4]{0:T(256)(128)(2,1)S(1)}, s32[4,1]{0,1:T(1,128)S(1)}) fusion(s32[4]{0:T(128)S(1)} %get-tuple-element.287, s32[]{:T(128)} %bitcast.108, s32[]{:T(128)} %bitcast.109), kind=kLoop, calls=%fused_computation.90.clone.1 | loop fusion | flops 320 | bytes 72 | tf_op jit(solution)/shard_map/while/body/eval_jaxpr/jit(_where)/broadcast_in_dim | solution.py:64
  94.3 1.6 %fusion.145 = f32[6,2,128,256]{3,2,0,1:T(8,128)S(1)} fusion(f32[6,2,128,256]{3,2,0,1:T(8,128)S(1)} %get-tuple-element.279, s32[]{:T(128)} %get-tuple-element.278, bf16[4,2,192,320]{3,2,1,0:T(8,128)(2,1)S(1)} %get-tuple-element.288, s32[4]{0:T(128)S(1)} %get-tuple-element.260, s32[256,320]{0,1:T(8,128)S(1)} %iota_subtract_fusion.4, ...), kind=kOutput, calls=%fused_computation.17.clone.1 | convolution fusion | flops 299532288 | bytes 1905668 | tf_op jit(solution)/shard_map/while/body/eval_jaxpr/eirk,eck->irc/dot_general | solution.py:82
  96.5 1.3 %fusion.144 = (bf16[4]{0:T(256)(128)(2,1)S(1)}, s32[4,1]{0,1:T(1,128)S(1)}, bf16[4]{0:T(256)(128)(2,1)S(1)}, s32[4,1]{0,1:T(1,128)S(1)}) fusion(s32[4]{0:T(128)S(1)} %get-tuple-element.287, s32[]{:T(128)} %bitcast.108, s32[]{:T(128)} %bitcast.109), kind=kLoop, calls=%fused_computation.90.clone.1 | loop fusion | flops 320 | bytes 72 | tf_op jit(solution)/shard_map/while/body/eval_jaxpr/jit(_where)/broadcast_in_dim | solution.py:64
  99.2 1.6 %fusion.145 = f32[6,2,128,256]{3,2,0,1:T(8,128)S(1)} fusion(f32[6,2,128,256]{3,2,0,1:T(8,128)S(1)} %get-tuple-element.279, s32[]{:T(128)} %get-tuple-element.278, bf16[4,2,192,320]{3,2,1,0:T(8,128)(2,1)S(1)} %get-tuple-element.288, s32[4]{0:T(128)S(1)} %get-tuple-element.260, s32[256,320]{0,1:T(8,128)S(1)} %iota_subtract_fusion.4, ...), kind=kOutput, calls=%fused_computation.17.clone.1 | convolution fusion | flops 299532288 | bytes 1905668 | tf_op jit(solution)/shard_map/while/body/eval_jaxpr/eirk,eck->irc/dot_general | solution.py:82
  101.4 1.3 %fusion.144 = (bf16[4]{0:T(256)(128)(2,1)S(1)}, s32[4,1]{0,1:T(1,128)S(1)}, bf16[4]{0:T(256)(128)(2,1)S(1)}, s32[4,1]{0,1:T(1,128)S(1)}) fusion(s32[4]{0:T(128)S(1)} %get-tuple-element.287, s32[]{:T(128)} %bitcast.108, s32[]{:T(128)} %bitcast.109), kind=kLoop, calls=%fused_computation.90.clone.1 | loop fusion | flops 320 | bytes 72 | tf_op jit(solution)/shard_map/while/body/eval_jaxpr/jit(_where)/broadcast_in_dim | solution.py:64
  104.0 1.6 %fusion.145 = f32[6,2,128,256]{3,2,0,1:T(8,128)S(1)} fusion(f32[6,2,128,256]{3,2,0,1:T(8,128)S(1)} %get-tuple-element.279, s32[]{:T(128)} %get-tuple-element.278, bf16[4,2,192,320]{3,2,1,0:T(8,128)(2,1)S(1)} %get-tuple-element.288, s32[4]{0:T(128)S(1)} %get-tuple-element.260, s32[256,320]{0,1:T(8,128)S(1)} %iota_subtract_fusion.4, ...), kind=kOutput, calls=%fused_computation.17.clone.1 | convolution fusion | flops 299532288 | bytes 1905668 | tf_op jit(solution)/shard_map/while/body/eval_jaxpr/eirk,eck->irc/dot_general | solution.py:82
  (64 shorter events, 19.9 us)
Async XLA Ops:
  0.0 17.7 %copy-start = (f32[1,128,256]{2,1,0:T(8,128)S(1)}, f32[1,128,256]{2,1,0:T(8,128)}, u32[]{:S(2)}) copy-start(f32[1,128,256]{2,1,0:T(8,128)} %param.8) | copy-start | bytes 393220
  1.7 8.7 %collective-permute-start = (f32[2,1,4,256]{3,2,1,0:T(4,128)S(1)}, f32[2,1,4,256]{3,2,1,0:T(4,128)S(1)}, u32[]{:S(2)}, u32[]{:S(2)}) collective-permute-start(f32[2,1,4,256]{3,2,1,0:T(4,128)S(1)} %get-tuple-element.184), channel_id=1, source_target_pairs={{0,8},{8,16},{16,24},{1,9},{9,17},{17,25},{2,10},{10,18},{18,26},{... | collective-permute-start | bytes 24584 | tf_op jit(solution)/shard_map/ppermute | solution.py:18
  6.6 5.5 %collective-permute-start.1 = (f32[2,1,4,256]{3,2,1,0:T(4,128)S(1)}, f32[2,1,4,256]{3,2,1,0:T(4,128)S(1)}, u32[]{:S(2)}, u32[]{:S(2)}) collective-permute-start(f32[2,1,4,256]{3,2,1,0:T(4,128)S(1)} %get-tuple-element.185), channel_id=1, source_target_pairs={{8,0},{16,8},{24,16},{9,1},{17,9},{25,17},{10,2},{18,10},{26,18},{... | collective-permute-start | bytes 24584 | tf_op jit(solution)/shard_map/ppermute | solution.py:20
  13.2 3.3 %collective-permute-start.2 = (f32[2,1,136,4]{3,2,1,0:T(8,128)S(1)}, f32[2,1,136,4]{3,2,1,0:T(8,128)S(1)}, u32[]{:S(2)}, u32[]{:S(2)}) collective-permute-start(f32[2,1,136,4]{3,2,1,0:T(8,128)S(1)} %get-tuple-element.182), channel_id=1, source_target_pairs={{0,4},{1,5},{2,6},{3,7},{8,12},{9,13},{10,14},{11,15},{16,20},{17,... | collective-permute-start | bytes 13064 | tf_op jit(solution)/shard_map/ppermute | solution.py:18
  14.5 3.3 %collective-permute-start.3 = (f32[2,1,136,4]{3,2,1,0:T(8,128)S(1)}, f32[2,1,136,4]{3,2,1,0:T(8,128)S(1)}, u32[]{:S(2)}, u32[]{:S(2)}) collective-permute-start(f32[2,1,136,4]{3,2,1,0:T(8,128)S(1)} %get-tuple-element.183), channel_id=1, source_target_pairs={{4,0},{5,1},{6,2},{7,3},{12,8},{13,9},{14,10},{15,11},{20,16},{21,... | collective-permute-start | bytes 13064 | tf_op jit(solution)/shard_map/ppermute | solution.py:20
  58.1 6.8 %collective-permute-start.4 = (bf16[4,2,32,256]{3,2,1,0:T(8,128)(2,1)S(1)}, bf16[4,2,32,256]{3,2,1,0:T(8,128)(2,1)S(1)}, u32[]{:S(2)}, u32[]{:S(2)}) collective-permute-start(bf16[4,2,32,256]{3,2,1,0:T(8,128)(2,1)S(1)} %get-tuple-element.179), channel_id=1, source_target_pairs={{0,8},{8,16},{16,24},{1,9},{9,17},{17,25},{2,10},{10,18},{18,26},{... | collective-permute-start | bytes 393224 | tf_op jit(solution)/shard_map/ppermute | solution.py:18
  62.4 6.9 %collective-permute-start.5 = (bf16[4,2,32,256]{3,2,1,0:T(8,128)(2,1)S(1)}, bf16[4,2,32,256]{3,2,1,0:T(8,128)(2,1)S(1)}, u32[]{:S(2)}, u32[]{:S(2)}) collective-permute-start(bf16[4,2,32,256]{3,2,1,0:T(8,128)(2,1)S(1)} %get-tuple-element.178), channel_id=1, source_target_pairs={{8,0},{16,8},{24,16},{9,1},{17,9},{25,17},{10,2},{18,10},{26,18},{... | collective-permute-start | bytes 393224 | tf_op jit(solution)/shard_map/ppermute | solution.py:20
  69.5 2.7 %collective-permute-start.6 = (bf16[4,2,192,32]{3,2,1,0:T(8,128)(2,1)S(1)}, bf16[4,2,192,32]{3,2,1,0:T(8,128)(2,1)S(1)}, u32[]{:S(2)}, u32[]{:S(2)}) collective-permute-start(bf16[4,2,192,32]{3,2,1,0:T(8,128)(2,1)S(1)} %get-tuple-element.176), channel_id=1, source_target_pairs={{0,4},{1,5},{2,6},{3,7},{8,12},{9,13},{10,14},{11,15},{16,20},{17,... | collective-permute-start | bytes 294920 | tf_op jit(solution)/shard_map/ppermute | solution.py:18
  70.8 3.7 %collective-permute-start.7 = (bf16[4,2,192,32]{3,2,1,0:T(8,128)(2,1)S(1)}, bf16[4,2,192,32]{3,2,1,0:T(8,128)(2,1)}, u32[]{:S(2)}, u32[]{:S(2)}) collective-permute-start(bf16[4,2,192,32]{3,2,1,0:T(8,128)(2,1)S(1)} %get-tuple-element.177), channel_id=1, source_target_pairs={{4,0},{5,1},{6,2},{7,3},{12,8},{13,9},{14,10},{15,11},{20,16},{21,... | collective-permute-start | bytes 294920 | tf_op jit(solution)/shard_map/ppermute | solution.py:20
  72.1 4.3 %copy-start.2 = (s32[4]{0:T(128)S(1)}, s32[4]{0:T(128)}, u32[]{:S(2)}) copy-start(s32[4]{0:T(128)} %param.10) | copy-start | bytes 52
  72.1 4.3 %copy-start.3 = (s32[6,2]{0,1:T(2,128)S(1)}, s32[6,2]{0,1:T(2,128)}, u32[]{:S(2)}) copy-start(s32[6,2]{0,1:T(2,128)} %param.11) | copy-start | bytes 148
  72.2 0.7 copy-start.1
where the time goes:
time: 108 us; the launch traced here: 107 us
  other arithmetic  48 us (44%)
  starting transfers between devices  16.9 us (16%)
  blocking collectives  16.2 us (15%)
  waiting for transfers between devices  10.1 us (9%)
  matrix products  9.44 us (9%)
  local copies, waits for them, and re-layouts  5.51 us (5%)
    all_gather x1, blocking collectives, shards(): every_epoch = lax.all_gather(images, 'ea', axis=0, tiled=True)  16.2 us
    another operation x3, other arithmetic, shards(): images = jnp.stack([psi, phi], 1)  12.1 us
    add x2, other arithmetic, blur(): acc = acc + kern[:, k, None, None] * field[:, k:k + rows, :]  11.8 us
    ppermute x4, starting transfers between devices, extended(): lax.ppermute(tail, axis, [(i, (i + 1) % count) for i in range(ends)])  11.7 us
    dot_general x6, matrix products, one_hyp(): jnp.einsum('eirk,eck->irc', moved_rows, col_band, preferred_element_type=...  9.44 us
    ppermute x4, waiting for transfers between devices, extended(): lax.ppermute(head, axis, [((i + 1) % count, i) for i in range(ends)])  8.86 us
    sub x18, other arithmetic, band_matrix(): offset = target - source - (REACH + whole - 1)[:, None, None]  7.97 us
    broadcast_in_dim x12, other arithmetic, band_matrix(): jnp.where(offset == a, weights[:, a, None, None], jnp.zeros((), jnp.bfloa...  7.85 us
  transfers between devices with their start and end apart: 8, of which 5 were waited for; matrix products, arithmetic and copies ran while one was open for 3% of the time, Pallas kernels for 0%

commit v1 on v0

v1 whole, which is shorter than its diff:
```python
import functools

import jax
import jax.numpy as jnp
from jax import lax
from jax.experimental import pallas as pl
from jax.experimental.pallas import tpu as pltpu
from jax.sharding import PartitionSpec as P

REACH = 32
PR = 4
RIM = 40
HALF = 64
GROUP = 4
VMEM_LIMIT = 60 * 1024 * 1024


def spline_taps(speed, tvals):
    moved = jnp.floor_divide(speed * tvals, 8)
    whole = jnp.floor_divide(moved, 16)
    frac = (moved - 16 * whole).astype(jnp.float32) / 16.0
    frac2 = frac * frac
    frac3 = frac2 * frac
    weights = jnp.stack(
        [
            (1.0 - frac) ** 3 / 6.0,
            (3.0 * frac3 - 6.0 * frac2 + 4.0) / 6.0,
            (-3.0 * frac3 + 3.0 * frac2 + 3.0 * frac + 1.0) / 6.0,
            frac3 / 6.0,
        ],
        -1,
    )
    return (whole, weights.astype(jnp.bfloat16))


def pack_kernel(sci_ref, iv_ref, taps_ref, out_ref):
    rows, cols = sci_ref.shape[1:]
    iv = iv_ref[0]
    out_ref[0:rows, :] = (sci_ref[0] * iv).astype(jnp.bfloat16)
    out_ref[rows : 2 * rows, :] = iv.astype(jnp.bfloat16)
    taps = taps_ref[...]
    p = taps / jnp.sum(taps, axis=1, keepdims=True)
    p = jnp.concatenate([p, jnp.zeros((1, cols - p.shape[1]), jnp.float32)], axis=1)
    hi = p.astype(jnp.bfloat16).astype(jnp.float32)
    mid = (p - hi).astype(jnp.bfloat16).astype(jnp.float32)
    low = p - hi - mid
    row = lax.broadcasted_iota(jnp.int32, (16, cols), 0)
    block = jnp.where(row == 0, hi, jnp.where(row == 1, mid, jnp.where(row == 2, low, 0.0)))
    out_ref[2 * rows :, :] = block.astype(jnp.bfloat16)


def strip_kernel(rows, *refs):
    count = len(refs) - 2
    up_ref, down_ref = refs[count:]
    for k in range(count):
        both = [refs[k][i * rows : (i + 1) * rows, :].astype(jnp.float32) for i in range(2)]
        up_ref[k] = jnp.concatenate([x[:RIM] for x in both], 0).astype(jnp.bfloat16)
        down_ref[k] = jnp.concatenate([x[rows - RIM :] for x in both], 0).astype(jnp.bfloat16)


def band(shape, count, first, weights, row_axis):
    source = lax.broadcasted_iota(jnp.int32, shape, 1 - row_axis)
    target = lax.broadcasted_iota(jnp.int32, shape, row_axis)
    d = source - target - first
    d = jnp.where(d >= count, d - count, d)
    acc = jnp.zeros(shape, jnp.float32)
    for a, w in enumerate(weights):
        acc = jnp.where(d == a, w, acc)
    return acc.astype(jnp.bfloat16)


def shift_kernel(hyps, rows, rim_rows, rim_cols, whole_ref, w_ref, rb_ref, cb_ref):
    def one(index, carry):
        e = index // hyps
        h = index % hyps
        at = index * 2
        ws = [w_ref[at * 4 + a] for a in range(4)]
        rb_ref[e, pl.ds(pl.multiple_of(h * rows, rows), rows), :] = band(
            (rows, rim_rows), rim_rows, whole_ref[at] - 1, ws, 0
        )
        ws = [w_ref[at * 4 + 4 + a] for a in range(4)]
        cb_ref[h, e] = band((rim_cols, 128), rim_cols, whole_ref[at + 1] - 1, ws, 1)
        return carry

    lax.fori_loop(0, rb_ref.shape[0] * hyps, one, 0)


def circle(position, count, last):
    return jnp.where(position < last, position, position - count)


def blur_kernel(rows, cols, place_ref, *refs):
    count = len(refs) - 2
    br_ref, bc_ref = refs[count:]
    out_rows, in_rows = br_ref.shape[2:]
    all_cols = bc_ref.shape[2]
    low_row = place_ref[0]
    high_row = place_ref[1]
    low_col = place_ref[2]
    high_col = place_ref[3]
    n = circle(lax.broadcasted_iota(jnp.int32, (out_rows, in_rows), 0), out_rows, rows + REACH)
    k = circle(lax.broadcasted_iota(jnp.int32, (out_rows, in_rows), 1), in_rows, rows + HALF)
    d_r = jnp.where((n >= low_row) & (n < high_row), k - n + PR, -1)
    k = circle(lax.broadcasted_iota(jnp.int32, (all_cols, all_cols), 0), all_cols, cols + HALF)
    n = circle(lax.broadcasted_iota(jnp.int32, (all_cols, all_cols), 1), all_cols, cols + HALF)
    d_c = jnp.where((n >= low_col) & (n < high_col), k - n + PR, -1)
    for e in range(count):
        block = refs[e][2 * rows : 2 * rows + 16, :].astype(jnp.float32)
        p = block[0:1] + block[1:2] + block[2:3]
        q = p * p
        for d, ref in ((d_r, br_ref), (d_c, bc_ref)):
            acc_p = jnp.zeros(d.shape, jnp.float32)
            acc_q = acc_p
            for t in range(2 * PR + 1):
                hit = d == t
                acc_p = jnp.where(hit, p[:, t : t + 1], acc_p)
                acc_q = jnp.where(hit, q[:, t : t + 1], acc_q)
            ref[e, 0] = acc_p.astype(jnp.bfloat16)
            ref[e, 1] = acc_q.astype(jnp.bfloat16)


def dot(a, b):
    return jnp.dot(a, b, preferred_element_type=jnp.float32)


def stack_kernel(slots, hyps, rows, cols, first, final, side_ref, *refs):
    refs = list(refs)
    tiles = [refs.pop(0) for _ in range(slots)]
    above, below, side_tile, side_above, side_below, br, bc, rb, cb = [refs.pop(0) for _ in range(9)]
    acc_in = None if first else refs.pop(0)
    out, moved = refs
    rim_rows = br.shape[2]
    in_rows = br.shape[3]
    lane = lax.broadcasted_iota(jnp.int32, (1, 128), 1)
    keep = jnp.where(lane < HALF, side_ref[0], side_ref[1]) > 0
    for e in range(slots):
        pair = []
        for i in range(2):
            at = slice(i * rows, (i + 1) * rows)
            rim = slice(i * RIM, (i + 1) * RIM)
            left = jnp.concatenate(
                [
                    tiles[e][at, :].astype(jnp.float32),
                    below[e].astype(jnp.float32)[rim],
                    jnp.zeros((in_rows - rows - 2 * RIM, cols), jnp.float32),
                    above[e].astype(jnp.float32)[rim],
                ],
                0,
            )
            right = jnp.concatenate(
                [
                    side_tile[e, at, :].astype(jnp.float32),
                    side_below[e].astype(jnp.float32)[rim],
                    jnp.zeros((in_rows - rows - 2 * RIM, 128), jnp.float32),
                    side_above[e].astype(jnp.float32)[rim],
                ],
                0,
            )
            field = jnp.concatenate([left, jnp.where(keep, right, 0.0)], 1).astype(jnp.bfloat16)
            half = dot(br[e, i], field).astype(jnp.bfloat16)
            pair.append(dot(half, bc[e, i]).astype(jnp.bfloat16))
        both = jnp.concatenate(pair, 1)
        wide = pair[0].shape[1]
        for h in range(hyps):
            m = dot(rb[e, h * rows : (h + 1) * rows, :], both).astype(jnp.bfloat16)
            moved[h, 0:rows, e * wide : (e + 1) * wide] = m[:, :wide]
            moved[h, rows : 2 * rows, e * wide : (e + 1) * wide] = m[:, wide:]
    for h in range(hyps):
        cols_band = []
        for e in range(slots):
            c = cb[h, e]
            ends = c.shape[0] - 128
            cols_band.append(
                jnp.concatenate([c, jnp.concatenate([c[ends:], c[:ends]], 0)], 1)
            )
        total = dot(moved[h], jnp.concatenate(cols_band, 0))
        if acc_in is not None:
            total = total + acc_in[h]
        if final:
            out[h] = total[:rows] / jnp.sqrt(total[rows:])
        else:
            out[h] = total


VMEM = pl.BlockSpec(memory_space=pltpu.VMEM)
SMEM = pl.BlockSpec(memory_space=pltpu.SMEM)
PARAMS = pltpu.CompilerParams(vmem_limit_bytes=VMEM_LIMIT)


def call(kernel, specs, shapes, *args, scratch=(), flops=0, bytes_accessed=0):
    single = not isinstance(shapes, (list, tuple))
    return pl.pallas_call(
        kernel,
        out_shape=shapes,
        in_specs=specs,
        out_specs=VMEM if single else [VMEM] * len(shapes),
        scratch_shapes=list(scratch),
        compiler_params=PARAMS,
        cost_estimate=pl.CostEstimate(
            flops=flops, bytes_accessed=bytes_accessed, transcendentals=0
        ),
    )(*args)


def bf16(*shape):
    return jax.ShapeDtypeStruct(shape, jnp.bfloat16)


def side_swap(x):
    count = lax.axis_size("ty")
    me = lax.axis_index("ty")
    head = x[..., :128]
    tail = x[..., x.shape[-1] - 128 :]
    if count == 2:
        return lax.ppermute(jnp.where(me == 0, tail, head), "ty", [(0, 1), (1, 0)])
    after = lax.ppermute(head, "ty", [(i + 1, i) for i in range(count - 1)])
    before = lax.ppermute(tail, "ty", [(i, i + 1) for i in range(count - 1)])
    lane = lax.broadcasted_iota(jnp.int32, x.shape[:-1] + (128,), x.ndim - 1)
    return jnp.where(lane < HALF, after, before)


def shards(science, inv_variance, psf_taps, epoch_times, velocities):
    rows, cols = science.shape[1:]
    hyps = velocities.shape[0]
    epochs = lax.axis_size("ea")
    tx = lax.axis_size("tx")
    ty = lax.axis_size("ty")
    here_x = lax.axis_index("tx")
    here_y = lax.axis_index("ty")
    here_e = lax.axis_index("ea")
    rim_rows = rows + 2 * REACH
    in_rows = rows + 2 * HALF
    all_cols = cols + 2 * HALF
    slots = min(GROUP, epochs)

    own = call(pack_kernel, [VMEM] * 3, bf16(2 * rows + 16, cols), science, inv_variance, psf_taps)
    payload = [own] + [
        lax.ppermute(own, "ea", [(i, i ^ k) for i in range(epochs)]) for k in range(1, epochs)
    ]

    order = here_e ^ jnp.arange(epochs, dtype=jnp.int32)
    times = epoch_times[order]
    whole, weights = spline_taps(velocities[None, :, :], times[:, None, None])
    weights = weights.astype(jnp.float32)

    low_row = jnp.where(here_x == 0, 0, -REACH)
    high_row = jnp.where(here_x == tx - 1, rows, rows + REACH)
    low_col = jnp.where(here_y == 0, 0, -REACH)
    high_col = jnp.where(here_y == ty - 1, cols, cols + REACH)
    place = jnp.stack([low_row, high_row, low_col, high_col]).astype(jnp.int32)
    side = jnp.stack([here_y < ty - 1, here_y > 0]).astype(jnp.int32)

    def group(tiles, whole, weights, total, final):
        up, down = call(
            functools.partial(strip_kernel, rows),
            [VMEM] * slots,
            [bf16(slots, 2 * RIM, cols)] * 2,
            *tiles,
        )
        above = lax.ppermute(down, "tx", [(i, i + 1) for i in range(tx - 1)])
        below = lax.ppermute(up, "tx", [(i + 1, i) for i in range(tx - 1)])
        side_tile = side_swap(jnp.stack(tiles))
        side_above = side_swap(above)
        side_below = side_swap(below)
        rb, cb = call(
            functools.partial(shift_kernel, hyps, rows, rim_rows, all_cols),
            [SMEM] * 2,
            [bf16(slots, hyps * rows, rim_rows), bf16(hyps, slots, all_cols, 128)],
            whole.reshape(-1),
            weights.reshape(-1),
        )
        br, bc = call(
            functools.partial(blur_kernel, rows, cols),
            [SMEM] + [VMEM] * slots,
            [bf16(slots, 2, rim_rows, in_rows), bf16(slots, 2, all_cols, all_cols)],
            place,
            *tiles,
        )
        args = [side, *tiles, above, below, side_tile, side_above, side_below, br, bc, rb, cb]
        if total is not None:
            args.append(total)
        shape = (hyps, rows, cols) if final else (hyps, 2 * rows, cols)
        return call(
            functools.partial(stack_kernel, slots, hyps, rows, cols, total is None, final),
            [SMEM] + [VMEM] * (len(args) - 1),
            jax.ShapeDtypeStruct(shape, jnp.float32),
            *args,
            scratch=[pltpu.VMEM((hyps, 2 * rows, slots * all_cols), jnp.bfloat16)],
        )

    if epochs == slots:
        return group(payload, whole, weights, None, True)

    def step(total, xs):
        tiles, whole, weights = xs
        return group([tiles[k] for k in range(slots)], whole, weights, total, False), None

    split = lambda x: x.reshape((epochs // slots, slots) + x.shape[1:])
    zeros = jnp.zeros((hyps, 2 * rows, cols), jnp.float32)
    total, _ = lax.scan(step, zeros, (split(jnp.stack(payload)), split(whole), split(weights)))
    return total[:, :rows] / jnp.sqrt(total[:, rows:])


def solution(mesh):
    in_specs = (P("ea", "tx", "ty"), P("ea", "tx", "ty"), P("ea", None), P(), P("ea", None))
    out_specs = P("ea", "tx", "ty")
    return jax.shard_map(shards, mesh=mesh, in_specs=in_specs, out_specs=out_specs, check_vma=False)
```

time: 108 us -> 53.4 us (0.49)
  the two profiles are of different devices: /device:TPU:0 before, /device:TPU:1 now
where the time goes in v1:
time: 53.4 us; the launch traced here: 53.1 us
  Pallas kernels  27.5 us (51%)
  starting transfers between devices  13.1 us (25%)
  local copies, waits for them, and re-layouts  4.37 us (8%)
  waiting for transfers between devices  4.06 us (8%)
  other arithmetic  3.86 us (7%)
    pallas_call x5, Pallas kernels, call(): pl.pallas_call(kernel, out_shape=shapes, in_specs=specs, out_specs=VMEM i...  27.5 us
    ppermute x3, starting transfers between devices, shards(): lax.ppermute(own, 'ea', [(i, i ^ k) for i in range(epochs)])  4.44 us
    ppermute x3, starting transfers between devices, side_swap(): return lax.ppermute(jnp.where(me == 0, tail, head), 'ty', [(0, 1), (1, 0)])  4.25 us
    ppermute x1, waiting for transfers between devices, group(): below = lax.ppermute(up, 'tx', [(i + 1, i) for i in range(tx - 1)])  3.38 us
    ppermute x1, starting transfers between devices, group(): above = lax.ppermute(down, 'tx', [(i, i + 1) for i in range(tx - 1)])  3.11 us
    unnamed x19, local copies, waits for them, and re-layouts  2.82 us
    ppermute x1, starting transfers between devices, group(): below = lax.ppermute(up, 'tx', [(i + 1, i) for i in range(tx - 1)])  1.29 us
    another operation x1, other arithmetic, group(): side_tile = side_swap(jnp.stack(tiles))  1.18 us
  transfers between devices with their start and end apart: 8, of which 2 were waited for; matrix products, arithmetic and copies ran while one was open for 12% of the time, Pallas kernels for 27%

profile of v1, /device:TPU:1, one launch (start us, length us, event | category | flops | bytes accessed | tf_op | source)
XLA Modules:
  0.0 53.1 jit_solution(13893292267989019691)
XLA Ops:
  0.0 1.7 %shard_map.55.refs_0_ = bf16[272,256]{1,0:T(8,128)(2,1)} custom-call(f32[1,128,256]{2,1,0:T(8,128)} %sci_ref.1, f32[1,128,256]{2,1,0:T(8,128)} %iv_ref.1, f32[1,9]{1,0:T(1,128)} %taps_ref.1), custom_call_target="tpu_custom_call" | custom-call | tf_op jit(solution)/shard_map/pallas_call | solution.py:192
  1.7 4.2 %collective-permute-start.2 = (bf16[272,256]{1,0:T(8,128)(2,1)}, bf16[272,256]{1,0:T(8,128)(2,1)S(1)}, u32[]{:S(2)}, u32[]{:S(2)}) collective-permute-start(bf16[272,256]{1,0:T(8,128)(2,1)} %shard_map.55.refs_0_), channel_id=1, source_target_pairs={{0,3},{1,2},{2,1},{3,0},{4,7},{5,6},{6,5},{7,4},{8,11},{9,10},{10,... | collective-permute-start | bytes 417800 | tf_op jit(solution)/shard_map/ppermute | solution.py:238
  5.9 0.3 collective-permute-start
  6.2 0.8 %copy.10 = s32[6,2]{1,0:T(8,128)S(1)} copy(s32[6,2]{0,1:T(2,128)} %param.9) | data formatting | bytes 96 | tf_op args[4]
  7.0 0.6 %gather_fusion = s32[4]{0:T(128)S(1)} fusion(s32[4]{0:T(128)S(1)} %copy-done, s32[1024]{0:T(1024)S(1)} %pad_clamp_fusion), kind=kCustom, calls=%fused_computation | custom fusion | bytes 48 | tf_op jit(solution)/shard_map/gather | solution.py:242
  7.6 0.8 %fusion.15 = (bf16[4,6,2,1]{1,0,3,2:T(4,128)(2,1)S(1)}, bf16[4,6,2,1]{1,0,3,2:T(4,128)(2,1)S(1)}, bf16[4,6,2,1]{1,0,3,2:T(4,128)(2,1)S(1)}, bf16[4,6,2,1]{1,0,3,2:T(4,128)(2,1)S(1)}) fusion(s32[4]{0:T(128)S(1)} %gather_fusion, s32[6,2]{0,1:T(2,128)} %param.9), kind=kLoop, calls=%fused_computation.37 | loop fusion | flops 2784 | bytes 448 | tf_op jit(solution)/shard_map/convert.1
  8.4 0.1 broadcast_multiply_fusion
  8.4 0.1 mul.159
  8.5 0.5 %and_select_fusion.whole_ref = s32[48]{0:T(128)} fusion(s32[48]{0:T(128)S(1)} %mul.159), kind=kLoop, calls=%fused_computation.46 | loop fusion | flops 1440 | bytes 384 | tf_op jit(solution)/shard_map/jit(floor_divide)/jit(_where)/select_n | solution.py:20
  9.1 0.1 copy.11
  9.3 0.7 %reshape.189.w_ref = f32[192]{0:T(256)} reshape(f32[4,6,2,4]{3,2,1,0:T(2,128)S(1)} %copy.11) | data formatting | bytes 1536 | tf_op jit(solution)/shard_map/convert_element_type | solution.py:244
  9.9 6.2 %shard_map.58 = (bf16[4,768,192]{2,1,0:T(8,128)(2,1)}, bf16[6,4,384,128]{3,2,1,0:T(8,128)(2,1)}) custom-call(s32[48]{0:T(128)} %and_select_fusion.whole_ref, f32[192]{0:T(256)} %reshape.189.w_ref), custom_call_target="tpu_custom_call" | custom-call | tf_op jit(solution)/shard_map/pallas_call | solution.py:192
  16.2 0.6 %add_convert_fusion.side_ref = s32[2]{0:T(128)} fusion(pred[1]{0:T(512)(128)(4,1)} %bitcast.1, pred[1]{0:T(512)(128)(4,1)} %bitcast), kind=kLoop, calls=%fused_computation.45 | loop fusion | flops 4 | bytes 10 | tf_op jit(solution)/shard_map/convert_element_type | solution.py:251
  16.8 0.0 collective-permute-done.2.refs_3_
  16.8 0.7 %collective-permute-done.1.refs_2_ = bf16[272,256]{1,0:T(8,128)(2,1)S(1)} collective-permute-done((bf16[272,256]{1,0:T(8,128)(2,1)}, bf16[272,256]{1,0:T(8,128)(2,1)S(1)}, u32[]{:S(2)}, u32[]{:S(2)}) %collective-permute-start.1) | collective-permute-done | bytes 139296 | tf_op jit(solution)/shard_map/ppermute | solution.py:238
  17.5 0.0 collective-permute-done.refs_1_
  17.5 0.7 %copy-done.2 = bf16[272,256]{1,0:T(8,128)(2,1)} copy-done((bf16[272,256]{1,0:T(8,128)(2,1)}, bf16[272,256]{1,0:T(8,128)(2,1)S(1)}, u32[]{:S(2)}) %copy-start.2) | copy-done | bytes 139288
  18.2 0.7 %copy-done.3 = bf16[272,256]{1,0:T(8,128)(2,1)} copy-done((bf16[272,256]{1,0:T(8,128)(2,1)}, bf16[272,256]{1,0:T(8,128)(2,1)S(1)}, u32[]{:S(2)}) %copy-start.3) | copy-done | bytes 139288
  18.8 1.9 %shard_map.56 = (bf16[4,80,256]{2,1,0:T(8,128)(2,1)}, bf16[4,80,256]{2,1,0:T(8,128)(2,1)}) custom-call(bf16[272,256]{1,0:T(8,128)(2,1)} %shard_map.55.refs_0_, bf16[272,256]{1,0:T(8,128)(2,1)} %copy-done.3, bf16[272,256]{1,0:T(8,128)(2,1)} %copy-done.2, bf16[272,256]{1,0:T(8,128)(2,1)} %copy-done.1), custom_call_target="tpu_custom_call" | custom-call | tf_op jit(solution)/shard_map/pallas_call | solution.py:192
  20.7 3.1 %collective-permute-start.3 = (bf16[4,80,256]{2,1,0:T(8,128)(2,1)}, bf16[4,80,256]{2,1,0:T(8,128)(2,1)S(1)}, u32[]{:S(2)}, u32[]{:S(2)}) collective-permute-start(bf16[4,80,256]{2,1,0:T(8,128)(2,1)} %get-tuple-element.11), channel_id=1, source_target_pairs={{0,8},{8,16},{16,24},{1,9},{9,17},{17,25},{2,10},{10,18},{18,26},{... | collective-permute-start | bytes 491528 | tf_op jit(solution)/shard_map/ppermute | solution.py:260
  23.8 1.3 %collective-permute-start.4 = (bf16[4,80,256]{2,1,0:T(8,128)(2,1)}, bf16[4,80,256]{2,1,0:T(8,128)(2,1)S(1)}, u32[]{:S(2)}, u32[]{:S(2)}) collective-permute-start(bf16[4,80,256]{2,1,0:T(8,128)(2,1)} %get-tuple-element.12), channel_id=1, source_target_pairs={{8,0},{16,8},{24,16},{9,1},{17,9},{25,17},{10,2},{18,10},{26,18},{... | collective-permute-start | bytes 491528 | tf_op jit(solution)/shard_map/ppermute | solution.py:261
  25.1 1.2 %pad_maximum_fusion = bf16[4,272,256]{2,1,0:T(8,128)(2,1)S(1)} fusion(bf16[1,272,256]{2,1,0:T(8,128)(2,1)} %bitcast.13, bf16[1,272,256]{2,1,0:T(8,128)(2,1)} %bitcast.14, bf16[1,272,256]{2,1,0:T(8,128)(2,1)} %bitcast.15, bf16[1,272,256]{2,1,0:T(8,128)(2,1)} %bitcast.12), kind=kLoop, calls=%fused_computation.1 | loop fusion | flops 835584 | bytes 1114112 | tf_op jit(solution)/shard_map/stack | solution.py:262
  26.3 1.7 %collective-permute-start.5 = (bf16[4,272,128]{2,1,0:T(8,128)(2,1)S(1)}, bf16[4,272,128]{2,1,0:T(8,128)(2,1)S(1)}, u32[]{:S(2)}, u32[]{:S(2)}) collective-permute-start(bf16[4,272,128]{2,1,0:T(8,128)(2,1)S(1)} %slice_select_fusion), channel_id=1, source_target_pairs={{0,4},{4,0},{1,5},{5,1},{2,6},{6,2},{3,7},{7,3},{8,12},{12,8},{9,1... | collective-permute-start | bytes 835592 | tf_op jit(solution)/shard_map/ppermute | solution.py:215
  28.0 0.6 %collective-permute-start.6 = (bf16[4,80,128]{2,1,0:T(8,128)(2,1)S(1)}, bf16[4,80,128]{2,1,0:T(8,128)(2,1)S(1)}, u32[]{:S(2)}, u32[]{:S(2)}) collective-permute-start(bf16[4,80,128]{2,1,0:T(8,128)(2,1)S(1)} %slice_select_fusion.2), channel_id=1, source_target_pairs={{0,4},{4,0},{1,5},{5,1},{2,6},{6,2},{3,7},{7,3},{8,12},{12,8},{9,1... | collective-permute-start | bytes 245768 | tf_op jit(solution)/shard_map/ppermute | solution.py:215
  28.6 3.4 %collective-permute-done.4.refs_5_ = bf16[4,80,256]{2,1,0:T(8,128)(2,1)S(1)} collective-permute-done((bf16[4,80,256]{2,1,0:T(8,128)(2,1)}, bf16[4,80,256]{2,1,0:T(8,128)(2,1)S(1)}, u32[]{:S(2)}, u32[]{:S(2)}) %collective-permute-start.4) | collective-permute-done | bytes 163872 | tf_op jit(solution)/shard_map/ppermute | solution.py:261
  32.0 2.0 %collective-permute-start.7 = (bf16[4,80,128]{2,1,0:T(8,128)(2,1)S(1)}, bf16[4,80,128]{2,1,0:T(8,128)(2,1)S(1)}, u32[]{:S(2)}, u32[]{:S(2)}) collective-permute-start(bf16[4,80,128]{2,1,0:T(8,128)(2,1)S(1)} %slice_select_fusion.1), channel_id=1, source_target_pairs={{0,4},{4,0},{1,5},{5,1},{2,6},{6,2},{3,7},{7,3},{8,12},{12,8},{9,1... | collective-permute-start | bytes 245768 | tf_op jit(solution)/shard_map/ppermute | solution.py:215
  34.0 0.6 %pad_add_fusion.place_ref = s32[4]{0:T(128)} fusion(s32[1]{0:T(128)} %bitcast.9, s32[1]{0:T(128)} %bitcast.8, s32[1]{0:T(128)} %bitcast.7, s32[1]{0:T(128)} %bitcast.6), kind=kLoop, calls=%fused_computation.55 | loop fusion | flops 12 | bytes 32 | tf_op jit(solution)/shard_map/stack | solution.py:250
  34.6 8.2 %shard_map.57 = (bf16[4,2,192,256]{3,2,1,0:T(8,128)(2,1)}, bf16[4,2,384,384]{3,2,1,0:T(8,128)(2,1)}) custom-call(s32[4]{0:T(128)} %pad_add_fusion.place_ref, bf16[272,256]{1,0:T(8,128)(2,1)} %shard_map.55.refs_0_, bf16[272,256]{1,0:T(8,128)(2,1)} %copy-done.3, bf16[272,256]{1,0:T(8,128)(2,1)} %copy-done.2, bf16[272,256]{1,0:T(8,128)(2,1)} %copy-done.1), custom_call_target="tpu_custom_call" | custom-call | tf_op jit(solution)/shard_map/pallas_call | solution.py:192
  42.9 0.6 %copy-done.7 = bf16[4,80,128]{2,1,0:T(8,128)(2,1)} copy-done((bf16[4,80,128]{2,1,0:T(8,128)(2,1)}, bf16[4,80,128]{2,1,0:T(8,128)(2,1)S(1)}, u32[]{:S(2)}) %copy-start.7) | copy-done | bytes 81944
  43.4 0.0 copy-done.8
  43.5 0.1 copy-done.6
  43.6 9.5 %shard_map.59 = f32[6,128,256]{2,1,0:T(8,128)} custom-call(s32[2]{0:T(128)} %add_convert_fusion.side_ref, bf16[272,256]{1,0:T(8,128)(2,1)} %shard_map.55.refs_0_, bf16[272,256]{1,0:T(8,128)(2,1)} %copy-done.3, bf16[272,256]{1,0:T(8,128)(2,1)} %copy-done.2, bf16[272,256]{1,0:T(8,128)(2,1)} %copy-done.1, bf16[4,80,256]{2,1,0:T(8,128)(2,1)} %copy-done.4, ...), custom_call_target="tpu_custom_call" | custom-call | tf_op jit(solution)/shard_map/pallas_call | solution.py:192
  (24 shorter events, 0.1 us)
Async XLA Ops:
  0.0 7.0 %copy-start = (s32[4]{0:T(128)S(1)}, s32[4]{0:T(128)}, u32[]{:S(2)}) copy-start(s32[4]{0:T(128)} %param.8) | copy-start | bytes 52
  1.7 15.1 %collective-permute-start.2 = (bf16[272,256]{1,0:T(8,128)(2,1)}, bf16[272,256]{1,0:T(8,128)(2,1)S(1)}, u32[]{:S(2)}, u32[]{:S(2)}) collective-permute-start(bf16[272,256]{1,0:T(8,128)(2,1)} %shard_map.55.refs_0_), channel_id=1, source_target_pairs={{0,3},{1,2},{2,1},{3,0},{4,7},{5,6},{6,5},{7,4},{8,11},{9,10},{10,... | collective-permute-start | bytes 417800 | tf_op jit(solution)/shard_map/ppermute | solution.py:238
  5.9 11.6 %collective-permute-start.1 = (bf16[272,256]{1,0:T(8,128)(2,1)}, bf16[272,256]{1,0:T(8,128)(2,1)S(1)}, u32[]{:S(2)}, u32[]{:S(2)}) collective-permute-start(bf16[272,256]{1,0:T(8,128)(2,1)} %shard_map.55.refs_0_), channel_id=1, source_target_pairs={{0,2},{1,3},{2,0},{3,1},{4,6},{5,7},{6,4},{7,5},{8,10},{9,11},{10,... | collective-permute-start | bytes 417800 | tf_op jit(solution)/shard_map/ppermute | solution.py:238
  5.9 11.6 %collective-permute-start = (bf16[272,256]{1,0:T(8,128)(2,1)}, bf16[272,256]{1,0:T(8,128)(2,1)S(1)}, u32[]{:S(2)}, u32[]{:S(2)}) collective-permute-start(bf16[272,256]{1,0:T(8,128)(2,1)} %shard_map.55.refs_0_), channel_id=1, source_target_pairs={{0,1},{1,0},{2,3},{3,2},{4,5},{5,4},{6,7},{7,6},{8,9},{9,8},{10,11... | collective-permute-start | bytes 417800 | tf_op jit(solution)/shard_map/ppermute | solution.py:238
  16.8 0.7 %copy-start.1 = (bf16[272,256]{1,0:T(8,128)(2,1)}, bf16[272,256]{1,0:T(8,128)(2,1)S(1)}, u32[]{:S(2)}) copy-start(bf16[272,256]{1,0:T(8,128)(2,1)S(1)} %collective-permute-done.2.refs_3_) | copy-start | bytes 417796
  17.5 0.7 %copy-start.2 = (bf16[272,256]{1,0:T(8,128)(2,1)}, bf16[272,256]{1,0:T(8,128)(2,1)S(1)}, u32[]{:S(2)}) copy-start(bf16[272,256]{1,0:T(8,128)(2,1)S(1)} %collective-permute-done.1.refs_2_) | copy-start | bytes 417796
  18.1 0.7 %copy-start.3 = (bf16[272,256]{1,0:T(8,128)(2,1)}, bf16[272,256]{1,0:T(8,128)(2,1)S(1)}, u32[]{:S(2)}) copy-start(bf16[272,256]{1,0:T(8,128)(2,1)S(1)} %collective-permute-done.refs_1_) | copy-start | bytes 417796
  20.7 7.4 %collective-permute-start.3 = (bf16[4,80,256]{2,1,0:T(8,128)(2,1)}, bf16[4,80,256]{2,1,0:T(8,128)(2,1)S(1)}, u32[]{:S(2)}, u32[]{:S(2)}) collective-permute-start(bf16[4,80,256]{2,1,0:T(8,128)(2,1)} %get-tuple-element.11), channel_id=1, source_target_pairs={{0,8},{8,16},{16,24},{1,9},{9,17},{17,25},{2,10},{10,18},{18,26},{... | collective-permute-start | bytes 491528 | tf_op jit(solution)/shard_map/ppermute | solution.py:260
  23.8 8.2 %collective-permute-start.4 = (bf16[4,80,256]{2,1,0:T(8,128)(2,1)}, bf16[4,80,256]{2,1,0:T(8,128)(2,1)S(1)}, u32[]{:S(2)}, u32[]{:S(2)}) collective-permute-start(bf16[4,80,256]{2,1,0:T(8,128)(2,1)} %get-tuple-element.12), channel_id=1, source_target_pairs={{8,0},{16,8},{24,16},{9,1},{17,9},{25,17},{10,2},{18,10},{26,18},{... | collective-permute-start | bytes 491528 | tf_op jit(solution)/shard_map/ppermute | solution.py:261
  26.3 16.5 %collective-permute-start.5 = (bf16[4,272,128]{2,1,0:T(8,128)(2,1)S(1)}, bf16[4,272,128]{2,1,0:T(8,128)(2,1)S(1)}, u32[]{:S(2)}, u32[]{:S(2)}) collective-permute-start(bf16[4,272,128]{2,1,0:T(8,128)(2,1)S(1)} %slice_select_fusion), channel_id=1, source_target_pairs={{0,4},{4,0},{1,5},{5,1},{2,6},{6,2},{3,7},{7,3},{8,12},{12,8},{9,1... | collective-permute-start | bytes 835592 | tf_op jit(solution)/shard_map/ppermute | solution.py:215
  28.0 14.8 %copy-start.4 = (bf16[4,80,256]{2,1,0:T(8,128)(2,1)}, bf16[4,80,256]{2,1,0:T(8,128)(2,1)S(1)}, u32[]{:S(2)}) copy-start(bf16[4,80,256]{2,1,0:T(8,128)(2,1)S(1)} %collective-permute-done.3.refs_4_) | copy-start | bytes 491524
  28.0 14.8 %collective-permute-start.6 = (bf16[4,80,128]{2,1,0:T(8,128)(2,1)S(1)}, bf16[4,80,128]{2,1,0:T(8,128)(2,1)S(1)}, u32[]{:S(2)}, u32[]{:S(2)}) collective-permute-start(bf16[4,80,128]{2,1,0:T(8,128)(2,1)S(1)} %slice_select_fusion.2), channel_id=1, source_target_pairs={{0,4},{4,0},{1,5},{5,1},{2,6},{6,2},{3,7},{7,3},{8,12},{12,8},{9,1... | collective-permute-start | bytes 245768 | tf_op jit(solution)/shard_map/ppermute | solution.py:215
  32.0 10.8 %copy-start.5 = (bf16[4,80,256]{2,1,0:T(8,128)(2,1)}, bf16[4,80,256]{2,1,0:T(8,128)(2,1)S(1)}, u32[]{:S(2)}) copy-start(bf16[4,80,256]{2,1,0:T(8,128)(2,1)S(1)} %collective-permute-done.4.refs_5_) | copy-start | bytes 491524
  32.0 10.8 %collective-permute-start.7 = (bf16[4,80,128]{2,1,0:T(8,128)(2,1)S(1)}, bf16[4,80,128]{2,1,0:T(8,128)(2,1)S(1)}, u32[]{:S(2)}, u32[]{:S(2)}) collective-permute-start(bf16[4,80,128]{2,1,0:T(8,128)(2,1)S(1)} %slice_select_fusion.1), channel_id=1, source_target_pairs={{0,4},{4,0},{1,5},{5,1},{2,6},{6,2},{3,7},{7,3},{8,12},{12,8},{9,1... | collective-permute-start | bytes 245768 | tf_op jit(solution)/shard_map/ppermute | solution.py:215
  42.8 0.6 %copy-start.7 = (bf16[4,80,128]{2,1,0:T(8,128)(2,1)}, bf16[4,80,128]{2,1,0:T(8,128)(2,1)S(1)}, u32[]{:S(2)}) copy-start(bf16[4,80,128]{2,1,0:T(8,128)(2,1)S(1)} %collective-permute-done.6.refs_7_) | copy-start | bytes 245764
  42.8 0.7 %copy-start.8 = (bf16[4,80,128]{2,1,0:T(8,128)(2,1)}, bf16[4,80,128]{2,1,0:T(8,128)(2,1)S(1)}, u32[]{:S(2)}) copy-start(bf16[4,80,128]{2,1,0:T(8,128)(2,1)S(1)} %collective-permute-done.7.refs_8_) | copy-start | bytes 245764
  42.8 0.7 %copy-start.6 = (bf16[4,272,128]{2,1,0:T(8,128)(2,1)}, bf16[4,272,128]{2,1,0:T(8,128)(2,1)S(1)}, u32[]{:S(2)}) copy-start(bf16[4,272,128]{2,1,0:T(8,128)(2,1)S(1)} %collective-permute-done.5.refs_6_) | copy-start | bytes 835588

commit v2 on v0

v2 whole, which is shorter than its diff:
```python
import functools

import jax
import jax.numpy as jnp
from jax import lax
from jax.experimental import pallas as pl
from jax.experimental.pallas import tpu as pltpu
from jax.sharding import PartitionSpec as P

REACH = 32
PR = 4
RIM = REACH + PR
GROUP = 4
VMEM_LIMIT = 24 * 1024 * 1024
STRIP_FLOPS = 10_000_000
SHIFT_FLOPS = 4_000_000_000
BLUR_FLOPS = 4_000_000_000
STACK_FLOPS = 2_000_000_000


def spline_taps(speed, time):
    moved = (speed * time) >> 3
    frac = (moved & 15).astype(jnp.float32) * (1.0 / 16.0)
    rest = 1.0 - frac
    frac2 = frac * frac
    frac3 = frac2 * frac
    sixth = 1.0 / 6.0
    weights = [
        rest * rest * rest * sixth,
        (3.0 * frac3 - 6.0 * frac2 + 4.0) * sixth,
        (-3.0 * frac3 + 3.0 * frac2 + 3.0 * frac + 1.0) * sixth,
        frac3 * sixth,
    ]
    return moved >> 4, weights


def pack_kernel(sci_hbm, iv_hbm, taps_hbm, out_ref, sci_ref, iv_ref, taps_ref, sems):
    copies = [
        pltpu.make_async_copy(src, dst, sems.at[i])
        for i, (src, dst) in enumerate(
            [(sci_hbm, sci_ref), (iv_hbm, iv_ref), (taps_hbm, taps_ref)]
        )
    ]
    for copy in copies:
        copy.start()
    for copy in copies:
        copy.wait()
    rows, cols = sci_ref.shape[1:]
    iv = iv_ref[0]
    out_ref[0:rows, :] = (sci_ref[0] * iv).astype(jnp.bfloat16)
    out_ref[rows : 2 * rows, :] = iv.astype(jnp.bfloat16)
    taps = taps_ref[...]
    p = taps / jnp.sum(taps, axis=1, keepdims=True)
    p = jnp.concatenate([p, jnp.zeros((1, cols - p.shape[1]), jnp.float32)], axis=1)
    hi = p.astype(jnp.bfloat16).astype(jnp.float32)
    mid = (p - hi).astype(jnp.bfloat16).astype(jnp.float32)
    low = p - hi - mid
    row = lax.broadcasted_iota(jnp.int32, (16, cols), 0)
    block = jnp.where(row == 0, hi, jnp.where(row == 1, mid, jnp.where(row == 2, low, 0.0)))
    out_ref[2 * rows :, :] = block.astype(jnp.bfloat16)


def strip_kernel(rows, place_ref, own_ref, a_ref, b_ref):
    odd = place_ref[4] > 0
    heads, tails = [], []
    for i in range(2):
        x = own_ref[i * rows : (i + 1) * rows, :].astype(jnp.float32)
        heads.append(x[:RIM])
        tails.append(x[rows - RIM :])
    head = jnp.concatenate(heads, 0)
    tail = jnp.concatenate(tails, 0)
    a_ref[...] = jnp.where(odd, head, tail).astype(jnp.bfloat16)
    b_ref[...] = jnp.where(odd, tail, head).astype(jnp.bfloat16)


def turned(pieces, by):
    count = len(pieces)
    whole, part = divmod(by, 128)
    near = pieces[-whole % count]
    if part == 0:
        return near
    far = pieces[(-whole - 1) % count]
    lane = lax.broadcasted_iota(jnp.int32, near.shape, 1)
    return jnp.where(lane >= part, pltpu.roll(near, part, 1), pltpu.roll(far, part, 1))


def select(d, weights):
    acc = jnp.zeros(d.shape, jnp.float32)
    for a, w in enumerate(weights):
        acc = jnp.where(d == a, w, acc)
    return acc


def shift_kernel(hyps, rows, all_cols, place_ref, base_ref, times_ref, speed_ref, rb_ref, cb_ref):
    circle = rb_ref.shape[2]
    r = lax.broadcasted_iota(jnp.int32, (8, circle), 0)
    k = lax.broadcasted_iota(jnp.int32, (8, circle), 1)
    row_base = k - r
    r = lax.broadcasted_iota(jnp.int32, (8, all_cols), 0)
    m = lax.broadcasted_iota(jnp.int32, (8, all_cols), 1)
    col_base = r - m

    def one(e, carry):
        time = times_ref[place_ref[2] ^ (base_ref[0] + e)]
        for h in range(hyps):
            whole, weights = spline_taps(speed_ref[h, 0], time)
            base = select((row_base - (whole - 1)) & (circle - 1), weights)
            pieces = [base[:, j : j + 128] for j in range(0, circle, 128)]
            turns = [pieces[-j:] + pieces[:-j] for j in range(len(pieces), 0, -1)]
            blocks = [
                jnp.concatenate([turned(turn, n) for turn in turns], 1) for n in range(0, rows, 8)
            ]
            rb_ref[e, h * rows : (h + 1) * rows, :] = jnp.concatenate(blocks, 0).astype(jnp.bfloat16)
            whole, weights = spline_taps(speed_ref[h, 1], time)
            d = col_base - (whole - 1)
            base = select(jnp.where(d < 0, d + all_cols, d), weights)
            pieces = [base[:, j : j + 128] for j in range(0, all_cols, 128)]
            cb_ref[h, e] = jnp.concatenate(
                [turned(pieces, n) for n in range(0, all_cols, 8)], 0
            ).astype(jnp.bfloat16)
        return carry

    lax.fori_loop(0, rb_ref.shape[0], one, 0)


def blur_kernel(rows, cols, place_ref, tile_ref, br_ref, bc_ref):
    out_rows = br_ref.shape[1]
    all_cols = bc_ref.shape[1]
    low_row = place_ref[0]
    high_row = place_ref[1]
    odd = place_ref[4]
    first_a = jnp.where(odd > 0, -RIM, rows)
    first_b = jnp.where(odd > 0, rows, -RIM)
    block = tile_ref[2 * rows : 2 * rows + 16, :].astype(jnp.float32)
    p = block[0:1] + block[1:2] + block[2:3]
    kernels = (p, p * p)

    def fill(d, images):
        found = [jnp.zeros(d.shape, jnp.float32)] * len(images)
        for t in range(2 * PR + 1):
            hit = d == t
            for at, i in enumerate(images):
                found[at] = jnp.where(hit, kernels[i][:, t : t + 1], found[at])
        return found

    zero = jnp.zeros((16, 128), jnp.float32)
    for n0 in range(0, out_rows, 16):
        start = n0 if n0 < rows + REACH else n0 - out_rows
        n = lax.broadcasted_iota(jnp.int32, (16, 128), 0) + start
        inside = (n >= low_row) & (n < high_row)
        k = lax.broadcasted_iota(jnp.int32, (16, 128), 1)
        tile = [zero, zero]
        if start + 16 + PR > 0 and start - PR < rows:
            tile = fill(jnp.where(inside, k - n + PR, -1), (0, 1))
        for i in range(2):
            rim = zero
            if start + 16 + PR > rows or start - PR < 0:
                w = k + 16 * i
                c = jnp.where(
                    (w >= i * RIM) & (w < (i + 1) * RIM),
                    first_a + w - i * RIM,
                    jnp.where(
                        (w >= (2 + i) * RIM) & (w < (3 + i) * RIM),
                        first_b + w - (2 + i) * RIM,
                        -4096,
                    ),
                )
                rim = fill(jnp.where(inside, c - n + PR, -1), (i,))[0]
            br_ref[i, n0 : n0 + 16, :] = jnp.concatenate([tile[i], rim], 1).astype(jnp.bfloat16)
    r = lax.broadcasted_iota(jnp.int32, (8, all_cols), 0)
    m = lax.broadcasted_iota(jnp.int32, (8, all_cols), 1)
    d = r - m + PR
    for i, base in enumerate(fill(jnp.where(d < 0, d + all_cols, d), (0, 1))):
        pieces = [base[:, j : j + 128] for j in range(0, all_cols, 128)]
        bc_ref[i] = jnp.concatenate(
            [turned(pieces, n) for n in range(0, all_cols, 8)], 0
        ).astype(jnp.bfloat16)


def dot(a, b):
    return jnp.dot(a, b, preferred_element_type=jnp.float32)


def widen(c, count):
    total = c.shape[0]
    return jnp.concatenate(
        [c] + [jnp.concatenate([c[total - 128 * j :], c[: total - 128 * j]], 0) for j in range(1, count)],
        1,
    )


def stack_kernel(slot, hyps, rows, cols, first, final, place_ref, *refs):
    refs = list(refs)
    tile, halo, side_tile, side_halo, br, bc, rb, cb = refs[:8]
    acc = None if first else refs[8]
    out = refs[-1]
    out_rows = br.shape[1]
    wide = cols + 128
    lane = lax.broadcasted_iota(jnp.int32, (1, 128), 1)
    after = jnp.where((lane < 64) & (place_ref[5] > 0), 1.0, 0.0)
    before = jnp.where((lane >= 64) & (place_ref[6] > 0), 1.0, 0.0)
    side = (after + before).astype(jnp.bfloat16)
    after = after.astype(jnp.bfloat16)
    before = before.astype(jnp.bfloat16)
    unused = jnp.zeros((out_rows - rows - 2 * REACH, wide), jnp.float32)
    upper = rows + REACH
    pair = []
    for i in range(2):
        at = slice(i * rows, (i + 1) * rows)
        rim = slice(16 * i, 16 * i + 128)
        left = jnp.concatenate([tile[at, :], halo[rim, :]], 0)
        right = jnp.concatenate([side_tile[at, :], side_halo[rim, :]], 0)
        right = right[:, :128] * after + right[:, cols - 128 :] * before
        field = jnp.concatenate([left, right], 1)
        half = jnp.concatenate([br[i, :upper, :], br[i, out_rows - REACH :, :]], 0)
        half = dot(half, field).astype(jnp.bfloat16)
        image = dot(half, widen(bc[i], wide // 128))
        image = jnp.concatenate([image[:upper], unused, image[upper:]], 0).astype(jnp.bfloat16)
        pair += [image[:, :cols], image[:, cols:] * side]
    moved = dot(rb[slot], jnp.concatenate(pair, 1)).astype(jnp.bfloat16)
    for h in range(hyps):
        at = slice(h * rows, (h + 1) * rows)
        both = jnp.concatenate([moved[at, :wide], moved[at, wide:]], 0)
        total = dot(both, widen(cb[h, slot], cols // 128))
        if not first:
            total = total + acc[h]
        if final:
            out[h] = total[:rows] / jnp.sqrt(total[rows:])
        else:
            out[h] = total


VMEM = pl.BlockSpec(memory_space=pltpu.VMEM)
SMEM = pl.BlockSpec(memory_space=pltpu.SMEM)
PARAMS = pltpu.CompilerParams(vmem_limit_bytes=VMEM_LIMIT)


def call(kernel, specs, shapes, *args, scratch=(), flops=0, bytes_accessed=0):
    single = not isinstance(shapes, (list, tuple))
    return pl.pallas_call(
        kernel,
        out_shape=shapes,
        in_specs=specs,
        out_specs=VMEM if single else [VMEM] * len(shapes),
        scratch_shapes=list(scratch),
        compiler_params=PARAMS,
        cost_estimate=pl.CostEstimate(
            flops=flops, bytes_accessed=bytes_accessed, transcendentals=0
        ),
    )(*args)


def bf16(*shape):
    return jax.ShapeDtypeStruct(shape, jnp.bfloat16)


def side_swap(x):
    count = lax.axis_size("ty")
    if count == 2:
        return lax.ppermute(x, "ty", [(0, 1), (1, 0)])
    after = lax.ppermute(x[:, :128], "ty", [(i + 1, i) for i in range(count - 1)])
    before = lax.ppermute(x[:, x.shape[1] - 128 :], "ty", [(i, i + 1) for i in range(count - 1)])
    return jnp.concatenate([after, before], 1)


def shards(science, inv_variance, psf_taps, epoch_times, velocities):
    rows, cols = science.shape[1:]
    hyps = velocities.shape[0]
    epochs = lax.axis_size("ea")
    tx = lax.axis_size("tx")
    ty = lax.axis_size("ty")
    here_x = lax.axis_index("tx")
    here_y = lax.axis_index("ty")
    here_e = lax.axis_index("ea")
    all_cols = cols + 128
    slots = min(GROUP, epochs)

    place = jnp.stack(
        [
            jnp.where(here_x == 0, 0, -REACH),
            jnp.where(here_x == tx - 1, rows, rows + REACH),
            here_e,
            here_x,
            here_x % 2,
            jnp.where(here_y < ty - 1, 1, 0),
            jnp.where(here_y > 0, 1, 0),
        ]
    ).astype(jnp.int32)

    own = call(
        pack_kernel,
        [pl.BlockSpec(memory_space=pltpu.HBM)] * 3,
        bf16(2 * rows + 16, cols),
        science,
        inv_variance,
        psf_taps,
        scratch=[
            pltpu.VMEM(science.shape, jnp.float32),
            pltpu.VMEM(science.shape, jnp.float32),
            pltpu.VMEM(psf_taps.shape, jnp.float32),
            pltpu.SemaphoreType.DMA((3,)),
        ],
    )
    tiles = [own] + [
        lax.ppermute(own, "ea", [(i, i ^ k) for i in range(epochs)]) for k in range(1, epochs)
    ]
    strip_a, strip_b = call(
        functools.partial(strip_kernel, rows),
        [SMEM, VMEM],
        [bf16(2 * RIM, cols)] * 2,
        place,
        own,
        flops=STRIP_FLOPS,
    )
    swap_b = [(i, i + 1) for i in range(1, tx - 1, 2)] + [(i + 1, i) for i in range(1, tx - 1, 2)]
    swap_a = [(i, i + 1) for i in range(0, tx - 1, 2)] + [(i + 1, i) for i in range(0, tx - 1, 2)]
    rim_b = lax.ppermute(strip_b, "tx", swap_b)
    rim_a = lax.ppermute(strip_a, "tx", swap_a)
    halo = jnp.concatenate([rim_a, rim_b], 0)
    def shift_bands(base):
        return call(
            functools.partial(shift_kernel, hyps, rows, all_cols),
            [SMEM] * 4,
            [bf16(slots, hyps * rows, 2 * rows), bf16(hyps, slots, all_cols, 128)],
            place,
            base,
            epoch_times,
            velocities,
            flops=SHIFT_FLOPS,
        )

    def blur_bands(tile):
        return call(
            functools.partial(blur_kernel, rows, cols),
            [SMEM, VMEM],
            [bf16(2, 2 * rows, 2 * rows), bf16(2, all_cols, 128)],
            place,
            tile,
            flops=BLUR_FLOPS,
        )

    def stack(slot, tile, halo, blurs, shifts, total, final):
        args = [place, tile, halo, side_swap(tile), side_swap(halo), *blurs, *shifts]
        if total is not None:
            args.append(total)
        shape = (hyps, rows, cols) if final else (hyps, 2 * rows, cols)
        return call(
            functools.partial(stack_kernel, slot, hyps, rows, cols, total is None, final),
            [SMEM] + [VMEM] * (len(args) - 1),
            jax.ShapeDtypeStruct(shape, jnp.float32),
            *args,
            flops=STACK_FLOPS,
        )

    if epochs == slots:
        shifts = shift_bands(jnp.zeros((1,), jnp.int32))
        blurs = [blur_bands(tile) for tile in tiles]
        *shifts, halo = lax.optimization_barrier((*shifts, halo))
        halos = [halo]
        for k in range(1, epochs):
            *blurs[k], sent = lax.optimization_barrier((*blurs[k], halo))
            halos.append(lax.ppermute(sent, "ea", [(i, i ^ k) for i in range(epochs)]))
        total = None
        order = [0, *range(epochs - 1, 0, -1)]
        for k in order:
            total = stack(k, tiles[k], halos[k], blurs[k], shifts, total, k == order[-1])
        return total

    halos = [halo] + [
        lax.ppermute(halo, "ea", [(i, i ^ k) for i in range(epochs)]) for k in range(1, epochs)
    ]

    def step(total, xs):
        tiles, halos, base = xs
        shifts = shift_bands(base)
        for k in range(slots):
            total = stack(k, tiles[k], halos[k], blur_bands(tiles[k]), shifts, total, False)
        return total, None

    split = lambda x: x.reshape((epochs // slots, slots) + x.shape[1:])
    zeros = jnp.zeros((hyps, 2 * rows, cols), jnp.float32)
    bases = jnp.arange(0, epochs, slots, dtype=jnp.int32)[:, None]
    every = (split(jnp.stack(tiles)), split(jnp.stack(halos)), bases)
    total, _ = lax.scan(step, zeros, every)
    return total[:, :rows] / jnp.sqrt(total[:, rows:])


def solution(mesh):
    in_specs = (P("ea", "tx", "ty"), P("ea", "tx", "ty"), P("ea", None), P(), P("ea", None))
    out_specs = P("ea", "tx", "ty")
    return jax.shard_map(shards, mesh=mesh, in_specs=in_specs, out_specs=out_specs, check_vma=False)
```

time: 108 us -> 37.3 us (0.35)
  the two profiles are of different devices: /device:TPU:0 before, /device:TPU:5 now
where the time goes in v2:
time: 37.3 us; the launch traced here: 36.8 us
  starting transfers between devices  16.8 us (45%)
  Pallas kernels  15.7 us (42%)
  local copies, waits for them, and re-layouts  2.65 us (7%)
  waiting for transfers between devices  1.49 us (4%)
    pallas_call x11, Pallas kernels, call(): pl.pallas_call(kernel, out_shape=shapes, in_specs=specs, out_specs=VMEM i...  15.7 us
    ppermute x8, starting transfers between devices, side_swap(): return lax.ppermute(x, 'ty', [(0, 1), (1, 0)])  6.6 us
    ppermute x3, starting transfers between devices, shards(): lax.ppermute(own, 'ea', [(i, i ^ k) for i in range(epochs)])  3.67 us
    ppermute x3, starting transfers between devices, shards(): halos.append(lax.ppermute(sent, 'ea', [(i, i ^ k) for i in range(epochs)]))  3.04 us
    unnamed x11, local copies, waits for them, and re-layouts  2.56 us
    ppermute x1, starting transfers between devices, shards(): rim_b = lax.ppermute(strip_b, 'tx', swap_b)  2.23 us
    ppermute x1, starting transfers between devices, shards(): rim_a = lax.ppermute(strip_a, 'tx', swap_a)  1.28 us
    ppermute x3, waiting for transfers between devices, shards(): lax.ppermute(own, 'ea', [(i, i ^ k) for i in range(epochs)])  1.26 us
  transfers between devices with their start and end apart: 16, of which 2 were waited for; matrix products, arithmetic and copies ran while one was open for 0% of the time, Pallas kernels for 33%

profile of v2, /device:TPU:5, one launch (start us, length us, event | category | flops | bytes accessed | tf_op | source)
XLA Modules:
  0.0 36.8 jit_solution(11650522233424989639)
XLA Ops:
  0.0 0.9 %copy-done = f32[1,128,256]{2,1,0:T(8,128)S(1)} copy-done((f32[1,128,256]{2,1,0:T(8,128)S(1)}, f32[1,128,256]{2,1,0:T(8,128)}, u32[]{:S(2)}) %copy-start) | copy-done | bytes 131096
  0.9 0.9 %copy-done.1 = f32[1,128,256]{2,1,0:T(8,128)S(1)} copy-done((f32[1,128,256]{2,1,0:T(8,128)S(1)}, f32[1,128,256]{2,1,0:T(8,128)}, u32[]{:S(2)}) %copy-start.1) | copy-done | bytes 131096
  1.8 0.7 %copy-done.2 = f32[1,9]{1,0:T(1,128)S(1)} copy-done((f32[1,9]{1,0:T(1,128)S(1)}, f32[1,9]{1,0:T(1,128)}, u32[]{:S(2)}) %copy-start.2) | copy-done | bytes 60
  2.5 0.4 %shard_map.55.own_ref.tile_ref.refs_0_ = bf16[272,256]{1,0:T(8,128)(2,1)S(1)} custom-call(f32[1,128,256]{2,1,0:T(8,128)S(1)} %copy-done, f32[1,128,256]{2,1,0:T(8,128)S(1)} %copy-done.1, f32[1,9]{1,0:T(1,128)S(1)} %copy-done.2), custom_call_target="tpu_custom_call" | custom-call | tf_op jit(solution)/shard_map/pallas_call | solution.py:240
  2.9 0.7 %collective-permute-start.14 = (bf16[272,256]{1,0:T(8,128)(2,1)S(1)}, bf16[272,256]{1,0:T(8,128)(2,1)S(1)}, u32[]{:S(2)}, u32[]{:S(2)}) collective-permute-start(bf16[272,256]{1,0:T(8,128)(2,1)S(1)} %shard_map.55.own_ref.tile_ref.refs_0_), channel_id=1, source_target_pairs={{0,4},{4,0},{1,5},{5,1},{2,6},{6,2},{3,7},{7,3},{8,12},{12,8},{9,1... | collective-permute-start | bytes 417800 | tf_op jit(solution)/shard_map/ppermute | solution.py:260
  3.7 3.3 %collective-permute-start.10 = (bf16[272,256]{1,0:T(8,128)(2,1)S(1)}, bf16[272,256]{1,0:T(8,128)(2,1)S(1)}, u32[]{:S(2)}, u32[]{:S(2)}) collective-permute-start(bf16[272,256]{1,0:T(8,128)(2,1)S(1)} %shard_map.55.own_ref.tile_ref.refs_0_), channel_id=1, source_target_pairs={{0,3},{1,2},{2,1},{3,0},{4,7},{5,6},{6,5},{7,4},{8,11},{9,10},{10,... | collective-permute-start | bytes 417800 | tf_op jit(solution)/shard_map/ppermute | solution.py:305
  7.0 0.1 stack.31.place_ref
  7.1 0.6 %shard_map.58 = (bf16[72,256]{1,0:T(8,128)(2,1)S(1)}, bf16[72,256]{1,0:T(8,128)(2,1)S(1)}) custom-call(s32[7]{0:T(128)S(1)} %stack.31.place_ref, bf16[272,256]{1,0:T(8,128)(2,1)S(1)} %shard_map.55.own_ref.tile_ref.refs_0_), custom_call_target="tpu_custom_call" | custom-call | flops 10000000 | tf_op jit(solution)/shard_map/pallas_call | solution.py:240
  7.6 1.3 %collective-permute-start.1 = (bf16[72,256]{1,0:T(8,128)(2,1)S(1)}, bf16[72,256]{1,0:T(8,128)(2,1)S(1)}, u32[]{:S(2)}, u32[]{:S(2)}) collective-permute-start(bf16[72,256]{1,0:T(8,128)(2,1)S(1)} %get-tuple-element.33), channel_id=1, source_target_pairs={{0,8},{16,24},{8,0},{24,16},{1,9},{17,25},{9,1},{25,17},{2,10},{18... | collective-permute-start | bytes 110600 | tf_op jit(solution)/shard_map/ppermute | solution.py:318
  8.9 2.2 %collective-permute-start.2 = (bf16[72,256]{1,0:T(8,128)(2,1)S(1)}, bf16[72,256]{1,0:T(8,128)(2,1)S(1)}, u32[]{:S(2)}, u32[]{:S(2)}) collective-permute-start(bf16[72,256]{1,0:T(8,128)(2,1)S(1)} %get-tuple-element.34), channel_id=1, source_target_pairs={{8,16},{16,8},{9,17},{17,9},{10,18},{18,10},{11,19},{19,11},{12,20... | collective-permute-start | bytes 110600 | tf_op jit(solution)/shard_map/ppermute | solution.py:317
  11.2 0.9 %shard_map.61 = (bf16[2,256,256]{2,1,0:T(8,128)(2,1)S(1)}, bf16[2,384,128]{2,1,0:T(8,128)(2,1)S(1)}) custom-call(s32[7]{0:T(128)S(1)} %stack.31.place_ref, bf16[272,256]{1,0:T(8,128)(2,1)S(1)} %shard_map.55.own_ref.tile_ref.refs_0_), custom_call_target="tpu_custom_call" | custom-call | flops 4000000000 | tf_op jit(solution)/shard_map/pallas_call | solution.py:240
  12.1 0.1 copy.6.speed_ref
  12.2 1.9 %shard_map.57 = (bf16[4,768,256]{2,1,0:T(8,128)(2,1)S(1)}, bf16[6,4,384,128]{3,2,1,0:T(8,128)(2,1)S(1)}) custom-call(s32[7]{0:T(128)S(1)} %stack.31.place_ref, s32[1]{0:T(128)} %constant.36.clone.1.base_ref, s32[4]{0:T(128)S(1)} %copy-done.3, s32[6,2]{1,0:T(8,128)S(1)} %copy.6.speed_ref), custom_call_target="tpu_custom_call" | custom-call | flops 4000000000 | tf_op jit(solution)/shard_map/pallas_call | solution.py:240
  14.1 0.3 collective-permute-start
  14.4 0.2 collective-permute-done.2
  14.7 1.8 %collective-permute-start.15 = (bf16[144,256]{1,0:T(8,128)(2,1)S(1)}, bf16[144,256]{1,0:T(8,128)(2,1)S(1)}, u32[]{:S(2)}, u32[]{:S(2)}) collective-permute-start(bf16[144,256]{1,0:T(8,128)(2,1)S(1)} %pad_maximum_fusion.refs_1_), channel_id=1, source_target_pairs={{0,4},{4,0},{1,5},{5,1},{2,6},{6,2},{3,7},{7,3},{8,12},{12,8},{9,1... | collective-permute-start | bytes 221192 | tf_op jit(solution)/shard_map/ppermute | solution.py:260
  16.4 0.9 %shard_map.60 = (bf16[2,256,256]{2,1,0:T(8,128)(2,1)S(1)}, bf16[2,384,128]{2,1,0:T(8,128)(2,1)S(1)}) custom-call(s32[7]{0:T(128)S(1)} %stack.31.place_ref, bf16[272,256]{1,0:T(8,128)(2,1)S(1)} %collective-permute-done.10.tile_ref.refs_0_), custom_call_target="tpu_custom_call" | custom-call | flops 4000000000 | tf_op jit(solution)/shard_map/pallas_call | solution.py:240
  17.3 2.9 %collective-permute-start.11 = (bf16[144,256]{1,0:T(8,128)(2,1)S(1)}, bf16[144,256]{1,0:T(8,128)(2,1)S(1)}, u32[]{:S(2)}, u32[]{:S(2)}) collective-permute-start(bf16[144,256]{1,0:T(8,128)(2,1)S(1)} %pad_maximum_fusion.refs_1_), channel_id=1, source_target_pairs={{0,3},{1,2},{2,1},{3,0},{4,7},{5,6},{6,5},{7,4},{8,11},{9,10},{10,... | collective-permute-start | bytes 221192 | tf_op jit(solution)/shard_map/ppermute | solution.py:362
  20.2 0.9 %shard_map.59 = (bf16[2,256,256]{2,1,0:T(8,128)(2,1)S(1)}, bf16[2,384,128]{2,1,0:T(8,128)(2,1)S(1)}) custom-call(s32[7]{0:T(128)S(1)} %stack.31.place_ref, bf16[272,256]{1,0:T(8,128)(2,1)S(1)} %collective-permute-done.6.tile_ref.refs_0_), custom_call_target="tpu_custom_call" | custom-call | flops 4000000000 | tf_op jit(solution)/shard_map/pallas_call | solution.py:240
  21.1 0.1 collective-permute-start.7
  21.2 1.3 %collective-permute-done.tile_ref.refs_0_ = bf16[272,256]{1,0:T(8,128)(2,1)S(1)} collective-permute-done((bf16[272,256]{1,0:T(8,128)(2,1)S(1)}, bf16[272,256]{1,0:T(8,128)(2,1)S(1)}, u32[]{:S(2)}, u32[]{:S(2)}) %collective-permute-start) | collective-permute-done | bytes 139296 | tf_op jit(solution)/shard_map/ppermute | solution.py:305
  22.5 0.9 %shard_map.56 = (bf16[2,256,256]{2,1,0:T(8,128)(2,1)S(1)}, bf16[2,384,128]{2,1,0:T(8,128)(2,1)S(1)}) custom-call(s32[7]{0:T(128)S(1)} %stack.31.place_ref, bf16[272,256]{1,0:T(8,128)(2,1)S(1)} %collective-permute-done.tile_ref.refs_0_), custom_call_target="tpu_custom_call" | custom-call | flops 4000000000 | tf_op jit(solution)/shard_map/pallas_call | solution.py:240
  23.4 0.1 collective-permute-start.3
  23.5 1.9 %collective-permute-start.12 = (bf16[272,256]{1,0:T(8,128)(2,1)S(1)}, bf16[272,256]{1,0:T(8,128)(2,1)S(1)}, u32[]{:S(2)}, u32[]{:S(2)}) collective-permute-start(bf16[272,256]{1,0:T(8,128)(2,1)S(1)} %collective-permute-done.10.tile_ref.refs_0_), channel_id=1, source_target_pairs={{0,4},{4,0},{1,5},{5,1},{2,6},{6,2},{3,7},{7,3},{8,12},{12,8},{9,1... | collective-permute-start | bytes 417800 | tf_op jit(solution)/shard_map/ppermute | solution.py:260
  25.3 0.1 collective-permute-start.8
  25.4 0.4 %collective-permute-start.13 = (bf16[144,256]{1,0:T(8,128)(2,1)S(1)}, bf16[144,256]{1,0:T(8,128)(2,1)S(1)}, u32[]{:S(2)}, u32[]{:S(2)}) collective-permute-start(bf16[144,256]{1,0:T(8,128)(2,1)S(1)} %collective-permute-done.11.refs_1_), channel_id=1, source_target_pairs={{0,4},{4,0},{1,5},{5,1},{2,6},{6,2},{3,7},{7,3},{8,12},{12,8},{9,1... | collective-permute-start | bytes 221192 | tf_op jit(solution)/shard_map/ppermute | solution.py:260
  25.9 2.0 %shard_map.62.refs_8_ = f32[6,256,256]{2,1,0:T(8,128)S(1)} custom-call(s32[7]{0:T(128)S(1)} %stack.31.place_ref, bf16[272,256]{1,0:T(8,128)(2,1)S(1)} %shard_map.55.own_ref.tile_ref.refs_0_, bf16[144,256]{1,0:T(8,128)(2,1)S(1)} %pad_maximum_fusion.refs_1_, bf16[272,256]{1,0:T(8,128)(2,1)S(1)} %collective-permute-done.14.refs_2_, ...), custom_call_target="tpu_custom_call" | custom-call | flops 2000000000 | tf_op jit(solution)/shard_map/pallas_call | solution.py:240
  27.9 0.4 collective-permute-start.4
  28.3 1.3 %collective-permute-start.9 = (bf16[144,256]{1,0:T(8,128)(2,1)S(1)}, bf16[144,256]{1,0:T(8,128)(2,1)S(1)}, u32[]{:S(2)}, u32[]{:S(2)}) collective-permute-start(bf16[144,256]{1,0:T(8,128)(2,1)S(1)} %collective-permute-done.7.refs_1_), channel_id=1, source_target_pairs={{0,4},{4,0},{1,5},{5,1},{2,6},{6,2},{3,7},{7,3},{8,12},{12,8},{9,1... | collective-permute-start | bytes 221192 | tf_op jit(solution)/shard_map/ppermute | solution.py:260
  29.6 2.1 %shard_map.63.refs_8_ = f32[6,256,256]{2,1,0:T(8,128)S(1)} custom-call(s32[7]{0:T(128)S(1)} %stack.31.place_ref, bf16[272,256]{1,0:T(8,128)(2,1)S(1)} %collective-permute-done.10.tile_ref.refs_0_, bf16[144,256]{1,0:T(8,128)(2,1)S(1)} %collective-permute-done.11.refs_1_, bf16[272,256]{1,0:T(8,128)(2,1)S(1)} %collective-permute-done.12.refs_2_, ...), custom_call_target="tpu_custom_call" | custom-call | flops 2000000000 | tf_op jit(solution)/shard_map/pallas_call | solution.py:240
  31.7 2.1 %shard_map.64.refs_8_ = f32[6,256,256]{2,1,0:T(8,128)S(1)} custom-call(s32[7]{0:T(128)S(1)} %stack.31.place_ref, bf16[272,256]{1,0:T(8,128)(2,1)S(1)} %collective-permute-done.6.tile_ref.refs_0_, bf16[144,256]{1,0:T(8,128)(2,1)S(1)} %collective-permute-done.7.refs_1_, bf16[272,256]{1,0:T(8,128)(2,1)S(1)} %collective-permute-done.8.refs_2_, ...), custom_call_target="tpu_custom_call" | custom-call | flops 2000000000 | tf_op jit(solution)/shard_map/pallas_call | solution.py:240
  33.8 3.0 %shard_map.65 = f32[6,128,256]{2,1,0:T(8,128)} custom-call(s32[7]{0:T(128)S(1)} %stack.31.place_ref, bf16[272,256]{1,0:T(8,128)(2,1)S(1)} %collective-permute-done.tile_ref.refs_0_, bf16[144,256]{1,0:T(8,128)(2,1)S(1)} %collective-permute-done.3.refs_1_, bf16[272,256]{1,0:T(8,128)(2,1)S(1)} %collective-permute-done.4.refs_2_, ...), custom_call_target="tpu_custom_call" | custom-call | flops 2000000000 | tf_op jit(solution)/shard_map/pallas_call | solution.py:240
  (24 shorter events, 0.1 us)
Async XLA Ops:
  0.0 0.9 %copy-start = (f32[1,128,256]{2,1,0:T(8,128)S(1)}, f32[1,128,256]{2,1,0:T(8,128)}, u32[]{:S(2)}) copy-start(f32[1,128,256]{2,1,0:T(8,128)} %sci_hbm.1) | copy-start | bytes 393220
  0.9 0.9 %copy-start.1 = (f32[1,128,256]{2,1,0:T(8,128)S(1)}, f32[1,128,256]{2,1,0:T(8,128)}, u32[]{:S(2)}) copy-start(f32[1,128,256]{2,1,0:T(8,128)} %iv_hbm.1) | copy-start | bytes 393220
  1.8 0.7 %copy-start.2 = (f32[1,9]{1,0:T(1,128)S(1)}, f32[1,9]{1,0:T(1,128)}, u32[]{:S(2)}) copy-start(f32[1,9]{1,0:T(1,128)} %taps_hbm.1) | copy-start | bytes 112
  2.9 22.4 %collective-permute-start.14 = (bf16[272,256]{1,0:T(8,128)(2,1)S(1)}, bf16[272,256]{1,0:T(8,128)(2,1)S(1)}, u32[]{:S(2)}, u32[]{:S(2)}) collective-permute-start(bf16[272,256]{1,0:T(8,128)(2,1)S(1)} %shard_map.55.own_ref.tile_ref.refs_0_), channel_id=1, source_target_pairs={{0,4},{4,0},{1,5},{5,1},{2,6},{6,2},{3,7},{7,3},{8,12},{12,8},{9,1... | collective-permute-start | bytes 417800 | tf_op jit(solution)/shard_map/ppermute | solution.py:260
  3.7 12.8 %collective-permute-start.10 = (bf16[272,256]{1,0:T(8,128)(2,1)S(1)}, bf16[272,256]{1,0:T(8,128)(2,1)S(1)}, u32[]{:S(2)}, u32[]{:S(2)}) collective-permute-start(bf16[272,256]{1,0:T(8,128)(2,1)S(1)} %shard_map.55.own_ref.tile_ref.refs_0_), channel_id=1, source_target_pairs={{0,3},{1,2},{2,1},{3,0},{4,7},{5,6},{6,5},{7,4},{8,11},{9,10},{10,... | collective-permute-start | bytes 417800 | tf_op jit(solution)/shard_map/ppermute | solution.py:305
  7.0 13.2 %collective-permute-start.6 = (bf16[272,256]{1,0:T(8,128)(2,1)S(1)}, bf16[272,256]{1,0:T(8,128)(2,1)S(1)}, u32[]{:S(2)}, u32[]{:S(2)}) collective-permute-start(bf16[272,256]{1,0:T(8,128)(2,1)S(1)} %shard_map.55.own_ref.tile_ref.refs_0_), channel_id=1, source_target_pairs={{0,2},{1,3},{2,0},{3,1},{4,6},{5,7},{6,4},{7,5},{8,10},{9,11},{10,... | collective-permute-start | bytes 417800 | tf_op jit(solution)/shard_map/ppermute | solution.py:305
  7.6 6.5 %collective-permute-start.1 = (bf16[72,256]{1,0:T(8,128)(2,1)S(1)}, bf16[72,256]{1,0:T(8,128)(2,1)S(1)}, u32[]{:S(2)}, u32[]{:S(2)}) collective-permute-start(bf16[72,256]{1,0:T(8,128)(2,1)S(1)} %get-tuple-element.33), channel_id=1, source_target_pairs={{0,8},{16,24},{8,0},{24,16},{1,9},{17,25},{9,1},{25,17},{2,10},{18... | collective-permute-start | bytes 110600 | tf_op jit(solution)/shard_map/ppermute | solution.py:318
  8.9 3.1 %copy-start.4 = (s32[6,2]{0,1:T(2,128)S(1)}, s32[6,2]{0,1:T(2,128)}, u32[]{:S(2)}) copy-start(s32[6,2]{0,1:T(2,128)} %param.9) | copy-start | bytes 148
  8.9 3.2 %copy-start.3 = (s32[4]{0:T(128)S(1)}, s32[4]{0:T(128)}, u32[]{:S(2)}) copy-start(s32[4]{0:T(128)} %times_ref.1) | copy-start | bytes 52
  8.9 5.7 %collective-permute-start.2 = (bf16[72,256]{1,0:T(8,128)(2,1)S(1)}, bf16[72,256]{1,0:T(8,128)(2,1)S(1)}, u32[]{:S(2)}, u32[]{:S(2)}) collective-permute-start(bf16[72,256]{1,0:T(8,128)(2,1)S(1)} %get-tuple-element.34), channel_id=1, source_target_pairs={{8,16},{16,8},{9,17},{17,9},{10,18},{18,10},{11,19},{19,11},{12,20... | collective-permute-start | bytes 110600 | tf_op jit(solution)/shard_map/ppermute | solution.py:317
  14.1 8.4 %collective-permute-start = (bf16[272,256]{1,0:T(8,128)(2,1)S(1)}, bf16[272,256]{1,0:T(8,128)(2,1)S(1)}, u32[]{:S(2)}, u32[]{:S(2)}) collective-permute-start(bf16[272,256]{1,0:T(8,128)(2,1)S(1)} %shard_map.55.own_ref.tile_ref.refs_0_), channel_id=1, source_target_pairs={{0,1},{1,0},{2,3},{3,2},{4,5},{5,4},{6,7},{7,6},{8,9},{9,8},{10,11... | collective-permute-start | bytes 417800 | tf_op jit(solution)/shard_map/ppermute | solution.py:305
  14.7 8.8 %collective-permute-start.15 = (bf16[144,256]{1,0:T(8,128)(2,1)S(1)}, bf16[144,256]{1,0:T(8,128)(2,1)S(1)}, u32[]{:S(2)}, u32[]{:S(2)}) collective-permute-start(bf16[144,256]{1,0:T(8,128)(2,1)S(1)} %pad_maximum_fusion.refs_1_), channel_id=1, source_target_pairs={{0,4},{4,0},{1,5},{5,1},{2,6},{6,2},{3,7},{7,3},{8,12},{12,8},{9,1... | collective-permute-start | bytes 221192 | tf_op jit(solution)/shard_map/ppermute | solution.py:260
  17.3 8.1 %collective-permute-start.11 = (bf16[144,256]{1,0:T(8,128)(2,1)S(1)}, bf16[144,256]{1,0:T(8,128)(2,1)S(1)}, u32[]{:S(2)}, u32[]{:S(2)}) collective-permute-start(bf16[144,256]{1,0:T(8,128)(2,1)S(1)} %pad_maximum_fusion.refs_1_), channel_id=1, source_target_pairs={{0,3},{1,2},{2,1},{3,0},{4,7},{5,6},{6,5},{7,4},{8,11},{9,10},{10,... | collective-permute-start | bytes 221192 | tf_op jit(solution)/shard_map/ppermute | solution.py:362
  21.1 6.8 %collective-permute-start.7 = (bf16[144,256]{1,0:T(8,128)(2,1)S(1)}, bf16[144,256]{1,0:T(8,128)(2,1)S(1)}, u32[]{:S(2)}, u32[]{:S(2)}) collective-permute-start(bf16[144,256]{1,0:T(8,128)(2,1)S(1)} %pad_maximum_fusion.refs_1_), channel_id=1, source_target_pairs={{0,2},{1,3},{2,0},{3,1},{4,6},{5,7},{6,4},{7,5},{8,10},{9,11},{10,... | collective-permute-start | bytes 221192 | tf_op jit(solution)/shard_map/ppermute | solution.py:362
  23.4 4.9 %collective-permute-start.3 = (bf16[144,256]{1,0:T(8,128)(2,1)S(1)}, bf16[144,256]{1,0:T(8,128)(2,1)S(1)}, u32[]{:S(2)}, u32[]{:S(2)}) collective-permute-start(bf16[144,256]{1,0:T(8,128)(2,1)S(1)} %pad_maximum_fusion.refs_1_), channel_id=1, source_target_pairs={{0,1},{1,0},{2,3},{3,2},{4,5},{5,4},{6,7},{7,6},{8,9},{9,8},{10,11... | collective-permute-start | bytes 221192 | tf_op jit(solution)/shard_map/ppermute | solution.py:362
  23.5 6.1 %collective-permute-start.12 = (bf16[272,256]{1,0:T(8,128)(2,1)S(1)}, bf16[272,256]{1,0:T(8,128)(2,1)S(1)}, u32[]{:S(2)}, u32[]{:S(2)}) collective-permute-start(bf16[272,256]{1,0:T(8,128)(2,1)S(1)} %collective-permute-done.10.tile_ref.refs_0_), channel_id=1, source_target_pairs={{0,4},{4,0},{1,5},{5,1},{2,6},{6,2},{3,7},{7,3},{8,12},{12,8},{9,1... | collective-permute-start | bytes 417800 | tf_op jit(solution)/shard_map/ppermute | solution.py:260
  25.3 6.4 %collective-permute-start.8 = (bf16[272,256]{1,0:T(8,128)(2,1)S(1)}, bf16[272,256]{1,0:T(8,128)(2,1)S(1)}, u32[]{:S(2)}, u32[]{:S(2)}) collective-permute-start(bf16[272,256]{1,0:T(8,128)(2,1)S(1)} %collective-permute-done.6.tile_ref.refs_0_), channel_id=1, source_target_pairs={{0,4},{4,0},{1,5},{5,1},{2,6},{6,2},{3,7},{7,3},{8,12},{12,8},{9,1... | collective-permute-start | bytes 417800 | tf_op jit(solution)/shard_map/ppermute | solution.py:260
  25.4 4.2 %collective-permute-start.13 = (bf16[144,256]{1,0:T(8,128)(2,1)S(1)}, bf16[144,256]{1,0:T(8,128)(2,1)S(1)}, u32[]{:S(2)}, u32[]{:S(2)}) collective-permute-start(bf16[144,256]{1,0:T(8,128)(2,1)S(1)} %collective-permute-done.11.refs_1_), channel_id=1, source_target_pairs={{0,4},{4,0},{1,5},{5,1},{2,6},{6,2},{3,7},{7,3},{8,12},{12,8},{9,1... | collective-permute-start | bytes 221192 | tf_op jit(solution)/shard_map/ppermute | solution.py:260
  27.9 5.9 %collective-permute-start.4 = (bf16[272,256]{1,0:T(8,128)(2,1)S(1)}, bf16[272,256]{1,0:T(8,128)(2,1)S(1)}, u32[]{:S(2)}, u32[]{:S(2)}) collective-permute-start(bf16[272,256]{1,0:T(8,128)(2,1)S(1)} %collective-permute-done.tile_ref.refs_0_), channel_id=1, source_target_pairs={{0,4},{4,0},{1,5},{5,1},{2,6},{6,2},{3,7},{7,3},{8,12},{12,8},{9,1... | collective-permute-start | bytes 417800 | tf_op jit(solution)/shard_map/ppermute | solution.py:260
  28.3 3.4 %collective-permute-start.9 = (bf16[144,256]{1,0:T(8,128)(2,1)S(1)}, bf16[144,256]{1,0:T(8,128)(2,1)S(1)}, u32[]{:S(2)}, u32[]{:S(2)}) collective-permute-start(bf16[144,256]{1,0:T(8,128)(2,1)S(1)} %collective-permute-done.7.refs_1_), channel_id=1, source_target_pairs={{0,4},{4,0},{1,5},{5,1},{2,6},{6,2},{3,7},{7,3},{8,12},{12,8},{9,1... | collective-permute-start | bytes 221192 | tf_op jit(solution)/shard_map/ppermute | solution.py:260
  29.6 4.2 %collective-permute-start.5 = (bf16[144,256]{1,0:T(8,128)(2,1)S(1)}, bf16[144,256]{1,0:T(8,128)(2,1)S(1)}, u32[]{:S(2)}, u32[]{:S(2)}) collective-permute-start(bf16[144,256]{1,0:T(8,128)(2,1)S(1)} %collective-permute-done.3.refs_1_), channel_id=1, source_target_pairs={{0,4},{4,0},{1,5},{5,1},{2,6},{6,2},{3,7},{7,3},{8,12},{12,8},{9,1... | collective-permute-start | bytes 221192 | tf_op jit(solution)/shard_map/ppermute | solution.py:260

commit v3 on v2

v3 whole, which is shorter than its diff:
```python
import functools

import jax
import jax.numpy as jnp
from jax import lax
from jax.experimental import pallas as pl
from jax.experimental.pallas import tpu as pltpu
from jax.sharding import PartitionSpec as P

REACH = 32
PR = 4
RIM = REACH + PR
GROUP = 4
VMEM_LIMIT = 24 * 1024 * 1024
STRIP_FLOPS = 10_000_000
SHIFT_FLOPS = 4_000_000_000
BLUR_FLOPS = 4_000_000_000
STACK_FLOPS = 2_000_000_000


def spline_taps(speed, time):
    moved = (speed * time) >> 3
    frac = (moved & 15).astype(jnp.float32) * (1.0 / 16.0)
    rest = 1.0 - frac
    frac2 = frac * frac
    frac3 = frac2 * frac
    sixth = 1.0 / 6.0
    weights = [
        rest * rest * rest * sixth,
        (3.0 * frac3 - 6.0 * frac2 + 4.0) * sixth,
        (-3.0 * frac3 + 3.0 * frac2 + 3.0 * frac + 1.0) * sixth,
        frac3 * sixth,
    ]
    return moved >> 4, weights


def packed(science, inv_variance, psf_taps):
    cols = science.shape[2]
    taps = jnp.broadcast_to(jnp.pad(psf_taps, ((0, 0), (0, cols - psf_taps.shape[1]))), (16, cols))
    hi = lax.reduce_precision(taps, 8, 7)
    mid = lax.reduce_precision(taps - hi, 8, 7)
    row = lax.broadcasted_iota(jnp.int32, (16, cols), 0)
    taps = jnp.where(row == 0, hi, jnp.where(row == 1, mid, taps - hi - mid))
    return jnp.concatenate([science[0] * inv_variance[0], inv_variance[0], taps], 0).astype(jnp.bfloat16)


def strip_kernel(rows, own_ref, a_ref, b_ref):
    odd = lax.axis_index("tx") % 2 > 0
    heads, tails = [], []
    for i in range(2):
        x = own_ref[i * rows : (i + 1) * rows, :].astype(jnp.float32)
        heads.append(x[:RIM])
        tails.append(x[rows - RIM :])
    head = jnp.concatenate(heads, 0)
    tail = jnp.concatenate(tails, 0)
    a_ref[...] = jnp.where(odd, head, tail).astype(jnp.bfloat16)
    b_ref[...] = jnp.where(odd, tail, head).astype(jnp.bfloat16)


def turned(pieces, by):
    count = len(pieces)
    whole, part = divmod(by, 128)
    near = pieces[-whole % count]
    if part == 0:
        return near
    far = pieces[(-whole - 1) % count]
    lane = lax.broadcasted_iota(jnp.int32, near.shape, 1)
    return jnp.where(lane >= part, pltpu.roll(near, part, 1), pltpu.roll(far, part, 1))


def cut(base):
    return [base[:, j : j + 128] for j in range(0, base.shape[1], 128)]


def select(d, weights):
    acc = jnp.zeros(d.shape, jnp.float32)
    for a, w in enumerate(weights):
        acc = jnp.where(d == a, w, acc)
    return acc.astype(jnp.bfloat16)


def distance(count, source_axis):
    d = lax.broadcasted_iota(jnp.int32, (16, count), source_axis) - lax.broadcasted_iota(
        jnp.int32, (16, count), 1 - source_axis
    )
    return d


def shift_kernel(hyps, rows, all_cols, base_ref, times_ref, speed_ref, rb_ref, cb_ref):
    circle = rb_ref.shape[2]
    row_base = distance(circle, 1)
    col_base = distance(all_cols, 0)

    def one(e, carry):
        time = times_ref[lax.axis_index("ea") ^ (base_ref[0] + e)]
        for h in range(hyps):
            whole, weights = spline_taps(speed_ref[h, 0], time)
            pieces = cut(select((row_base - (whole - 1)) & (circle - 1), weights))
            turns = [pieces[-j:] + pieces[:-j] for j in range(len(pieces), 0, -1)]
            for n in range(0, rows, 16):
                for j, turn in enumerate(turns):
                    rb_ref[e, h * rows + n : h * rows + n + 16, 128 * j : 128 * (j + 1)] = turned(turn, n)
            whole, weights = spline_taps(speed_ref[h, 1], time)
            d = col_base - (whole - 1)
            pieces = cut(select(jnp.where(d < 0, d + all_cols, d), weights))
            for n in range(0, all_cols, 16):
                cb_ref[h, e, n : n + 16, :] = turned(pieces, n)
        return carry

    lax.fori_loop(0, rb_ref.shape[0], one, 0)


def blur_kernel(rows, cols, last_x, tile_ref, br_ref, bc_ref):
    out_rows, circle = br_ref.shape[1:]
    all_cols = bc_ref.shape[1]
    here_x = lax.axis_index("tx")
    odd = here_x % 2 > 0
    one = jnp.ones((16, 128), jnp.float32)
    keep_above = jnp.where(here_x > 0, one, 0.0).astype(jnp.bfloat16)
    keep_below = jnp.where(here_x < last_x, one, 0.0).astype(jnp.bfloat16)
    block = tile_ref[2 * rows : 2 * rows + 16, :].astype(jnp.float32)
    p = block[0:1] + block[1:2] + block[2:3]
    p = p / jnp.sum(p, axis=1, keepdims=True)
    taps = [p[:, t : t + 1] for t in range(2 * PR + 1)]
    kernels = (taps, [t * t for t in taps])
    row_base = (distance(circle, 1) + PR) & (circle - 1)
    col_base = distance(all_cols, 0) + PR
    col_base = jnp.where(col_base < 0, col_base + all_cols, col_base)
    lane = lax.broadcasted_iota(jnp.int32, (16, 128), 1)
    for i in range(2):
        pieces = cut(select(row_base, kernels[i]))
        first_a = (RIM - 16) * i
        first_b = 2 * RIM + first_a

        def rim(n, lanes, coordinate):
            return jnp.where(
                (lane >= lanes) & (lane < lanes + RIM), turned(pieces, (n + lanes - coordinate) % circle), 0.0
            ).astype(jnp.bfloat16)

        for at in range(0, out_rows, 16):
            n = at if at < rows + REACH else at - out_rows
            left = turned(pieces, n % circle)
            right = jnp.zeros((16, 128), jnp.bfloat16)
            if n - PR < 0:
                right = jnp.where(odd, rim(n, first_a, -RIM), rim(n, first_b, -RIM))
            elif n + 16 + PR > rows:
                right = jnp.where(odd, rim(n, first_b, rows), rim(n, first_a, rows))
            if n < 0 or n >= rows:
                keep = keep_above if n < 0 else keep_below
                left, right = left * keep, right * keep
            br_ref[i, at : at + 16, :128] = left
            br_ref[i, at : at + 16, 128:] = right
        pieces = cut(select(col_base, kernels[i]))
        for n in range(0, all_cols, 16):
            bc_ref[i, n : n + 16, :] = turned(pieces, n)


def dot(a, b):
    return jnp.dot(a, b, preferred_element_type=jnp.float32)


def widen(c, count):
    total = c.shape[0]
    return jnp.concatenate(
        [c] + [jnp.concatenate([c[total - 128 * j :], c[: total - 128 * j]], 0) for j in range(1, count)],
        1,
    )


def stack_kernel(slots, hyps, rows, cols, last_y, first, final, spots, *refs):
    count = len(slots)
    refs = list(refs)
    tiles, halos, brs, bcs = [[refs.pop(0) for _ in range(count)] for _ in range(4)]
    side_tiles, side_halos, rb, cb = [refs.pop(0) for _ in range(4)]
    acc = None if first else refs.pop(0)
    out = refs.pop(0)
    wide = cols + 128
    lane = lax.broadcasted_iota(jnp.int32, (1, 128), 1)
    here_y = lax.axis_index("ty")
    after = jnp.where((lane < 64) & (here_y < last_y), 1.0, 0.0)
    before = jnp.where((lane >= 64) & (here_y > 0), 1.0, 0.0)
    side = (after + before).astype(jnp.bfloat16)
    after = after.astype(jnp.bfloat16)
    before = before.astype(jnp.bfloat16)
    upper = rows + REACH
    unused = jnp.zeros((rb.shape[2] - rows - 2 * REACH, wide), jnp.float32)
    moved = []
    for j in range(count):
        pair = []
        tile_at, halo_at = spots[j]
        for i in range(2):
            at = i * rows
            rim = 16 * i
            left = jnp.concatenate([tiles[j][at : at + rows, :], halos[j][rim : rim + 128, :]], 0)
            right = [
                side_tiles[tile_at + at : tile_at + at + rows, :],
                side_halos[halo_at + rim : halo_at + rim + 128, :],
            ]
            right = jnp.concatenate(right, 0)
            right = right[:, :128] * after + right[:, cols - 128 :] * before
            half = dot(brs[j][i], jnp.concatenate([left, right], 1)).astype(jnp.bfloat16)
            image = dot(half, widen(bcs[j][i], wide // 128))
            image = jnp.concatenate([image[:upper], unused, image[upper:]], 0).astype(jnp.bfloat16)
            pair += [image[:, :cols], image[:, cols:] * side]
        moved.append(dot(rb[slots[j]], jnp.concatenate(pair, 1)).astype(jnp.bfloat16))
    copies = []
    for h in range(hyps):
        at = slice(h * rows, (h + 1) * rows)
        both = [jnp.concatenate([m[at, :wide], m[at, wide:]], 0) for m in moved]
        bands = [widen(cb[h, k], cols // 128) for k in slots]
        total = dot(jnp.concatenate(both, 1), jnp.concatenate(bands, 0))
        if not first:
            total = total + acc[h]
        if final:
            held, sems = refs
            held[h] = total[:rows] * lax.rsqrt(total[rows:])
            copies.append(pltpu.make_async_copy(held.at[h], out.at[h], sems.at[h]))
            copies[-1].start()
        else:
            out[h] = total
    for copy in copies:
        copy.wait()


VMEM = pl.BlockSpec(memory_space=pltpu.VMEM)
SMEM = pl.BlockSpec(memory_space=pltpu.SMEM)
PARAMS = pltpu.CompilerParams(vmem_limit_bytes=VMEM_LIMIT)


def call(kernel, specs, shapes, *args, scratch=(), flops=0, out=VMEM):
    single = not isinstance(shapes, (list, tuple))
    return pl.pallas_call(
        kernel,
        out_shape=shapes,
        in_specs=specs,
        out_specs=out if single else [out] * len(shapes),
        scratch_shapes=list(scratch),
        compiler_params=PARAMS,
        cost_estimate=pl.CostEstimate(flops=flops, bytes_accessed=0, transcendentals=0),
    )(*args)


def bf16(*shape):
    return jax.ShapeDtypeStruct(shape, jnp.bfloat16)


def side_swap(x):
    count = lax.axis_size("ty")
    if count == 2:
        return lax.ppermute(x, "ty", [(0, 1), (1, 0)])
    after = lax.ppermute(x[:, :128], "ty", [(i + 1, i) for i in range(count - 1)])
    before = lax.ppermute(x[:, x.shape[1] - 128 :], "ty", [(i, i + 1) for i in range(count - 1)])
    return jnp.concatenate([after, before], 1)


def shards(science, inv_variance, psf_taps, epoch_times, velocities):
    rows, cols = science.shape[1:]
    hyps = velocities.shape[0]
    epochs = lax.axis_size("ea")
    tx = lax.axis_size("tx")
    ty = lax.axis_size("ty")
    all_cols = cols + 128
    slots = min(GROUP, epochs)

    own = packed(science, inv_variance, psf_taps)
    tiles = [own] + [
        lax.ppermute(own, "ea", [(i, i ^ k) for i in range(epochs)]) for k in range(1, epochs)
    ]
    cut_from = own
    if epochs == slots:
        pass
    strip_a, strip_b = call(
        functools.partial(strip_kernel, rows),
        [VMEM],
        [bf16(2 * RIM, cols)] * 2,
        cut_from,
        flops=STRIP_FLOPS,
    )
    swap_b = [(i, i + 1) for i in range(1, tx - 1, 2)] + [(i + 1, i) for i in range(1, tx - 1, 2)]
    swap_a = [(i, i + 1) for i in range(0, tx - 1, 2)] + [(i + 1, i) for i in range(0, tx - 1, 2)]
    rim_b = lax.ppermute(strip_b, "tx", swap_b)
    rim_a = lax.ppermute(strip_a, "tx", swap_a)
    halo = jnp.concatenate([rim_a, rim_b], 0)
    def shift_bands(base):
        return call(
            functools.partial(shift_kernel, hyps, rows, all_cols),
            [SMEM] * 3,
            [bf16(slots, hyps * rows, 2 * rows), bf16(hyps, slots, all_cols, 128)],
            base,
            epoch_times,
            velocities,
            flops=SHIFT_FLOPS,
        )

    def blur_bands(tile):
        return call(
            functools.partial(blur_kernel, rows, cols, tx - 1),
            [VMEM],
            [bf16(2, rows + 2 * REACH, 2 * rows), bf16(2, all_cols, 128)],
            tile,
            flops=BLUR_FLOPS,
        )

    def stack(slots, tiles, halos, blurs, side_tiles, side_halos, shifts, total, final):
        args = [*tiles, *halos, *[x[0] for x in blurs], *[x[1] for x in blurs], side_tiles, side_halos, *shifts]
        if total is not None:
            args.append(total)
        shape = (hyps, rows, cols) if final else (hyps, 2 * rows, cols)
        shape = jax.ShapeDtypeStruct(shape, jnp.float32)
        spots = [(j * own.shape[0], j * halo.shape[0]) for j in range(len(slots))]
        return call(
            functools.partial(
                stack_kernel, slots, hyps, rows, cols, ty - 1, total is None, final, spots
            ),
            [VMEM] * len(args),
            shape,
            *args,
            flops=STACK_FLOPS,
            out=pl.BlockSpec(memory_space=pltpu.HBM) if final else VMEM,
            scratch=[pltpu.VMEM(shape.shape, jnp.float32), pltpu.SemaphoreType.DMA((hyps,))] if final else [],
        )

    def beside(arrays):
        return side_swap(jnp.concatenate(arrays, 0))

    if epochs == slots:
        shifts = shift_bands(jnp.zeros((1,), jnp.int32))
        *shifts, halo = lax.optimization_barrier((*shifts, halo))
        halos = [halo] + [
            lax.ppermute(halo, "ea", [(i, i ^ k) for i in range(epochs)]) for k in range(1, epochs)
        ]
        side = beside([own, halo])
        total = stack([0], [own], [halo], [blur_bands(own)], side[: own.shape[0]], side[own.shape[0] :], shifts, None, False)
        taken = [1, 3, 2]
        total, *others = lax.optimization_barrier((total, *[tiles[k] for k in taken]))
        others = [others[taken.index(k)] for k in range(1, epochs)]
        blurs = [blur_bands(x) for x in others]
        later = beside(others)
        flat = [x for pair in blurs for x in pair]
        taken = [1, 3, 2]
        total, later, *rest = lax.optimization_barrier((total, later, *flat, *[halos[k] for k in taken]))
        blurs = [rest[2 * j : 2 * j + 2] for j in range(epochs - 1)]
        rims = rest[2 * (epochs - 1) :]
        rims = [rims[taken.index(k)] for k in range(1, epochs)]
        return stack(list(range(1, epochs)), others, rims, blurs, later, beside(rims), shifts, total, True)

    halos = [halo] + [
        lax.ppermute(halo, "ea", [(i, i ^ k) for i in range(epochs)]) for k in range(1, epochs)
    ]

    def step(total, xs):
        tiles, halos, base = xs
        tiles = [tiles[k] for k in range(slots)]
        halos = [halos[k] for k in range(slots)]
        blurs = [blur_bands(x) for x in tiles]
        shifts = shift_bands(base)
        return stack(list(range(slots)), tiles, halos, blurs, beside(tiles), beside(halos), shifts, total, False), None

    split = lambda x: x.reshape((epochs // slots, slots) + x.shape[1:])
    zeros = jnp.zeros((hyps, 2 * rows, cols), jnp.float32)
    bases = jnp.arange(0, epochs, slots, dtype=jnp.int32)[:, None]
    every = (split(jnp.stack(tiles)), split(jnp.stack(halos)), bases)
    total, _ = lax.scan(step, zeros, every)
    return total[:, :rows] / jnp.sqrt(total[:, rows:])


def solution(mesh):
    in_specs = (P("ea", "tx", "ty"), P("ea", "tx", "ty"), P("ea", None), P(), P("ea", None))
    out_specs = P("ea", "tx", "ty")
    return jax.shard_map(shards, mesh=mesh, in_specs=in_specs, out_specs=out_specs, check_vma=False)
```

time: 37.3 us -> 32.2 us (0.86)
  Pallas kernels: 15.7 us -> 9.4 us
  waiting for transfers between devices: 1.49 us -> 4.48 us
  starting transfers between devices: 16.8 us -> 14.7 us
  other arithmetic: 0.01 us -> 1.22 us
  local copies, waits for them, and re-layouts: 2.65 us -> 2.1 us
    pallas_call x11 -> x8, Pallas kernels: 15.7 us -> 9.4 us  [call(): pl.pallas_call(kernel, out_shape=shapes, in_specs=specs, out_specs=out if...]
    ppermute x3, waiting for transfers between devices: 0.01 us -> 2.89 us  [shards(): lax.ppermute(halo, 'ea', [(i, i ^ k) for i in range(epochs)])]
    ppermute x8 -> x3, starting transfers between devices: 6.6 us -> 3.89 us  [side_swap(): return lax.ppermute(x, 'ty', [(0, 1), (1, 0)])]
    ppermute x3, waiting for transfers between devices: 1.26 us -> 0.01 us  [shards(): lax.ppermute(own, 'ea', [(i, i ^ k) for i in range(epochs)])]
    unnamed x11 -> x3, local copies, waits for them, and re-layouts: 2.56 us -> 1.42 us
    another operation x0 -> x2, other arithmetic: none -> 1.13 us
    ppermute x8 -> x3, waiting for transfers between devices: 0.02 us -> 1.11 us  [side_swap(): return lax.ppermute(x, 'ty', [(0, 1), (1, 0)])]
    ppermute x3, starting transfers between devices: 3.04 us -> 3.73 us  [shards(): lax.ppermute(halo, 'ea', [(i, i ^ k) for i in range(epochs)])]
  transfers between devices with their start and end apart: 16 -> 11, of which waited for: 2 -> 4; matrix products, arithmetic and copies ran while one was open for 0% -> 3% of each run, Pallas kernels for 33% -> 15%
where the time goes in v3:
time: 32.2 us; the launch traced here: 32 us
  starting transfers between devices  14.7 us (46%)
  Pallas kernels  9.4 us (29%)
  waiting for transfers between devices  4.48 us (14%)
  local copies, waits for them, and re-layouts  2.1 us (7%)
  other arithmetic  1.22 us (4%)
    pallas_call x8, Pallas kernels, call(): pl.pallas_call(kernel, out_shape=shapes, in_specs=specs, out_specs=out if...  9.4 us
    ppermute x3, starting transfers between devices, side_swap(): return lax.ppermute(x, 'ty', [(0, 1), (1, 0)])  3.89 us
    ppermute x3, starting transfers between devices, shards(): lax.ppermute(halo, 'ea', [(i, i ^ k) for i in range(epochs)])  3.73 us
    ppermute x3, starting transfers between devices, shards(): lax.ppermute(own, 'ea', [(i, i ^ k) for i in range(epochs)])  3.67 us
    ppermute x3, waiting for transfers between devices, shards(): lax.ppermute(halo, 'ea', [(i, i ^ k) for i in range(epochs)])  2.89 us
    ppermute x1, starting transfers between devices, shards(): rim_b = lax.ppermute(strip_b, 'tx', swap_b)  2.09 us
    unnamed x3, local copies, waits for them, and re-layouts  1.42 us
    ppermute x1, starting transfers between devices, shards(): rim_a = lax.ppermute(strip_a, 'tx', swap_a)  1.28 us
  transfers between devices with their start and end apart: 11, of which 4 were waited for; matrix products, arithmetic and copies ran while one was open for 3% of the time, Pallas kernels for 15%

profile of v3, /device:TPU:5, one launch (start us, length us, event | category | flops | bytes accessed | tf_op | source)
XLA Modules:
  0.0 32.0 jit_solution(17221270516043584479)
XLA Ops:
  0.0 0.7 %pad.4 = f32[1,256]{1,0:T(1,128)S(1)} pad(f32[1,9]{1,0:T(1,128)} %param.7, f32[]{:T(128)} %constant.2.clone.1), padding=0_0x0_247 | pad | bytes 1064 | tf_op jit(solution)/shard_map/jit(_pad)/pad | solution.py:39
  0.7 1.1 %fusion = (bf16[128,256]{1,0:T(8,128)(2,1)S(1)}, bf16[128,256]{1,0:T(8,128)(2,1)S(1)}) fusion(f32[1,128,256]{2,1,0:T(8,128)} %param.5, f32[1,128,256]{2,1,0:T(8,128)} %param.6), kind=kLoop, calls=%fused_computation.6 | loop fusion | flops 98304 | bytes 393216 | tf_op jit(solution)/shard_map/convert
  1.7 0.1 select_convert_fusion
  1.8 2.4 %collective-permute-start.5 = (bf16[272,256]{1,0:T(8,128)(2,1)S(1)}, bf16[272,256]{1,0:T(8,128)(2,1)S(1)}, u32[]{:S(2)}, u32[]{:S(2)}) collective-permute-start(bf16[272,256]{1,0:T(8,128)(2,1)S(1)} %pad_maximum_fusion.3.own_ref.tile_ref.refs_0_), channel_id=1, source_target_pairs={{0,2},{1,3},{2,0},{3,1},{4,6},{5,7},{6,4},{7,5},{8,10},{9,11},{10,... | collective-permute-start | bytes 417800 | tf_op jit(solution)/shard_map/ppermute | solution.py:267
  4.2 1.1 %collective-permute-start.4 = (bf16[272,256]{1,0:T(8,128)(2,1)S(1)}, bf16[272,256]{1,0:T(8,128)(2,1)S(1)}, u32[]{:S(2)}, u32[]{:S(2)}) collective-permute-start(bf16[272,256]{1,0:T(8,128)(2,1)S(1)} %pad_maximum_fusion.3.own_ref.tile_ref.refs_0_), channel_id=1, source_target_pairs={{0,3},{1,2},{2,1},{3,0},{4,7},{5,6},{6,5},{7,4},{8,11},{9,10},{10,... | collective-permute-start | bytes 417800 | tf_op jit(solution)/shard_map/ppermute | solution.py:267
  5.3 0.2 collective-permute-start.3
  5.5 1.3 %collective-permute-start = (bf16[72,256]{1,0:T(8,128)(2,1)S(1)}, bf16[72,256]{1,0:T(8,128)(2,1)S(1)}, u32[]{:S(2)}, u32[]{:S(2)}) collective-permute-start(bf16[72,256]{1,0:T(8,128)(2,1)S(1)} %get-tuple-element.37), channel_id=1, source_target_pairs={{0,8},{16,24},{8,0},{24,16},{1,9},{17,25},{9,1},{25,17},{2,10},{18... | collective-permute-start | bytes 110600 | tf_op jit(solution)/shard_map/ppermute | solution.py:282
  6.8 2.1 %collective-permute-start.1 = (bf16[72,256]{1,0:T(8,128)(2,1)S(1)}, bf16[72,256]{1,0:T(8,128)(2,1)S(1)}, u32[]{:S(2)}, u32[]{:S(2)}) collective-permute-start(bf16[72,256]{1,0:T(8,128)(2,1)S(1)} %get-tuple-element.38), channel_id=1, source_target_pairs={{8,16},{16,8},{9,17},{17,9},{10,18},{18,10},{11,19},{19,11},{12,20... | collective-permute-start | bytes 110600 | tf_op jit(solution)/shard_map/ppermute | solution.py:281
  8.9 0.8 %copy.6.speed_ref = s32[6,2]{1,0:T(8,128)S(1)} copy(s32[6,2]{0,1:T(2,128)} %param.9) | data formatting | bytes 96 | tf_op args[4]
  9.7 0.7 %copy-done = s32[4]{0:T(128)S(1)} copy-done((s32[4]{0:T(128)S(1)}, s32[4]{0:T(128)}, u32[]{:S(2)}) %copy-start) | copy-done | bytes 40
  10.3 1.9 %shard_map.55 = (bf16[4,768,256]{2,1,0:T(8,128)(2,1)S(1)}, bf16[6,4,384,128]{3,2,1,0:T(8,128)(2,1)S(1)}) custom-call(s32[1]{0:T(128)} %constant.8.clone.1.base_ref, s32[4]{0:T(128)S(1)} %copy-done, s32[6,2]{1,0:T(8,128)S(1)} %copy.6.speed_ref), custom_call_target="tpu_custom_call" | custom-call | flops 4000000000 | tf_op jit(solution)/shard_map/pallas_call | solution.py:232
  12.2 0.0 collective-permute-done
  12.2 0.5 %collective-permute-done.1 = bf16[72,256]{1,0:T(8,128)(2,1)S(1)} collective-permute-done((bf16[72,256]{1,0:T(8,128)(2,1)S(1)}, bf16[72,256]{1,0:T(8,128)(2,1)S(1)}, u32[]{:S(2)}, u32[]{:S(2)}) %collective-permute-start.1) | collective-permute-done | bytes 36896 | tf_op jit(solution)/shard_map/ppermute | solution.py:281
  12.7 2.4 %collective-permute-start.2 = (bf16[416,256]{1,0:T(8,128)(2,1)S(1)}, bf16[416,256]{1,0:T(8,128)(2,1)S(1)}, u32[]{:S(2)}, u32[]{:S(2)}) collective-permute-start(bf16[416,256]{1,0:T(8,128)(2,1)S(1)} %pad_maximum_fusion.2), channel_id=1, source_target_pairs={{0,4},{4,0},{1,5},{5,1},{2,6},{6,2},{3,7},{7,3},{8,12},{12,8},{9,1... | collective-permute-start | bytes 638984 | tf_op jit(solution)/shard_map/ppermute | solution.py:250
  15.1 0.4 %shard_map.57 = (bf16[2,192,256]{2,1,0:T(8,128)(2,1)S(1)}, bf16[2,384,128]{2,1,0:T(8,128)(2,1)S(1)}) custom-call(bf16[272,256]{1,0:T(8,128)(2,1)S(1)} %pad_maximum_fusion.3.own_ref.tile_ref.refs_0_), custom_call_target="tpu_custom_call" | custom-call | flops 4000000000 | tf_op jit(solution)/shard_map/pallas_call | solution.py:232
  15.5 2.6 %collective-permute-start.9 = (bf16[144,256]{1,0:T(8,128)(2,1)S(1)}, bf16[144,256]{1,0:T(8,128)(2,1)S(1)}, u32[]{:S(2)}, u32[]{:S(2)}) collective-permute-start(bf16[144,256]{1,0:T(8,128)(2,1)S(1)} %pad_maximum_fusion.4.refs_1_), channel_id=1, source_target_pairs={{0,2},{1,3},{2,0},{3,1},{4,6},{5,7},{6,4},{7,5},{8,10},{9,11},{10,... | collective-permute-start | bytes 221192 | tf_op jit(solution)/shard_map/ppermute | solution.py:330
  18.1 0.0 collective-permute-done.2
  18.1 1.1 %collective-permute-start.8 = (bf16[144,256]{1,0:T(8,128)(2,1)S(1)}, bf16[144,256]{1,0:T(8,128)(2,1)S(1)}, u32[]{:S(2)}, u32[]{:S(2)}) collective-permute-start(bf16[144,256]{1,0:T(8,128)(2,1)S(1)} %pad_maximum_fusion.4.refs_1_), channel_id=1, source_target_pairs={{0,3},{1,2},{2,1},{3,0},{4,7},{5,6},{6,5},{7,4},{8,11},{9,10},{10,... | collective-permute-start | bytes 221192 | tf_op jit(solution)/shard_map/ppermute | solution.py:330
  19.2 1.5 %shard_map.58.refs_16_ = f32[6,256,256]{2,1,0:T(8,128)S(1)} custom-call(bf16[272,256]{1,0:T(8,128)(2,1)S(1)} %pad_maximum_fusion.3.own_ref.tile_ref.refs_0_, bf16[144,256]{1,0:T(8,128)(2,1)S(1)} %pad_maximum_fusion.4.refs_1_, bf16[2,192,256]{2,1,0:T(8,128)(2,1)S(1)} %get-tuple-element.40.refs_2_, bf16[2,384,128]{2,1,0:T(8,128)(2,1)S(1)} %get-tuple-element.41.refs_3_, ...), custom_call_target="tpu_custom_call" | custom-call | flops 2000000000 | tf_op jit(solution)/shard_map/pallas_call | solution.py:232
  20.7 0.0 collective-permute-done.5.tile_ref.refs_1_
  20.7 0.1 collective-permute-start.7
  20.8 0.0 collective-permute-done.4.tile_ref.refs_2_
  20.8 0.0 collective-permute-done.3.tile_ref.refs_0_
  20.8 0.4 %shard_map.59 = (bf16[2,192,256]{2,1,0:T(8,128)(2,1)S(1)}, bf16[2,384,128]{2,1,0:T(8,128)(2,1)S(1)}) custom-call(bf16[272,256]{1,0:T(8,128)(2,1)S(1)} %collective-permute-done.3.tile_ref.refs_0_), custom_call_target="tpu_custom_call" | custom-call | flops 4000000000 | tf_op jit(solution)/shard_map/pallas_call | solution.py:232
  21.3 0.8 %collective-permute-start.6 = (bf16[816,256]{1,0:T(8,128)(2,1)S(1)}, bf16[816,256]{1,0:T(8,128)(2,1)S(1)}, u32[]{:S(2)}, u32[]{:S(2)}) collective-permute-start(bf16[816,256]{1,0:T(8,128)(2,1)S(1)} %pad_maximum_fusion), channel_id=1, source_target_pairs={{0,4},{4,0},{1,5},{5,1},{2,6},{6,2},{3,7},{7,3},{8,12},{12,8},{9,1... | collective-permute-start | bytes 1253384 | tf_op jit(solution)/shard_map/ppermute | solution.py:250
  22.1 0.4 %shard_map.60 = (bf16[2,192,256]{2,1,0:T(8,128)(2,1)S(1)}, bf16[2,384,128]{2,1,0:T(8,128)(2,1)S(1)}) custom-call(bf16[272,256]{1,0:T(8,128)(2,1)S(1)} %collective-permute-done.5.tile_ref.refs_1_), custom_call_target="tpu_custom_call" | custom-call | flops 4000000000 | tf_op jit(solution)/shard_map/pallas_call | solution.py:232
  22.5 0.4 %shard_map.61 = (bf16[2,192,256]{2,1,0:T(8,128)(2,1)S(1)}, bf16[2,384,128]{2,1,0:T(8,128)(2,1)S(1)}) custom-call(bf16[272,256]{1,0:T(8,128)(2,1)S(1)} %collective-permute-done.4.tile_ref.refs_2_), custom_call_target="tpu_custom_call" | custom-call | flops 4000000000 | tf_op jit(solution)/shard_map/pallas_call | solution.py:232
  22.9 0.6 %collective-permute-done.8.refs_5_ = bf16[144,256]{1,0:T(8,128)(2,1)S(1)} collective-permute-done((bf16[144,256]{1,0:T(8,128)(2,1)S(1)}, bf16[144,256]{1,0:T(8,128)(2,1)S(1)}, u32[]{:S(2)}, u32[]{:S(2)}) %collective-permute-start.8) | collective-permute-done | bytes 73760 | tf_op jit(solution)/shard_map/ppermute | solution.py:330
  23.5 2.3 %collective-permute-done.7.refs_3_ = bf16[144,256]{1,0:T(8,128)(2,1)S(1)} collective-permute-done((bf16[144,256]{1,0:T(8,128)(2,1)S(1)}, bf16[144,256]{1,0:T(8,128)(2,1)S(1)}, u32[]{:S(2)}, u32[]{:S(2)}) %collective-permute-start.7) | collective-permute-done | bytes 73760 | tf_op jit(solution)/shard_map/ppermute | solution.py:330
  25.8 0.6 %collective-permute-start.10 = (bf16[432,256]{1,0:T(8,128)(2,1)S(1)}, bf16[432,256]{1,0:T(8,128)(2,1)S(1)}, u32[]{:S(2)}, u32[]{:S(2)}) collective-permute-start(bf16[432,256]{1,0:T(8,128)(2,1)S(1)} %pad_maximum_fusion.1), channel_id=1, source_target_pairs={{0,4},{4,0},{1,5},{5,1},{2,6},{6,2},{3,7},{7,3},{8,12},{12,8},{9,1... | collective-permute-start | bytes 663560 | tf_op jit(solution)/shard_map/ppermute | solution.py:250
  26.4 1.1 %collective-permute-done.10.refs_13_ = bf16[432,256]{1,0:T(8,128)(2,1)S(1)} collective-permute-done((bf16[432,256]{1,0:T(8,128)(2,1)S(1)}, bf16[432,256]{1,0:T(8,128)(2,1)S(1)}, u32[]{:S(2)}, u32[]{:S(2)}) %collective-permute-start.10) | collective-permute-done | bytes 221216 | tf_op jit(solution)/shard_map/ppermute | solution.py:250
  27.5 4.5 %shard_map.62 = f32[6,128,256]{2,1,0:T(8,128)} custom-call(bf16[272,256]{1,0:T(8,128)(2,1)S(1)} %collective-permute-done.3.tile_ref.refs_0_, bf16[272,256]{1,0:T(8,128)(2,1)S(1)} %collective-permute-done.5.tile_ref.refs_1_, bf16[272,256]{1,0:T(8,128)(2,1)S(1)} %collective-permute-done.4.tile_ref.refs_2_, ...), custom_call_target="tpu_custom_call" | custom-call | flops 2000000000 | tf_op jit(solution)/shard_map/pallas_call | solution.py:232
  (13 shorter events, 0.1 us)
Async XLA Ops:
  1.8 18.9 %collective-permute-start.5 = (bf16[272,256]{1,0:T(8,128)(2,1)S(1)}, bf16[272,256]{1,0:T(8,128)(2,1)S(1)}, u32[]{:S(2)}, u32[]{:S(2)}) collective-permute-start(bf16[272,256]{1,0:T(8,128)(2,1)S(1)} %pad_maximum_fusion.3.own_ref.tile_ref.refs_0_), channel_id=1, source_target_pairs={{0,2},{1,3},{2,0},{3,1},{4,6},{5,7},{6,4},{7,5},{8,10},{9,11},{10,... | collective-permute-start | bytes 417800 | tf_op jit(solution)/shard_map/ppermute | solution.py:267
  4.2 16.6 %collective-permute-start.4 = (bf16[272,256]{1,0:T(8,128)(2,1)S(1)}, bf16[272,256]{1,0:T(8,128)(2,1)S(1)}, u32[]{:S(2)}, u32[]{:S(2)}) collective-permute-start(bf16[272,256]{1,0:T(8,128)(2,1)S(1)} %pad_maximum_fusion.3.own_ref.tile_ref.refs_0_), channel_id=1, source_target_pairs={{0,3},{1,2},{2,1},{3,0},{4,7},{5,6},{6,5},{7,4},{8,11},{9,10},{10,... | collective-permute-start | bytes 417800 | tf_op jit(solution)/shard_map/ppermute | solution.py:267
  5.3 15.5 %collective-permute-start.3 = (bf16[272,256]{1,0:T(8,128)(2,1)S(1)}, bf16[272,256]{1,0:T(8,128)(2,1)S(1)}, u32[]{:S(2)}, u32[]{:S(2)}) collective-permute-start(bf16[272,256]{1,0:T(8,128)(2,1)S(1)} %pad_maximum_fusion.3.own_ref.tile_ref.refs_0_), channel_id=1, source_target_pairs={{0,1},{1,0},{2,3},{3,2},{4,5},{5,4},{6,7},{7,6},{8,9},{9,8},{10,11... | collective-permute-start | bytes 417800 | tf_op jit(solution)/shard_map/ppermute | solution.py:267
  5.5 6.7 %collective-permute-start = (bf16[72,256]{1,0:T(8,128)(2,1)S(1)}, bf16[72,256]{1,0:T(8,128)(2,1)S(1)}, u32[]{:S(2)}, u32[]{:S(2)}) collective-permute-start(bf16[72,256]{1,0:T(8,128)(2,1)S(1)} %get-tuple-element.37), channel_id=1, source_target_pairs={{0,8},{16,24},{8,0},{24,16},{1,9},{17,25},{9,1},{25,17},{2,10},{18... | collective-permute-start | bytes 110600 | tf_op jit(solution)/shard_map/ppermute | solution.py:282
  6.8 5.9 %collective-permute-start.1 = (bf16[72,256]{1,0:T(8,128)(2,1)S(1)}, bf16[72,256]{1,0:T(8,128)(2,1)S(1)}, u32[]{:S(2)}, u32[]{:S(2)}) collective-permute-start(bf16[72,256]{1,0:T(8,128)(2,1)S(1)} %get-tuple-element.38), channel_id=1, source_target_pairs={{8,16},{16,8},{9,17},{17,9},{10,18},{18,10},{11,19},{19,11},{12,20... | collective-permute-start | bytes 110600 | tf_op jit(solution)/shard_map/ppermute | solution.py:281
  9.7 0.7 %copy-start = (s32[4]{0:T(128)S(1)}, s32[4]{0:T(128)}, u32[]{:S(2)}) copy-start(s32[4]{0:T(128)} %times_ref.1) | copy-start | bytes 52
  12.7 5.4 %collective-permute-start.2 = (bf16[416,256]{1,0:T(8,128)(2,1)S(1)}, bf16[416,256]{1,0:T(8,128)(2,1)S(1)}, u32[]{:S(2)}, u32[]{:S(2)}) collective-permute-start(bf16[416,256]{1,0:T(8,128)(2,1)S(1)} %pad_maximum_fusion.2), channel_id=1, source_target_pairs={{0,4},{4,0},{1,5},{5,1},{2,6},{6,2},{3,7},{7,3},{8,12},{12,8},{9,1... | collective-permute-start | bytes 638984 | tf_op jit(solution)/shard_map/ppermute | solution.py:250
  15.5 7.3 %collective-permute-start.9 = (bf16[144,256]{1,0:T(8,128)(2,1)S(1)}, bf16[144,256]{1,0:T(8,128)(2,1)S(1)}, u32[]{:S(2)}, u32[]{:S(2)}) collective-permute-start(bf16[144,256]{1,0:T(8,128)(2,1)S(1)} %pad_maximum_fusion.4.refs_1_), channel_id=1, source_target_pairs={{0,2},{1,3},{2,0},{3,1},{4,6},{5,7},{6,4},{7,5},{8,10},{9,11},{10,... | collective-permute-start | bytes 221192 | tf_op jit(solution)/shard_map/ppermute | solution.py:330
  18.1 5.4 %collective-permute-start.8 = (bf16[144,256]{1,0:T(8,128)(2,1)S(1)}, bf16[144,256]{1,0:T(8,128)(2,1)S(1)}, u32[]{:S(2)}, u32[]{:S(2)}) collective-permute-start(bf16[144,256]{1,0:T(8,128)(2,1)S(1)} %pad_maximum_fusion.4.refs_1_), channel_id=1, source_target_pairs={{0,3},{1,2},{2,1},{3,0},{4,7},{5,6},{6,5},{7,4},{8,11},{9,10},{10,... | collective-permute-start | bytes 221192 | tf_op jit(solution)/shard_map/ppermute | solution.py:330
  20.7 5.0 %collective-permute-start.7 = (bf16[144,256]{1,0:T(8,128)(2,1)S(1)}, bf16[144,256]{1,0:T(8,128)(2,1)S(1)}, u32[]{:S(2)}, u32[]{:S(2)}) collective-permute-start(bf16[144,256]{1,0:T(8,128)(2,1)S(1)} %pad_maximum_fusion.4.refs_1_), channel_id=1, source_target_pairs={{0,1},{1,0},{2,3},{3,2},{4,5},{5,4},{6,7},{7,6},{8,9},{9,8},{10,11... | collective-permute-start | bytes 221192 | tf_op jit(solution)/shard_map/ppermute | solution.py:330
  21.3 4.5 %collective-permute-start.6 = (bf16[816,256]{1,0:T(8,128)(2,1)S(1)}, bf16[816,256]{1,0:T(8,128)(2,1)S(1)}, u32[]{:S(2)}, u32[]{:S(2)}) collective-permute-start(bf16[816,256]{1,0:T(8,128)(2,1)S(1)} %pad_maximum_fusion), channel_id=1, source_target_pairs={{0,4},{4,0},{1,5},{5,1},{2,6},{6,2},{3,7},{7,3},{8,12},{12,8},{9,1... | collective-permute-start | bytes 1253384 | tf_op jit(solution)/shard_map/ppermute | solution.py:250
  25.8 1.7 %collective-permute-start.10 = (bf16[432,256]{1,0:T(8,128)(2,1)S(1)}, bf16[432,256]{1,0:T(8,128)(2,1)S(1)}, u32[]{:S(2)}, u32[]{:S(2)}) collective-permute-start(bf16[432,256]{1,0:T(8,128)(2,1)S(1)} %pad_maximum_fusion.1), channel_id=1, source_target_pairs={{0,4},{4,0},{1,5},{5,1},{2,6},{6,2},{3,7},{7,3},{8,12},{12,8},{9,1... | collective-permute-start | bytes 663560 | tf_op jit(solution)/shard_map/ppermute | solution.py:250

commit v4 on v3

--- a/solution.py
+++ b/solution.py
@@ -34,16 +34,6 @@
     return moved >> 4, weights
 
 
-def packed(science, inv_variance, psf_taps):
-    cols = science.shape[2]
-    taps = jnp.broadcast_to(jnp.pad(psf_taps, ((0, 0), (0, cols - psf_taps.shape[1]))), (16, cols))
-    hi = lax.reduce_precision(taps, 8, 7)
-    mid = lax.reduce_precision(taps - hi, 8, 7)
-    row = lax.broadcasted_iota(jnp.int32, (16, cols), 0)
-    taps = jnp.where(row == 0, hi, jnp.where(row == 1, mid, taps - hi - mid))
-    return jnp.concatenate([science[0] * inv_variance[0], inv_variance[0], taps], 0).astype(jnp.bfloat16)
-
-
 def strip_kernel(rows, own_ref, a_ref, b_ref):
     odd = lax.axis_index("tx") % 2 > 0
     heads, tails = [], []
@@ -55,6 +45,23 @@
     tail = jnp.concatenate(tails, 0)
     a_ref[...] = jnp.where(odd, head, tail).astype(jnp.bfloat16)
     b_ref[...] = jnp.where(odd, tail, head).astype(jnp.bfloat16)
+
+
+SPARE = ((0, RIM - 1), (RIM, 2 * RIM - 1), (3 * RIM - 1, 2 * RIM))
+
+
+def rim_kernel(taps_ref, a_ref, b_ref, out_ref):
+    odd = lax.axis_index("tx") % 2 > 0
+    cols = out_ref.shape[1]
+    taps = taps_ref[...]
+    taps = jnp.concatenate([taps, jnp.zeros((1, cols - taps.shape[1]), jnp.float32)], 1)
+    hi = taps.astype(jnp.bfloat16).astype(jnp.float32)
+    mid = (taps - hi).astype(jnp.bfloat16).astype(jnp.float32)
+    rims = jnp.concatenate([a_ref[...].astype(jnp.float32), b_ref[...].astype(jnp.float32)], 0)
+    row = lax.broadcasted_iota(jnp.int32, rims.shape, 0)
+    for (on_odd, on_even), part in zip(SPARE, (hi, mid, taps - hi - mid)):
+        rims = jnp.where(row == jnp.where(odd, on_odd, on_even), part, rims)
+    out_ref[...] = rims.astype(jnp.bfloat16)
 
 
 def turned(pieces, by):
@@ -110,7 +117,13 @@
     lax.fori_loop(0, rb_ref.shape[0], one, 0)
 
 
-def blur_kernel(rows, cols, last_x, tile_ref, br_ref, bc_ref):
+def blur_kernel(rows, cols, last_x, *refs):
+    count = len(refs) // 3
+    for j in range(count):
+        blur_one(rows, cols, last_x, refs[j], refs[count + 2 * j], refs[count + 2 * j + 1])
+
+
+def blur_one(rows, cols, last_x, halo_ref, br_ref, bc_ref):
     out_rows, circle = br_ref.shape[1:]
     all_cols = bc_ref.shape[1]
     here_x = lax.axis_index("tx")
@@ -118,8 +131,12 @@
     one = jnp.ones((16, 128), jnp.float32)
     keep_above = jnp.where(here_x > 0, one, 0.0).astype(jnp.bfloat16)
     keep_below = jnp.where(here_x < last_x, one, 0.0).astype(jnp.bfloat16)
-    block = tile_ref[2 * rows : 2 * rows + 16, :].astype(jnp.float32)
-    p = block[0:1] + block[1:2] + block[2:3]
+
+    def held(row):
+        block = halo_ref[row // 16 * 16 : row // 16 * 16 + 16, :].astype(jnp.float32)
+        return block[row % 16 : row % 16 + 1]
+
+    p = sum(jnp.where(odd, held(on_odd), held(on_even)) for on_odd, on_even in SPARE)
     p = p / jnp.sum(p, axis=1, keepdims=True)
     taps = [p[:, t : t + 1] for t in range(2 * PR + 1)]
     kernels = (taps, [t * t for t in taps])
@@ -262,7 +279,7 @@
     all_cols = cols + 128
     slots = min(GROUP, epochs)
 
-    own = packed(science, inv_variance, psf_taps)
+    own = jnp.concatenate([science[0] * inv_variance[0], inv_variance[0]], 0).astype(jnp.bfloat16)
     tiles = [own] + [
         lax.ppermute(own, "ea", [(i, i ^ k) for i in range(epochs)]) for k in range(1, epochs)
     ]
@@ -280,7 +297,7 @@
     swap_a = [(i, i + 1) for i in range(0, tx - 1, 2)] + [(i + 1, i) for i in range(0, tx - 1, 2)]
     rim_b = lax.ppermute(strip_b, "tx", swap_b)
     rim_a = lax.ppermute(strip_a, "tx", swap_a)
-    halo = jnp.concatenate([rim_a, rim_b], 0)
+    halo = call(rim_kernel, [VMEM] * 3, bf16(4 * RIM, cols), psf_taps, rim_a, rim_b, flops=STRIP_FLOPS)
     def shift_bands(base):
         return call(
             functools.partial(shift_kernel, hyps, rows, all_cols),
@@ -292,14 +309,16 @@
             flops=SHIFT_FLOPS,
         )
 
-    def blur_bands(tile):
-        return call(
+    def blur_bands(halos):
+        count = len(halos)
+        bands = call(
             functools.partial(blur_kernel, rows, cols, tx - 1),
-            [VMEM],
-            [bf16(2, rows + 2 * REACH, 2 * rows), bf16(2, all_cols, 128)],
-            tile,
+            [VMEM] * count,
+            [bf16(2, rows + 2 * REACH, 2 * rows), bf16(2, all_cols, 128)] * count,
+            *halos,
             flops=BLUR_FLOPS,
         )
+        return [bands[2 * j : 2 * j + 2] for j in range(count)]
 
     def stack(slots, tiles, halos, blurs, side_tiles, side_halos, shifts, total, final):
         args = [*tiles, *halos, *[x[0] for x in blurs], *[x[1] for x in blurs], side_tiles, side_halos, *shifts]
@@ -330,18 +349,15 @@
             lax.ppermute(halo, "ea", [(i, i ^ k) for i in range(epochs)]) for k in range(1, epochs)
         ]
         side = beside([own, halo])
-        total = stack([0], [own], [halo], [blur_bands(own)], side[: own.shape[0]], side[own.shape[0] :], shifts, None, False)
+        total = stack([0], [own], [halo], blur_bands([halo]), side[: own.shape[0]], side[own.shape[0] :], shifts, None, False)
         taken = [1, 3, 2]
-        total, *others = lax.optimization_barrier((total, *[tiles[k] for k in taken]))
+        others = lax.optimization_barrier([tiles[k] for k in taken])
         others = [others[taken.index(k)] for k in range(1, epochs)]
-        blurs = [blur_bands(x) for x in others]
         later = beside(others)
-        flat = [x for pair in blurs for x in pair]
         taken = [1, 3, 2]
-        total, later, *rest = lax.optimization_barrier((total, later, *flat, *[halos[k] for k in taken]))
-        blurs = [rest[2 * j : 2 * j + 2] for j in range(epochs - 1)]
-        rims = rest[2 * (epochs - 1) :]
-        rims = [rims[taken.index(k)] for k in range(1, epochs)]
+        total, later, *rest = lax.optimization_barrier((total, later, *[halos[k] for k in taken]))
+        rims = [rest[taken.index(k)] for k in range(1, epochs)]
+        blurs = blur_bands(rims)
         return stack(list(range(1, epochs)), others, rims, blurs, later, beside(rims), shifts, total, True)
 
     halos = [halo] + [
@@ -352,7 +368,7 @@
         tiles, halos, base = xs
         tiles = [tiles[k] for k in range(slots)]
         halos = [halos[k] for k in range(slots)]
-        blurs = [blur_bands(x) for x in tiles]
+        blurs = blur_bands(halos)
         shifts = shift_bands(base)
         return stack(list(range(slots)), tiles, halos, blurs, beside(tiles), beside(halos), shifts, total, False), None
 

time: 32.2 us -> 29.6 us (0.919)
  waiting for transfers between devices: 4.48 us -> 1.08 us
  starting transfers between devices: 14.7 us -> 16.3 us
  local copies, waits for them, and re-layouts: 2.1 us -> 1.44 us
    ppermute x3, waiting for transfers between devices: 2.89 us -> 0.01 us  [shards(): lax.ppermute(halo, 'ea', [(i, i ^ k) for i in range(epochs)])]
    ppermute x3, starting transfers between devices: 3.89 us -> 6.12 us  [side_swap(): return lax.ppermute(x, 'ty', [(0, 1), (1, 0)])]
    pad x1 -> x0, local copies, waits for them, and re-layouts: 0.66 us -> none  [packed(): jnp.pad(psf_taps, ((0, 0), (0, cols - psf_taps.shape[1])))]
    ppermute x3, starting transfers between devices: 3.73 us -> 3.18 us  [shards(): lax.ppermute(halo, 'ea', [(i, i ^ k) for i in range(epochs)])]
    ppermute x3, waiting for transfers between devices: 1.11 us -> 0.6 us  [side_swap(): return lax.ppermute(x, 'ty', [(0, 1), (1, 0)])]
    another operation x2 -> x1, other arithmetic: 1.13 us -> 1.05 us
    pallas_call x8 -> x7, Pallas kernels: 9.4 us -> 9.34 us  [call(): pl.pallas_call(kernel, out_shape=shapes, in_specs=specs, out_specs=out if...]
    unnamed x3 -> x5, local copies, waits for them, and re-layouts: 1.42 us -> 1.43 us
  transfers between devices with their start and end apart: 11 -> 11, of which waited for: 4 -> 2; matrix products, arithmetic and copies ran while one was open for 3% -> 3% of each run, Pallas kernels for 15% -> 17%
where the time goes in v4:
time: 29.6 us; the launch traced here: 29.5 us
  starting transfers between devices  16.3 us (55%)
  Pallas kernels  9.34 us (32%)
  local copies, waits for them, and re-layouts  1.44 us (5%)
  other arithmetic  1.12 us (4%)
  waiting for transfers between devices  1.08 us (4%)
    pallas_call x7, Pallas kernels, call(): pl.pallas_call(kernel, out_shape=shapes, in_specs=specs, out_specs=out if...  9.34 us
    ppermute x3, starting transfers between devices, side_swap(): return lax.ppermute(x, 'ty', [(0, 1), (1, 0)])  6.12 us
    ppermute x3, starting transfers between devices, shards(): lax.ppermute(own, 'ea', [(i, i ^ k) for i in range(epochs)])  3.67 us
    ppermute x3, starting transfers between devices, shards(): lax.ppermute(halo, 'ea', [(i, i ^ k) for i in range(epochs)])  3.18 us
    ppermute x1, starting transfers between devices, shards(): rim_b = lax.ppermute(strip_b, 'tx', swap_b)  2.09 us
    unnamed x5, local copies, waits for them, and re-layouts  1.43 us
    ppermute x1, starting transfers between devices, shards(): rim_a = lax.ppermute(strip_a, 'tx', swap_a)  1.28 us
    another operation x1, other arithmetic  1.05 us
  transfers between devices with their start and end apart: 11, of which 2 were waited for; matrix products, arithmetic and copies ran while one was open for 3% of the time, Pallas kernels for 17%

profile of v4, /device:TPU:5, one launch (start us, length us, event | category | flops | bytes accessed | tf_op | source)
XLA Modules:
  0.0 29.5 jit_solution(7762309427623677602)
XLA Ops:
  0.0 1.1 %fusion = (bf16[128,256]{1,0:T(8,128)(2,1)S(1)}, bf16[128,256]{1,0:T(8,128)(2,1)S(1)}) fusion(f32[1,128,256]{2,1,0:T(8,128)} %param.5, f32[1,128,256]{2,1,0:T(8,128)} %param.6), kind=kLoop, calls=%fused_computation.5 | loop fusion | flops 98304 | bytes 393216 | tf_op jit(solution)/shard_map/convert
  1.1 2.4 %collective-permute-start.2 = (bf16[256,256]{1,0:T(8,128)(2,1)S(1)}, bf16[256,256]{1,0:T(8,128)(2,1)S(1)}, u32[]{:S(2)}, u32[]{:S(2)}) collective-permute-start(bf16[256,256]{1,0:T(8,128)(2,1)S(1)} %pad_maximum_fusion.3.own_ref.refs_0_), channel_id=1, source_target_pairs={{0,2},{1,3},{2,0},{3,1},{4,6},{5,7},{6,4},{7,5},{8,10},{9,11},{10,... | collective-permute-start | bytes 393224 | tf_op jit(solution)/shard_map/ppermute | solution.py:284
  3.4 1.1 %collective-permute-start.1 = (bf16[256,256]{1,0:T(8,128)(2,1)S(1)}, bf16[256,256]{1,0:T(8,128)(2,1)S(1)}, u32[]{:S(2)}, u32[]{:S(2)}) collective-permute-start(bf16[256,256]{1,0:T(8,128)(2,1)S(1)} %pad_maximum_fusion.3.own_ref.refs_0_), channel_id=1, source_target_pairs={{0,3},{1,2},{2,1},{3,0},{4,7},{5,6},{6,5},{7,4},{8,11},{9,10},{10,... | collective-permute-start | bytes 393224 | tf_op jit(solution)/shard_map/ppermute | solution.py:284
  4.5 0.2 collective-permute-start
  4.8 1.3 %collective-permute-start.3 = (bf16[72,256]{1,0:T(8,128)(2,1)S(1)}, bf16[72,256]{1,0:T(8,128)(2,1)S(1)}, u32[]{:S(2)}, u32[]{:S(2)}) collective-permute-start(bf16[72,256]{1,0:T(8,128)(2,1)S(1)} %get-tuple-element.33), channel_id=1, source_target_pairs={{0,8},{16,24},{8,0},{24,16},{1,9},{17,25},{9,1},{25,17},{2,10},{18... | collective-permute-start | bytes 110600 | tf_op jit(solution)/shard_map/ppermute | solution.py:299
  6.1 2.1 %collective-permute-start.4 = (bf16[72,256]{1,0:T(8,128)(2,1)S(1)}, bf16[72,256]{1,0:T(8,128)(2,1)S(1)}, u32[]{:S(2)}, u32[]{:S(2)}) collective-permute-start(bf16[72,256]{1,0:T(8,128)(2,1)S(1)} %get-tuple-element.34), channel_id=1, source_target_pairs={{8,16},{16,8},{9,17},{17,9},{10,18},{18,10},{11,19},{19,11},{12,20... | collective-permute-start | bytes 110600 | tf_op jit(solution)/shard_map/ppermute | solution.py:298
  8.2 0.8 %copy.6.speed_ref = s32[6,2]{1,0:T(8,128)S(1)} copy(s32[6,2]{0,1:T(2,128)} %param.9) | data formatting | bytes 96 | tf_op args[4]
  8.9 0.0 copy-start.1
  8.9 0.7 %copy-done.1 = s32[4]{0:T(128)S(1)} copy-done((s32[4]{0:T(128)S(1)}, s32[4]{0:T(128)}, u32[]{:S(2)}) %copy-start.1) | copy-done | bytes 40
  9.6 1.9 %shard_map.55 = (bf16[4,768,256]{2,1,0:T(8,128)(2,1)S(1)}, bf16[6,4,384,128]{3,2,1,0:T(8,128)(2,1)S(1)}) custom-call(s32[1]{0:T(128)} %constant.0.clone.1.base_ref, s32[4]{0:T(128)S(1)} %copy-done.1, s32[6,2]{1,0:T(8,128)S(1)} %copy.6.speed_ref), custom_call_target="tpu_custom_call" | custom-call | flops 4000000000 | tf_op jit(solution)/shard_map/pallas_call | solution.py:249
  11.5 0.0 collective-permute-done.3.a_ref
  11.5 0.5 %collective-permute-done.4.b_ref = bf16[72,256]{1,0:T(8,128)(2,1)S(1)} collective-permute-done((bf16[72,256]{1,0:T(8,128)(2,1)S(1)}, bf16[72,256]{1,0:T(8,128)(2,1)S(1)}, u32[]{:S(2)}, u32[]{:S(2)}) %collective-permute-start.4) | collective-permute-done | bytes 36896 | tf_op jit(solution)/shard_map/ppermute | solution.py:298
  11.9 0.0 copy-done
  12.0 2.0 %collective-permute-start.9 = (bf16[144,256]{1,0:T(8,128)(2,1)S(1)}, bf16[144,256]{1,0:T(8,128)(2,1)S(1)}, u32[]{:S(2)}, u32[]{:S(2)}) collective-permute-start(bf16[144,256]{1,0:T(8,128)(2,1)S(1)} %shard_map.57.refs_0_.refs_1_), channel_id=1, source_target_pairs={{0,2},{1,3},{2,0},{3,1},{4,6},{5,7},{6,4},{7,5},{8,10},{9,11},{10,... | collective-permute-start | bytes 221192 | tf_op jit(solution)/shard_map/ppermute | solution.py:349
  14.0 1.1 %collective-permute-start.8 = (bf16[144,256]{1,0:T(8,128)(2,1)S(1)}, bf16[144,256]{1,0:T(8,128)(2,1)S(1)}, u32[]{:S(2)}, u32[]{:S(2)}) collective-permute-start(bf16[144,256]{1,0:T(8,128)(2,1)S(1)} %shard_map.57.refs_0_.refs_1_), channel_id=1, source_target_pairs={{0,3},{1,2},{2,1},{3,0},{4,7},{5,6},{6,5},{7,4},{8,11},{9,10},{10,... | collective-permute-start | bytes 221192 | tf_op jit(solution)/shard_map/ppermute | solution.py:349
  15.1 0.0 collective-permute-done.2.refs_1_
  15.1 0.1 collective-permute-start.7
  15.2 0.0 collective-permute-done.1.refs_2_
  15.2 3.5 %collective-permute-start.5 = (bf16[400,256]{1,0:T(8,128)(2,1)S(1)}, bf16[400,256]{1,0:T(8,128)(2,1)S(1)}, u32[]{:S(2)}, u32[]{:S(2)}) collective-permute-start(bf16[400,256]{1,0:T(8,128)(2,1)S(1)} %pad_maximum_fusion.2), channel_id=1, source_target_pairs={{0,4},{4,0},{1,5},{5,1},{2,6},{6,2},{3,7},{7,3},{8,12},{12,8},{9,1... | collective-permute-start | bytes 614408 | tf_op jit(solution)/shard_map/ppermute | solution.py:267
  18.8 0.0 collective-permute-done.refs_0_
  18.8 0.1 collective-permute-start.6
  18.9 0.4 %shard_map.58 = (bf16[2,192,256]{2,1,0:T(8,128)(2,1)S(1)}, bf16[2,384,128]{2,1,0:T(8,128)(2,1)S(1)}) custom-call(bf16[144,256]{1,0:T(8,128)(2,1)S(1)} %shard_map.57.refs_0_.refs_1_), custom_call_target="tpu_custom_call" | custom-call | flops 4000000000 | tf_op jit(solution)/shard_map/pallas_call | solution.py:249
  19.3 0.6 %collective-permute-done.5 = bf16[400,256]{1,0:T(8,128)(2,1)S(1)} collective-permute-done((bf16[400,256]{1,0:T(8,128)(2,1)S(1)}, bf16[400,256]{1,0:T(8,128)(2,1)S(1)}, u32[]{:S(2)}, u32[]{:S(2)}) %collective-permute-start.5) | collective-permute-done | bytes 204832 | tf_op jit(solution)/shard_map/ppermute | solution.py:267
  19.9 1.5 %shard_map.59.refs_16_ = f32[6,256,256]{2,1,0:T(8,128)S(1)} custom-call(bf16[256,256]{1,0:T(8,128)(2,1)S(1)} %pad_maximum_fusion.3.own_ref.refs_0_, bf16[144,256]{1,0:T(8,128)(2,1)S(1)} %shard_map.57.refs_0_.refs_1_, bf16[2,192,256]{2,1,0:T(8,128)(2,1)S(1)} %get-tuple-element.36.refs_2_, bf16[2,384,128]{2,1,0:T(8,128)(2,1)S(1)} %get-tuple-element.37.refs_3_, ...), custom_call_target="tpu_custom_call" | custom-call | flops 2000000000 | tf_op jit(solution)/shard_map/pallas_call | solution.py:249
  21.4 0.0 collective-permute-done.9.refs_1_.refs_4_
  21.4 0.0 collective-permute-done.8.refs_2_.refs_5_
  21.4 0.0 collective-permute-done.7.refs_0_.refs_3_
  21.4 0.0 collective-permute-done.6.refs_12_
  21.4 2.5 %collective-permute-start.10 = (bf16[432,256]{1,0:T(8,128)(2,1)S(1)}, bf16[432,256]{1,0:T(8,128)(2,1)S(1)}, u32[]{:S(2)}, u32[]{:S(2)}) collective-permute-start(bf16[432,256]{1,0:T(8,128)(2,1)S(1)} %pad_maximum_fusion.1), channel_id=1, source_target_pairs={{0,4},{4,0},{1,5},{5,1},{2,6},{6,2},{3,7},{7,3},{8,12},{12,8},{9,1... | collective-permute-start | bytes 663560 | tf_op jit(solution)/shard_map/ppermute | solution.py:267
  23.9 1.1 %shard_map.60 = (bf16[2,192,256]{2,1,0:T(8,128)(2,1)S(1)}, bf16[2,384,128]{2,1,0:T(8,128)(2,1)S(1)}, bf16[2,192,256]{2,1,0:T(8,128)(2,1)S(1)}, bf16[2,384,128]{2...) custom-call(bf16[144,256]{1,0:T(8,128)(2,1)S(1)} %collective-permute-done.7.refs_0_.refs_3_, ...), custom_call_target="tpu_custom_call" | custom-call | flops 4000000000 | tf_op jit(solution)/shard_map/pallas_call | solution.py:249
  25.0 0.0 collective-permute-done.10.refs_13_
  25.0 4.5 %shard_map.61 = f32[6,128,256]{2,1,0:T(8,128)} custom-call(bf16[256,256]{1,0:T(8,128)(2,1)S(1)} %collective-permute-done.refs_0_, bf16[256,256]{1,0:T(8,128)(2,1)S(1)} %collective-permute-done.2.refs_1_, bf16[256,256]{1,0:T(8,128)(2,1)S(1)} %collective-permute-done.1.refs_2_, bf16[144,256]{1,0:T(8,128)(2,1)S(1)} %collective-permute-done.7.refs_0_.refs_3_, ...), custom_call_target="tpu_custom_call" | custom-call | flops 2000000000 | tf_op jit(solution)/shard_map/pallas_call | solution.py:249
  (9 shorter events, 0.2 us)
Async XLA Ops:
  1.1 14.1 %collective-permute-start.2 = (bf16[256,256]{1,0:T(8,128)(2,1)S(1)}, bf16[256,256]{1,0:T(8,128)(2,1)S(1)}, u32[]{:S(2)}, u32[]{:S(2)}) collective-permute-start(bf16[256,256]{1,0:T(8,128)(2,1)S(1)} %pad_maximum_fusion.3.own_ref.refs_0_), channel_id=1, source_target_pairs={{0,2},{1,3},{2,0},{3,1},{4,6},{5,7},{6,4},{7,5},{8,10},{9,11},{10,... | collective-permute-start | bytes 393224 | tf_op jit(solution)/shard_map/ppermute | solution.py:284
  3.4 11.8 %collective-permute-start.1 = (bf16[256,256]{1,0:T(8,128)(2,1)S(1)}, bf16[256,256]{1,0:T(8,128)(2,1)S(1)}, u32[]{:S(2)}, u32[]{:S(2)}) collective-permute-start(bf16[256,256]{1,0:T(8,128)(2,1)S(1)} %pad_maximum_fusion.3.own_ref.refs_0_), channel_id=1, source_target_pairs={{0,3},{1,2},{2,1},{3,0},{4,7},{5,6},{6,5},{7,4},{8,11},{9,10},{10,... | collective-permute-start | bytes 393224 | tf_op jit(solution)/shard_map/ppermute | solution.py:284
  4.5 14.2 %collective-permute-start = (bf16[256,256]{1,0:T(8,128)(2,1)S(1)}, bf16[256,256]{1,0:T(8,128)(2,1)S(1)}, u32[]{:S(2)}, u32[]{:S(2)}) collective-permute-start(bf16[256,256]{1,0:T(8,128)(2,1)S(1)} %pad_maximum_fusion.3.own_ref.refs_0_), channel_id=1, source_target_pairs={{0,1},{1,0},{2,3},{3,2},{4,5},{5,4},{6,7},{7,6},{8,9},{9,8},{10,11... | collective-permute-start | bytes 393224 | tf_op jit(solution)/shard_map/ppermute | solution.py:284
  4.8 6.7 %collective-permute-start.3 = (bf16[72,256]{1,0:T(8,128)(2,1)S(1)}, bf16[72,256]{1,0:T(8,128)(2,1)S(1)}, u32[]{:S(2)}, u32[]{:S(2)}) collective-permute-start(bf16[72,256]{1,0:T(8,128)(2,1)S(1)} %get-tuple-element.33), channel_id=1, source_target_pairs={{0,8},{16,24},{8,0},{24,16},{1,9},{17,25},{9,1},{25,17},{2,10},{18... | collective-permute-start | bytes 110600 | tf_op jit(solution)/shard_map/ppermute | solution.py:299
  6.1 5.9 %collective-permute-start.4 = (bf16[72,256]{1,0:T(8,128)(2,1)S(1)}, bf16[72,256]{1,0:T(8,128)(2,1)S(1)}, u32[]{:S(2)}, u32[]{:S(2)}) collective-permute-start(bf16[72,256]{1,0:T(8,128)(2,1)S(1)} %get-tuple-element.34), channel_id=1, source_target_pairs={{8,16},{16,8},{9,17},{17,9},{10,18},{18,10},{11,19},{19,11},{12,20... | collective-permute-start | bytes 110600 | tf_op jit(solution)/shard_map/ppermute | solution.py:298
  8.9 0.7 %copy-start.1 = (s32[4]{0:T(128)S(1)}, s32[4]{0:T(128)}, u32[]{:S(2)}) copy-start(s32[4]{0:T(128)} %times_ref.1) | copy-start | bytes 52
  9.6 2.4 %copy-start = (f32[1,9]{1,0:T(1,128)S(1)}, f32[1,9]{1,0:T(1,128)}, u32[]{:S(2)}) copy-start(f32[1,9]{1,0:T(1,128)} %taps_ref.1) | copy-start | bytes 112
  12.0 9.4 %collective-permute-start.9 = (bf16[144,256]{1,0:T(8,128)(2,1)S(1)}, bf16[144,256]{1,0:T(8,128)(2,1)S(1)}, u32[]{:S(2)}, u32[]{:S(2)}) collective-permute-start(bf16[144,256]{1,0:T(8,128)(2,1)S(1)} %shard_map.57.refs_0_.refs_1_), channel_id=1, source_target_pairs={{0,2},{1,3},{2,0},{3,1},{4,6},{5,7},{6,4},{7,5},{8,10},{9,11},{10,... | collective-permute-start | bytes 221192 | tf_op jit(solution)/shard_map/ppermute | solution.py:349
  14.0 7.4 %collective-permute-start.8 = (bf16[144,256]{1,0:T(8,128)(2,1)S(1)}, bf16[144,256]{1,0:T(8,128)(2,1)S(1)}, u32[]{:S(2)}, u32[]{:S(2)}) collective-permute-start(bf16[144,256]{1,0:T(8,128)(2,1)S(1)} %shard_map.57.refs_0_.refs_1_), channel_id=1, source_target_pairs={{0,3},{1,2},{2,1},{3,0},{4,7},{5,6},{6,5},{7,4},{8,11},{9,10},{10,... | collective-permute-start | bytes 221192 | tf_op jit(solution)/shard_map/ppermute | solution.py:349
  15.1 6.3 %collective-permute-start.7 = (bf16[144,256]{1,0:T(8,128)(2,1)S(1)}, bf16[144,256]{1,0:T(8,128)(2,1)S(1)}, u32[]{:S(2)}, u32[]{:S(2)}) collective-permute-start(bf16[144,256]{1,0:T(8,128)(2,1)S(1)} %shard_map.57.refs_0_.refs_1_), channel_id=1, source_target_pairs={{0,1},{1,0},{2,3},{3,2},{4,5},{5,4},{6,7},{7,6},{8,9},{9,8},{10,11... | collective-permute-start | bytes 221192 | tf_op jit(solution)/shard_map/ppermute | solution.py:349
  15.2 4.6 %collective-permute-start.5 = (bf16[400,256]{1,0:T(8,128)(2,1)S(1)}, bf16[400,256]{1,0:T(8,128)(2,1)S(1)}, u32[]{:S(2)}, u32[]{:S(2)}) collective-permute-start(bf16[400,256]{1,0:T(8,128)(2,1)S(1)} %pad_maximum_fusion.2), channel_id=1, source_target_pairs={{0,4},{4,0},{1,5},{5,1},{2,6},{6,2},{3,7},{7,3},{8,12},{12,8},{9,1... | collective-permute-start | bytes 614408 | tf_op jit(solution)/shard_map/ppermute | solution.py:267
  18.8 2.6 %collective-permute-start.6 = (bf16[768,256]{1,0:T(8,128)(2,1)S(1)}, bf16[768,256]{1,0:T(8,128)(2,1)S(1)}, u32[]{:S(2)}, u32[]{:S(2)}) collective-permute-start(bf16[768,256]{1,0:T(8,128)(2,1)S(1)} %pad_maximum_fusion), channel_id=1, source_target_pairs={{0,4},{4,0},{1,5},{5,1},{2,6},{6,2},{3,7},{7,3},{8,12},{12,8},{9,1... | collective-permute-start | bytes 1179656 | tf_op jit(solution)/shard_map/ppermute | solution.py:267
  21.4 3.6 %collective-permute-start.10 = (bf16[432,256]{1,0:T(8,128)(2,1)S(1)}, bf16[432,256]{1,0:T(8,128)(2,1)S(1)}, u32[]{:S(2)}, u32[]{:S(2)}) collective-permute-start(bf16[432,256]{1,0:T(8,128)(2,1)S(1)} %pad_maximum_fusion.1), channel_id=1, source_target_pairs={{0,4},{4,0},{1,5},{5,1},{2,6},{6,2},{3,7},{7,3},{8,12},{12,8},{9,1... | collective-permute-start | bytes 663560 | tf_op jit(solution)/shard_map/ppermute | solution.py:267

commit v5 on v4

--- a/solution.py
+++ b/solution.py
@@ -117,13 +117,32 @@
     lax.fori_loop(0, rb_ref.shape[0], one, 0)
 
 
+def held_taps(halo_ref):
+    odd = lax.axis_index("tx") % 2 > 0
+
+    def held(row):
+        block = halo_ref[row // 16 * 16 : row // 16 * 16 + 16, :].astype(jnp.float32)
+        return block[row % 16 : row % 16 + 1]
+
+    return sum(jnp.where(odd, held(on_odd), held(on_even)) for on_odd, on_even in SPARE)
+
+
 def blur_kernel(rows, cols, last_x, *refs):
-    count = len(refs) // 3
+    count = len(refs) // 5
+    tiles, halos, outs = refs[:count], refs[count : 2 * count], refs[2 * count :]
     for j in range(count):
-        blur_one(rows, cols, last_x, refs[j], refs[count + 2 * j], refs[count + 2 * j + 1])
-
-
-def blur_one(rows, cols, last_x, halo_ref, br_ref, bc_ref):
+        br, bc, half = outs[3 * j : 3 * j + 3]
+        blur_bands(rows, cols, last_x, held_taps(halos[j]), br, bc)
+        for i in range(2):
+            half[i] = row_blur(rows, i, tiles[j], halos[j], br)
+
+
+def row_blur(rows, i, tile, halo, br):
+    field = [tile[i * rows : (i + 1) * rows, :], halo[16 * i : 16 * i + 128, :]]
+    return dot(br[i], jnp.concatenate(field, 0)).astype(jnp.bfloat16)
+
+
+def blur_bands(rows, cols, last_x, p, br_ref, bc_ref):
     out_rows, circle = br_ref.shape[1:]
     all_cols = bc_ref.shape[1]
     here_x = lax.axis_index("tx")
@@ -131,12 +150,6 @@
     one = jnp.ones((16, 128), jnp.float32)
     keep_above = jnp.where(here_x > 0, one, 0.0).astype(jnp.bfloat16)
     keep_below = jnp.where(here_x < last_x, one, 0.0).astype(jnp.bfloat16)
-
-    def held(row):
-        block = halo_ref[row // 16 * 16 : row // 16 * 16 + 16, :].astype(jnp.float32)
-        return block[row % 16 : row % 16 + 1]
-
-    p = sum(jnp.where(odd, held(on_odd), held(on_even)) for on_odd, on_even in SPARE)
     p = p / jnp.sum(p, axis=1, keepdims=True)
     taps = [p[:, t : t + 1] for t in range(2 * PR + 1)]
     kernels = (taps, [t * t for t in taps])
@@ -187,7 +200,7 @@
 def stack_kernel(slots, hyps, rows, cols, last_y, first, final, spots, *refs):
     count = len(slots)
     refs = list(refs)
-    tiles, halos, brs, bcs = [[refs.pop(0) for _ in range(count)] for _ in range(4)]
+    made, brs, bcs = [[refs.pop(0) for _ in range(count)] for _ in range(3)]
     side_tiles, side_halos, rb, cb = [refs.pop(0) for _ in range(4)]
     acc = None if first else refs.pop(0)
     out = refs.pop(0)
@@ -208,14 +221,13 @@
         for i in range(2):
             at = i * rows
             rim = 16 * i
-            left = jnp.concatenate([tiles[j][at : at + rows, :], halos[j][rim : rim + 128, :]], 0)
             right = [
                 side_tiles[tile_at + at : tile_at + at + rows, :],
                 side_halos[halo_at + rim : halo_at + rim + 128, :],
             ]
             right = jnp.concatenate(right, 0)
             right = right[:, :128] * after + right[:, cols - 128 :] * before
-            half = dot(brs[j][i], jnp.concatenate([left, right], 1)).astype(jnp.bfloat16)
+            half = jnp.concatenate([made[j][i], dot(brs[j][i], right).astype(jnp.bfloat16)], 1)
             image = dot(half, widen(bcs[j][i], wide // 128))
             image = jnp.concatenate([image[:upper], unused, image[upper:]], 0).astype(jnp.bfloat16)
             pair += [image[:, :cols], image[:, cols:] * side]
@@ -298,6 +310,8 @@
     rim_b = lax.ppermute(strip_b, "tx", swap_b)
     rim_a = lax.ppermute(strip_a, "tx", swap_a)
     halo = call(rim_kernel, [VMEM] * 3, bf16(4 * RIM, cols), psf_taps, rim_a, rim_b, flops=STRIP_FLOPS)
+    band_shapes = [bf16(2, rows + 2 * REACH, 2 * rows), bf16(2, all_cols, 128)]
+
     def shift_bands(base):
         return call(
             functools.partial(shift_kernel, hyps, rows, all_cols),
@@ -309,19 +323,20 @@
             flops=SHIFT_FLOPS,
         )
 
-    def blur_bands(halos):
+    def blurred(tiles, halos):
         count = len(halos)
-        bands = call(
+        made = call(
             functools.partial(blur_kernel, rows, cols, tx - 1),
-            [VMEM] * count,
-            [bf16(2, rows + 2 * REACH, 2 * rows), bf16(2, all_cols, 128)] * count,
+            [VMEM] * (2 * count),
+            [*band_shapes, bf16(2, rows + 2 * REACH, cols)] * count,
+            *tiles,
             *halos,
             flops=BLUR_FLOPS,
         )
-        return [bands[2 * j : 2 * j + 2] for j in range(count)]
-
-    def stack(slots, tiles, halos, blurs, side_tiles, side_halos, shifts, total, final):
-        args = [*tiles, *halos, *[x[0] for x in blurs], *[x[1] for x in blurs], side_tiles, side_halos, *shifts]
+        return [made[j::3] for j in range(3)]
+
+    def stack(slots, made, brs, bcs, side_tiles, side_halos, shifts, total, final):
+        args = [*made, *brs, *bcs, side_tiles, side_halos, *shifts]
         if total is not None:
             args.append(total)
         shape = (hyps, rows, cols) if final else (hyps, 2 * rows, cols)
@@ -349,16 +364,17 @@
             lax.ppermute(halo, "ea", [(i, i ^ k) for i in range(epochs)]) for k in range(1, epochs)
         ]
         side = beside([own, halo])
-        total = stack([0], [own], [halo], blur_bands([halo]), side[: own.shape[0]], side[own.shape[0] :], shifts, None, False)
-        taken = [1, 3, 2]
+        brs, bcs, made = blurred([own], [halo])
+        total = stack([0], made, brs, bcs, side[: own.shape[0]], side[own.shape[0] :], shifts, None, False)
+        taken = [3, 1, 2]
         others = lax.optimization_barrier([tiles[k] for k in taken])
         others = [others[taken.index(k)] for k in range(1, epochs)]
         later = beside(others)
         taken = [1, 3, 2]
         total, later, *rest = lax.optimization_barrier((total, later, *[halos[k] for k in taken]))
         rims = [rest[taken.index(k)] for k in range(1, epochs)]
-        blurs = blur_bands(rims)
-        return stack(list(range(1, epochs)), others, rims, blurs, later, beside(rims), shifts, total, True)
+        brs, bcs, made = blurred(others, rims)
+        return stack(list(range(1, epochs)), made, brs, bcs, later, beside(rims), shifts, total, True)
 
     halos = [halo] + [
         lax.ppermute(halo, "ea", [(i, i ^ k) for i in range(epochs)]) for k in range(1, epochs)
@@ -368,9 +384,9 @@
         tiles, halos, base = xs
         tiles = [tiles[k] for k in range(slots)]
         halos = [halos[k] for k in range(slots)]
-        blurs = blur_bands(halos)
-        shifts = shift_bands(base)
-        return stack(list(range(slots)), tiles, halos, blurs, beside(tiles), beside(halos), shifts, total, False), None
+        brs, bcs, made = blurred(tiles, halos)
+        sides = beside(tiles), beside(halos)
+        return stack(list(range(slots)), made, brs, bcs, *sides, shift_bands(base), total, False), None
 
     split = lambda x: x.reshape((epochs // slots, slots) + x.shape[1:])
     zeros = jnp.zeros((hyps, 2 * rows, cols), jnp.float32)

time: 29.6 us -> 29.1 us (0.983); the launches traced: 29.5 us -> 28.7 us
  Pallas kernels: 9.34 us -> 8.75 us
  starting transfers between devices: 16.3 us -> 15.9 us
    ppermute x3, starting transfers between devices: 6.12 us -> 5.2 us  [side_swap(): return lax.ppermute(x, 'ty', [(0, 1), (1, 0)])]
    pallas_call x7, Pallas kernels: 9.34 us -> 8.75 us  [call(): pl.pallas_call(kernel, out_shape=shapes, in_specs=specs, out_specs=out if...]
    ppermute x3, starting transfers between devices: 3.18 us -> 3.68 us  [shards(): lax.ppermute(halo, 'ea', [(i, i ^ k) for i in range(epochs)])]
  transfers between devices with their start and end apart: 11 -> 11, of which waited for: 2 -> 3; matrix products, arithmetic and copies ran while one was open for 3% -> 3% of each run, Pallas kernels for 17% -> 16%
where the time goes in v5:
time: 29.1 us; the launch traced here: 28.7 us
  starting transfers between devices  15.9 us (55%)
  Pallas kernels  8.75 us (30%)
  local copies, waits for them, and re-layouts  1.44 us (5%)
  waiting for transfers between devices  1.31 us (5%)
  other arithmetic  1.12 us (4%)
    pallas_call x7, Pallas kernels, call(): pl.pallas_call(kernel, out_shape=shapes, in_specs=specs, out_specs=out if...  8.75 us
    ppermute x3, starting transfers between devices, side_swap(): return lax.ppermute(x, 'ty', [(0, 1), (1, 0)])  5.2 us
    ppermute x3, starting transfers between devices, shards(): lax.ppermute(halo, 'ea', [(i, i ^ k) for i in range(epochs)])  3.68 us
    ppermute x3, starting transfers between devices, shards(): lax.ppermute(own, 'ea', [(i, i ^ k) for i in range(epochs)])  3.67 us
    ppermute x1, starting transfers between devices, shards(): rim_b = lax.ppermute(strip_b, 'tx', swap_b)  2.09 us
    unnamed x5, local copies, waits for them, and re-layouts  1.43 us
    ppermute x1, starting transfers between devices, shards(): rim_a = lax.ppermute(strip_a, 'tx', swap_a)  1.28 us
    another operation x1, other arithmetic  1.05 us
  transfers between devices with their start and end apart: 11, of which 3 were waited for; matrix products, arithmetic and copies ran while one was open for 3% of the time, Pallas kernels for 16%

profile of v5, /device:TPU:5, one launch (start us, length us, event | category | flops | bytes accessed | tf_op | source)
XLA Modules:
  0.0 28.7 jit_solution(16049558841017736010)
XLA Ops:
  0.0 1.1 %fusion = (bf16[128,256]{1,0:T(8,128)(2,1)S(1)}, bf16[128,256]{1,0:T(8,128)(2,1)S(1)}) fusion(f32[1,128,256]{2,1,0:T(8,128)} %param.5, f32[1,128,256]{2,1,0:T(8,128)} %param.6), kind=kLoop, calls=%fused_computation.5 | loop fusion | flops 98304 | bytes 393216 | tf_op jit(solution)/shard_map/convert
  1.1 2.4 %collective-permute-start.2 = (bf16[256,256]{1,0:T(8,128)(2,1)S(1)}, bf16[256,256]{1,0:T(8,128)(2,1)S(1)}, u32[]{:S(2)}, u32[]{:S(2)}) collective-permute-start(bf16[256,256]{1,0:T(8,128)(2,1)S(1)} %pad_maximum_fusion.3.own_ref.refs_0_), channel_id=1, source_target_pairs={{0,2},{1,3},{2,0},{3,1},{4,6},{5,7},{6,4},{7,5},{8,10},{9,11},{10,... | collective-permute-start | bytes 393224 | tf_op jit(solution)/shard_map/ppermute | solution.py:296
  3.4 1.3 %collective-permute-start.1 = (bf16[256,256]{1,0:T(8,128)(2,1)S(1)}, bf16[256,256]{1,0:T(8,128)(2,1)S(1)}, u32[]{:S(2)}, u32[]{:S(2)}) collective-permute-start(bf16[256,256]{1,0:T(8,128)(2,1)S(1)} %pad_maximum_fusion.3.own_ref.refs_0_), channel_id=1, source_target_pairs={{0,1},{1,0},{2,3},{3,2},{4,5},{5,4},{6,7},{7,6},{8,9},{9,8},{10,11... | collective-permute-start | bytes 393224 | tf_op jit(solution)/shard_map/ppermute | solution.py:296
  4.7 0.0 collective-permute-start
  4.8 1.3 %collective-permute-start.3 = (bf16[72,256]{1,0:T(8,128)(2,1)S(1)}, bf16[72,256]{1,0:T(8,128)(2,1)S(1)}, u32[]{:S(2)}, u32[]{:S(2)}) collective-permute-start(bf16[72,256]{1,0:T(8,128)(2,1)S(1)} %get-tuple-element.37), channel_id=1, source_target_pairs={{0,8},{16,24},{8,0},{24,16},{1,9},{17,25},{9,1},{25,17},{2,10},{18... | collective-permute-start | bytes 110600 | tf_op jit(solution)/shard_map/ppermute | solution.py:311
  6.1 2.1 %collective-permute-start.4 = (bf16[72,256]{1,0:T(8,128)(2,1)S(1)}, bf16[72,256]{1,0:T(8,128)(2,1)S(1)}, u32[]{:S(2)}, u32[]{:S(2)}) collective-permute-start(bf16[72,256]{1,0:T(8,128)(2,1)S(1)} %get-tuple-element.38), channel_id=1, source_target_pairs={{8,16},{16,8},{9,17},{17,9},{10,18},{18,10},{11,19},{19,11},{12,20... | collective-permute-start | bytes 110600 | tf_op jit(solution)/shard_map/ppermute | solution.py:310
  8.2 0.8 %copy.6.speed_ref = s32[6,2]{1,0:T(8,128)S(1)} copy(s32[6,2]{0,1:T(2,128)} %param.9) | data formatting | bytes 96 | tf_op args[4]
  8.9 0.0 copy-start.1
  8.9 0.7 %copy-done.1 = s32[4]{0:T(128)S(1)} copy-done((s32[4]{0:T(128)S(1)}, s32[4]{0:T(128)}, u32[]{:S(2)}) %copy-start.1) | copy-done | bytes 40
  9.6 1.9 %shard_map.55 = (bf16[4,768,256]{2,1,0:T(8,128)(2,1)S(1)}, bf16[6,4,384,128]{3,2,1,0:T(8,128)(2,1)S(1)}) custom-call(s32[1]{0:T(128)} %constant.0.clone.1.base_ref, s32[4]{0:T(128)S(1)} %copy-done.1, s32[6,2]{1,0:T(8,128)S(1)} %copy.6.speed_ref), custom_call_target="tpu_custom_call" | custom-call | flops 4000000000 | tf_op jit(solution)/shard_map/pallas_call | solution.py:261
  11.5 0.0 collective-permute-done.3.a_ref
  11.5 0.5 %collective-permute-done.4.b_ref = bf16[72,256]{1,0:T(8,128)(2,1)S(1)} collective-permute-done((bf16[72,256]{1,0:T(8,128)(2,1)S(1)}, bf16[72,256]{1,0:T(8,128)(2,1)S(1)}, u32[]{:S(2)}, u32[]{:S(2)}) %collective-permute-start.4) | collective-permute-done | bytes 36896 | tf_op jit(solution)/shard_map/ppermute | solution.py:310
  11.9 0.0 copy-done
  12.0 1.1 %collective-permute-start.9 = (bf16[144,256]{1,0:T(8,128)(2,1)S(1)}, bf16[144,256]{1,0:T(8,128)(2,1)S(1)}, u32[]{:S(2)}, u32[]{:S(2)}) collective-permute-start(bf16[144,256]{1,0:T(8,128)(2,1)S(1)} %shard_map.57.refs_1_), channel_id=1, source_target_pairs={{0,2},{1,3},{2,0},{3,1},{4,6},{5,7},{6,4},{7,5},{8,10},{9,11},{10,... | collective-permute-start | bytes 221192 | tf_op jit(solution)/shard_map/ppermute | solution.py:364
  13.1 2.3 %collective-permute-start.8 = (bf16[144,256]{1,0:T(8,128)(2,1)S(1)}, bf16[144,256]{1,0:T(8,128)(2,1)S(1)}, u32[]{:S(2)}, u32[]{:S(2)}) collective-permute-start(bf16[144,256]{1,0:T(8,128)(2,1)S(1)} %shard_map.57.refs_1_), channel_id=1, source_target_pairs={{0,3},{1,2},{2,1},{3,0},{4,7},{5,6},{6,5},{7,4},{8,11},{9,10},{10,... | collective-permute-start | bytes 221192 | tf_op jit(solution)/shard_map/ppermute | solution.py:364
  15.4 0.0 collective-permute-done.2.refs_1_
  15.4 0.3 collective-permute-start.7
  15.7 0.0 collective-permute-done.1.refs_0_
  15.7 3.2 %collective-permute-start.5 = (bf16[400,256]{1,0:T(8,128)(2,1)S(1)}, bf16[400,256]{1,0:T(8,128)(2,1)S(1)}, u32[]{:S(2)}, u32[]{:S(2)}) collective-permute-start(bf16[400,256]{1,0:T(8,128)(2,1)S(1)} %pad_maximum_fusion.2), channel_id=1, source_target_pairs={{0,4},{4,0},{1,5},{5,1},{2,6},{6,2},{3,7},{7,3},{8,12},{12,8},{9,1... | collective-permute-start | bytes 614408 | tf_op jit(solution)/shard_map/ppermute | solution.py:279
  18.9 0.0 collective-permute-done.refs_2_
  18.9 0.1 collective-permute-start.6
  19.0 0.5 %shard_map.58 = (bf16[2,192,256]{2,1,0:T(8,128)(2,1)S(1)}, bf16[2,384,128]{2,1,0:T(8,128)(2,1)S(1)}, bf16[2,192,256]{2,1,0:T(8,128)(2,1)S(1)}) custom-call(bf16[256,256]{1,0:T(8,128)(2,1)S(1)} %pad_maximum_fusion.3.own_ref.refs_0_, bf16[144,256]{1,0:T(8,128)(2,1)S(1)} %shard_map.57.refs_1_), custom_call_target="tpu_custom_call" | custom-call | flops 4000000000 | tf_op jit(solution)/shard_map/pallas_call | solution.py:261
  19.5 0.5 %collective-permute-done.5 = bf16[400,256]{1,0:T(8,128)(2,1)S(1)} collective-permute-done((bf16[400,256]{1,0:T(8,128)(2,1)S(1)}, bf16[400,256]{1,0:T(8,128)(2,1)S(1)}, u32[]{:S(2)}, u32[]{:S(2)}) %collective-permute-start.5) | collective-permute-done | bytes 204832 | tf_op jit(solution)/shard_map/ppermute | solution.py:279
  20.0 1.4 %shard_map.59.refs_13_ = f32[6,256,256]{2,1,0:T(8,128)S(1)} custom-call(bf16[2,192,256]{2,1,0:T(8,128)(2,1)S(1)} %get-tuple-element.40.refs_0_, bf16[2,192,256]{2,1,0:T(8,128)(2,1)S(1)} %get-tuple-element.41.refs_1_, bf16[2,384,128]{2,1,0:T(8,128)(2,1)S(1)} %get-tuple-element.42.refs_2_, bf16[256,256]{1,0:T(8,128)(2,1)S(1)} %slice.8.refs_3_, ...), custom_call_target="tpu_custom_call" | custom-call | flops 2000000000 | tf_op jit(solution)/shard_map/pallas_call | solution.py:261
  21.4 0.0 collective-permute-done.9.refs_4_
  21.4 0.0 collective-permute-done.8.refs_5_
  21.4 0.0 collective-permute-done.7.refs_3_
  21.4 0.0 collective-permute-done.6.refs_9_
  21.5 1.9 %collective-permute-start.10 = (bf16[432,256]{1,0:T(8,128)(2,1)S(1)}, bf16[432,256]{1,0:T(8,128)(2,1)S(1)}, u32[]{:S(2)}, u32[]{:S(2)}) collective-permute-start(bf16[432,256]{1,0:T(8,128)(2,1)S(1)} %pad_maximum_fusion.1), channel_id=1, source_target_pairs={{0,4},{4,0},{1,5},{5,1},{2,6},{6,2},{3,7},{7,3},{8,12},{12,8},{9,1... | collective-permute-start | bytes 663560 | tf_op jit(solution)/shard_map/ppermute | solution.py:279
  23.4 0.7 %shard_map.60 = (bf16[2,192,256]{2,1,0:T(8,128)(2,1)S(1)}, bf16[2,384,128]{2,1,0:T(8,128)(2,1)S(1)}, bf16[2,192,256]{2,1,0:T(8,128)(2,1)S(1)}, bf16[2,192,256]{2...) custom-call(bf16[256,256]{1,0:T(8,128)(2,1)S(1)} %collective-permute, ...), custom_call_target="tpu_custom_call" | custom-call | flops 4000000000 | tf_op jit(solution)/shard_map/pallas_call | solution.py:261
  24.1 0.4 %collective-permute-done.10.refs_10_ = bf16[432,256]{1,0:T(8,128)(2,1)S(1)} collective-permute-done((bf16[432,256]{1,0:T(8,128)(2,1)S(1)}, bf16[432,256]{1,0:T(8,128)(2,1)S(1)}, u32[]{:S(2)}, u32[]{:S(2)}) %collective-permute-start.10) | collective-permute-done | bytes 221216 | tf_op jit(solution)/shard_map/ppermute | solution.py:279
  24.5 4.2 %shard_map.61 = f32[6,128,256]{2,1,0:T(8,128)} custom-call(bf16[2,192,256]{2,1,0:T(8,128)(2,1)S(1)} %get-tuple-element.48.refs_0_, bf16[2,192,256]{2,1,0:T(8,128)(2,1)S(1)} %get-tuple-element.49.refs_1_, bf16[2,192,256]{2,1,0:T(8,128)(2,1)S(1)} %get-tuple-element.50.refs_2_, bf16[2,192,256]{2,1,0:T(8,128)(2,1)S(1)} %get-tuple-element.51.refs_3_, ...), custom_call_target="tpu_custom_call" | custom-call | flops 2000000000 | tf_op jit(solution)/shard_map/pallas_call | solution.py:261
  (9 shorter events, 0.2 us)
Async XLA Ops:
  1.1 14.3 %collective-permute-start.2 = (bf16[256,256]{1,0:T(8,128)(2,1)S(1)}, bf16[256,256]{1,0:T(8,128)(2,1)S(1)}, u32[]{:S(2)}, u32[]{:S(2)}) collective-permute-start(bf16[256,256]{1,0:T(8,128)(2,1)S(1)} %pad_maximum_fusion.3.own_ref.refs_0_), channel_id=1, source_target_pairs={{0,2},{1,3},{2,0},{3,1},{4,6},{5,7},{6,4},{7,5},{8,10},{9,11},{10,... | collective-permute-start | bytes 393224 | tf_op jit(solution)/shard_map/ppermute | solution.py:296
  3.4 12.3 %collective-permute-start.1 = (bf16[256,256]{1,0:T(8,128)(2,1)S(1)}, bf16[256,256]{1,0:T(8,128)(2,1)S(1)}, u32[]{:S(2)}, u32[]{:S(2)}) collective-permute-start(bf16[256,256]{1,0:T(8,128)(2,1)S(1)} %pad_maximum_fusion.3.own_ref.refs_0_), channel_id=1, source_target_pairs={{0,1},{1,0},{2,3},{3,2},{4,5},{5,4},{6,7},{7,6},{8,9},{9,8},{10,11... | collective-permute-start | bytes 393224 | tf_op jit(solution)/shard_map/ppermute | solution.py:296
  4.7 14.2 %collective-permute-start = (bf16[256,256]{1,0:T(8,128)(2,1)S(1)}, bf16[256,256]{1,0:T(8,128)(2,1)S(1)}, u32[]{:S(2)}, u32[]{:S(2)}) collective-permute-start(bf16[256,256]{1,0:T(8,128)(2,1)S(1)} %pad_maximum_fusion.3.own_ref.refs_0_), channel_id=1, source_target_pairs={{0,3},{1,2},{2,1},{3,0},{4,7},{5,6},{6,5},{7,4},{8,11},{9,10},{10,... | collective-permute-start | bytes 393224 | tf_op jit(solution)/shard_map/ppermute | solution.py:296
  4.8 6.7 %collective-permute-start.3 = (bf16[72,256]{1,0:T(8,128)(2,1)S(1)}, bf16[72,256]{1,0:T(8,128)(2,1)S(1)}, u32[]{:S(2)}, u32[]{:S(2)}) collective-permute-start(bf16[72,256]{1,0:T(8,128)(2,1)S(1)} %get-tuple-element.37), channel_id=1, source_target_pairs={{0,8},{16,24},{8,0},{24,16},{1,9},{17,25},{9,1},{25,17},{2,10},{18... | collective-permute-start | bytes 110600 | tf_op jit(solution)/shard_map/ppermute | solution.py:311
  6.1 5.9 %collective-permute-start.4 = (bf16[72,256]{1,0:T(8,128)(2,1)S(1)}, bf16[72,256]{1,0:T(8,128)(2,1)S(1)}, u32[]{:S(2)}, u32[]{:S(2)}) collective-permute-start(bf16[72,256]{1,0:T(8,128)(2,1)S(1)} %get-tuple-element.38), channel_id=1, source_target_pairs={{8,16},{16,8},{9,17},{17,9},{10,18},{18,10},{11,19},{19,11},{12,20... | collective-permute-start | bytes 110600 | tf_op jit(solution)/shard_map/ppermute | solution.py:310
  8.9 0.7 %copy-start.1 = (s32[4]{0:T(128)S(1)}, s32[4]{0:T(128)}, u32[]{:S(2)}) copy-start(s32[4]{0:T(128)} %times_ref.1) | copy-start | bytes 52
  9.6 2.4 %copy-start = (f32[1,9]{1,0:T(1,128)S(1)}, f32[1,9]{1,0:T(1,128)}, u32[]{:S(2)}) copy-start(f32[1,9]{1,0:T(1,128)} %taps_ref.1) | copy-start | bytes 112
  12.0 9.4 %collective-permute-start.9 = (bf16[144,256]{1,0:T(8,128)(2,1)S(1)}, bf16[144,256]{1,0:T(8,128)(2,1)S(1)}, u32[]{:S(2)}, u32[]{:S(2)}) collective-permute-start(bf16[144,256]{1,0:T(8,128)(2,1)S(1)} %shard_map.57.refs_1_), channel_id=1, source_target_pairs={{0,2},{1,3},{2,0},{3,1},{4,6},{5,7},{6,4},{7,5},{8,10},{9,11},{10,... | collective-permute-start | bytes 221192 | tf_op jit(solution)/shard_map/ppermute | solution.py:364
  13.1 8.3 %collective-permute-start.8 = (bf16[144,256]{1,0:T(8,128)(2,1)S(1)}, bf16[144,256]{1,0:T(8,128)(2,1)S(1)}, u32[]{:S(2)}, u32[]{:S(2)}) collective-permute-start(bf16[144,256]{1,0:T(8,128)(2,1)S(1)} %shard_map.57.refs_1_), channel_id=1, source_target_pairs={{0,3},{1,2},{2,1},{3,0},{4,7},{5,6},{6,5},{7,4},{8,11},{9,10},{10,... | collective-permute-start | bytes 221192 | tf_op jit(solution)/shard_map/ppermute | solution.py:364
  15.4 6.0 %collective-permute-start.7 = (bf16[144,256]{1,0:T(8,128)(2,1)S(1)}, bf16[144,256]{1,0:T(8,128)(2,1)S(1)}, u32[]{:S(2)}, u32[]{:S(2)}) collective-permute-start(bf16[144,256]{1,0:T(8,128)(2,1)S(1)} %shard_map.57.refs_1_), channel_id=1, source_target_pairs={{0,1},{1,0},{2,3},{3,2},{4,5},{5,4},{6,7},{7,6},{8,9},{9,8},{10,11... | collective-permute-start | bytes 221192 | tf_op jit(solution)/shard_map/ppermute | solution.py:364
  15.7 4.3 %collective-permute-start.5 = (bf16[400,256]{1,0:T(8,128)(2,1)S(1)}, bf16[400,256]{1,0:T(8,128)(2,1)S(1)}, u32[]{:S(2)}, u32[]{:S(2)}) collective-permute-start(bf16[400,256]{1,0:T(8,128)(2,1)S(1)} %pad_maximum_fusion.2), channel_id=1, source_target_pairs={{0,4},{4,0},{1,5},{5,1},{2,6},{6,2},{3,7},{7,3},{8,12},{12,8},{9,1... | collective-permute-start | bytes 614408 | tf_op jit(solution)/shard_map/ppermute | solution.py:279
  18.9 2.5 %collective-permute-start.6 = (bf16[768,256]{1,0:T(8,128)(2,1)S(1)}, bf16[768,256]{1,0:T(8,128)(2,1)S(1)}, u32[]{:S(2)}, u32[]{:S(2)}) collective-permute-start(bf16[768,256]{1,0:T(8,128)(2,1)S(1)} %pad_maximum_fusion), channel_id=1, source_target_pairs={{0,4},{4,0},{1,5},{5,1},{2,6},{6,2},{3,7},{7,3},{8,12},{12,8},{9,1... | collective-permute-start | bytes 1179656 | tf_op jit(solution)/shard_map/ppermute | solution.py:279
  21.5 3.0 %collective-permute-start.10 = (bf16[432,256]{1,0:T(8,128)(2,1)S(1)}, bf16[432,256]{1,0:T(8,128)(2,1)S(1)}, u32[]{:S(2)}, u32[]{:S(2)}) collective-permute-start(bf16[432,256]{1,0:T(8,128)(2,1)S(1)} %pad_maximum_fusion.1), channel_id=1, source_target_pairs={{0,4},{4,0},{1,5},{5,1},{2,6},{6,2},{3,7},{7,3},{8,12},{12,8},{9,1... | collective-permute-start | bytes 663560 | tf_op jit(solution)/shard_map/ppermute | solution.py:279

commit v6 on v5

--- a/solution.py
+++ b/solution.py
@@ -128,11 +128,11 @@
 
 
 def blur_kernel(rows, cols, last_x, *refs):
-    count = len(refs) // 5
+    count = len(refs) // 6
     tiles, halos, outs = refs[:count], refs[count : 2 * count], refs[2 * count :]
     for j in range(count):
-        br, bc, half = outs[3 * j : 3 * j + 3]
-        blur_bands(rows, cols, last_x, held_taps(halos[j]), br, bc)
+        br, bc, scale, half = outs[4 * j : 4 * j + 4]
+        blur_bands(rows, cols, last_x, held_taps(halos[j]), br, bc, scale)
         for i in range(2):
             half[i] = row_blur(rows, i, tiles[j], halos[j], br)
 
@@ -142,7 +142,7 @@
     return dot(br[i], jnp.concatenate(field, 0)).astype(jnp.bfloat16)
 
 
-def blur_bands(rows, cols, last_x, p, br_ref, bc_ref):
+def blur_bands(rows, cols, last_x, p, br_ref, bc_ref, scale_ref):
     out_rows, circle = br_ref.shape[1:]
     all_cols = bc_ref.shape[1]
     here_x = lax.axis_index("tx")
@@ -158,6 +158,9 @@
     col_base = jnp.where(col_base < 0, col_base + all_cols, col_base)
     lane = lax.broadcasted_iota(jnp.int32, (16, 128), 1)
     for i in range(2):
+        rounded = sum(t.astype(jnp.bfloat16).astype(jnp.float32) for t in kernels[i])
+        ratio = sum(kernels[i]) / rounded
+        scale_ref[i] = jnp.broadcast_to(ratio * ratio, scale_ref.shape[1:])
         pieces = cut(select(row_base, kernels[i]))
         first_a = (RIM - 16) * i
         first_b = 2 * RIM + first_a
@@ -200,7 +203,7 @@
 def stack_kernel(slots, hyps, rows, cols, last_y, first, final, spots, *refs):
     count = len(slots)
     refs = list(refs)
-    made, brs, bcs = [[refs.pop(0) for _ in range(count)] for _ in range(3)]
+    made, brs, bcs, scales = [[refs.pop(0) for _ in range(count)] for _ in range(4)]
     side_tiles, side_halos, rb, cb = [refs.pop(0) for _ in range(4)]
     acc = None if first else refs.pop(0)
     out = refs.pop(0)
@@ -228,7 +231,7 @@
             right = jnp.concatenate(right, 0)
             right = right[:, :128] * after + right[:, cols - 128 :] * before
             half = jnp.concatenate([made[j][i], dot(brs[j][i], right).astype(jnp.bfloat16)], 1)
-            image = dot(half, widen(bcs[j][i], wide // 128))
+            image = dot(half, widen(bcs[j][i], wide // 128)) * scales[j][i, 0:1, :]
             image = jnp.concatenate([image[:upper], unused, image[upper:]], 0).astype(jnp.bfloat16)
             pair += [image[:, :cols], image[:, cols:] * side]
         moved.append(dot(rb[slots[j]], jnp.concatenate(pair, 1)).astype(jnp.bfloat16))
@@ -310,7 +313,11 @@
     rim_b = lax.ppermute(strip_b, "tx", swap_b)
     rim_a = lax.ppermute(strip_a, "tx", swap_a)
     halo = call(rim_kernel, [VMEM] * 3, bf16(4 * RIM, cols), psf_taps, rim_a, rim_b, flops=STRIP_FLOPS)
-    band_shapes = [bf16(2, rows + 2 * REACH, 2 * rows), bf16(2, all_cols, 128)]
+    band_shapes = [
+        bf16(2, rows + 2 * REACH, 2 * rows),
+        bf16(2, all_cols, 128),
+        jax.ShapeDtypeStruct((2, 8, all_cols), jnp.float32),
+    ]
 
     def shift_bands(base):
         return call(
@@ -333,10 +340,10 @@
             *halos,
             flops=BLUR_FLOPS,
         )
-        return [made[j::3] for j in range(3)]
-
-    def stack(slots, made, brs, bcs, side_tiles, side_halos, shifts, total, final):
-        args = [*made, *brs, *bcs, side_tiles, side_halos, *shifts]
+        return [made[j::4] for j in range(4)]
+
+    def stack(slots, made, blurs, side_tiles, side_halos, shifts, total, final):
+        args = [*made, *[x for kind in blurs for x in kind], side_tiles, side_halos, *shifts]
         if total is not None:
             args.append(total)
         shape = (hyps, rows, cols) if final else (hyps, 2 * rows, cols)
@@ -364,8 +371,8 @@
             lax.ppermute(halo, "ea", [(i, i ^ k) for i in range(epochs)]) for k in range(1, epochs)
         ]
         side = beside([own, halo])
-        brs, bcs, made = blurred([own], [halo])
-        total = stack([0], made, brs, bcs, side[: own.shape[0]], side[own.shape[0] :], shifts, None, False)
+        *blurs, made = blurred([own], [halo])
+        total = stack([0], made, blurs, side[: own.shape[0]], side[own.shape[0] :], shifts, None, False)
         taken = [3, 1, 2]
         others = lax.optimization_barrier([tiles[k] for k in taken])
         others = [others[taken.index(k)] for k in range(1, epochs)]
@@ -373,8 +380,8 @@
         taken = [1, 3, 2]
         total, later, *rest = lax.optimization_barrier((total, later, *[halos[k] for k in taken]))
         rims = [rest[taken.index(k)] for k in range(1, epochs)]
-        brs, bcs, made = blurred(others, rims)
-        return stack(list(range(1, epochs)), made, brs, bcs, later, beside(rims), shifts, total, True)
+        *blurs, made = blurred(others, rims)
+        return stack(list(range(1, epochs)), made, blurs, later, beside(rims), shifts, total, True)
 
     halos = [halo] + [
         lax.ppermute(halo, "ea", [(i, i ^ k) for i in range(epochs)]) for k in range(1, epochs)
@@ -384,9 +391,9 @@
         tiles, halos, base = xs
         tiles = [tiles[k] for k in range(slots)]
         halos = [halos[k] for k in range(slots)]
-        brs, bcs, made = blurred(tiles, halos)
+        *blurs, made = blurred(tiles, halos)
         sides = beside(tiles), beside(halos)
-        return stack(list(range(slots)), made, brs, bcs, *sides, shift_bands(base), total, False), None
+        return stack(list(range(slots)), made, blurs, *sides, shift_bands(base), total, False), None
 
     split = lambda x: x.reshape((epochs // slots, slots) + x.shape[1:])
     zeros = jnp.zeros((hyps, 2 * rows, cols), jnp.float32)

time: 29.1 us -> 29 us (level)
  no operation moved by 1% of the time
where the time goes in v6:
time: 29 us; the launch traced here: 28.6 us
  starting transfers between devices  15.9 us (55%)
  Pallas kernels  8.81 us (30%)
  local copies, waits for them, and re-layouts  1.44 us (5%)
  waiting for transfers between devices  1.17 us (4%)
  other arithmetic  1.12 us (4%)
    pallas_call x7, Pallas kernels, call(): pl.pallas_call(kernel, out_shape=shapes, in_specs=specs, out_specs=out if...  8.81 us
    ppermute x3, starting transfers between devices, side_swap(): return lax.ppermute(x, 'ty', [(0, 1), (1, 0)])  5.2 us
    ppermute x3, starting transfers between devices, shards(): lax.ppermute(halo, 'ea', [(i, i ^ k) for i in range(epochs)])  3.68 us
    ppermute x3, starting transfers between devices, shards(): lax.ppermute(own, 'ea', [(i, i ^ k) for i in range(epochs)])  3.67 us
    ppermute x1, starting transfers between devices, shards(): rim_b = lax.ppermute(strip_b, 'tx', swap_b)  2.09 us
    unnamed x5, local copies, waits for them, and re-layouts  1.43 us
    ppermute x1, starting transfers between devices, shards(): rim_a = lax.ppermute(strip_a, 'tx', swap_a)  1.28 us
    another operation x1, other arithmetic  1.05 us
  transfers between devices with their start and end apart: 11, of which 3 were waited for; matrix products, arithmetic and copies ran while one was open for 3% of the time, Pallas kernels for 16%

profile of v6, /device:TPU:5, one launch (start us, length us, event | category | flops | bytes accessed | tf_op | source)
XLA Modules:
  0.0 28.6 jit_solution(17678103633101238755)
XLA Ops:
  0.0 1.1 %fusion = (bf16[128,256]{1,0:T(8,128)(2,1)S(1)}, bf16[128,256]{1,0:T(8,128)(2,1)S(1)}) fusion(f32[1,128,256]{2,1,0:T(8,128)} %param.5, f32[1,128,256]{2,1,0:T(8,128)} %param.6), kind=kLoop, calls=%fused_computation.5 | loop fusion | flops 98304 | bytes 393216 | tf_op jit(solution)/shard_map/convert
  1.1 2.4 %collective-permute-start.2 = (bf16[256,256]{1,0:T(8,128)(2,1)S(1)}, bf16[256,256]{1,0:T(8,128)(2,1)S(1)}, u32[]{:S(2)}, u32[]{:S(2)}) collective-permute-start(bf16[256,256]{1,0:T(8,128)(2,1)S(1)} %pad_maximum_fusion.3.own_ref.refs_0_), channel_id=1, source_target_pairs={{0,2},{1,3},{2,0},{3,1},{4,6},{5,7},{6,4},{7,5},{8,10},{9,11},{10,... | collective-permute-start | bytes 393224 | tf_op jit(solution)/shard_map/ppermute | solution.py:299
  3.4 1.3 %collective-permute-start.1 = (bf16[256,256]{1,0:T(8,128)(2,1)S(1)}, bf16[256,256]{1,0:T(8,128)(2,1)S(1)}, u32[]{:S(2)}, u32[]{:S(2)}) collective-permute-start(bf16[256,256]{1,0:T(8,128)(2,1)S(1)} %pad_maximum_fusion.3.own_ref.refs_0_), channel_id=1, source_target_pairs={{0,1},{1,0},{2,3},{3,2},{4,5},{5,4},{6,7},{7,6},{8,9},{9,8},{10,11... | collective-permute-start | bytes 393224 | tf_op jit(solution)/shard_map/ppermute | solution.py:299
  4.7 0.0 collective-permute-start
  4.8 1.3 %collective-permute-start.3 = (bf16[72,256]{1,0:T(8,128)(2,1)S(1)}, bf16[72,256]{1,0:T(8,128)(2,1)S(1)}, u32[]{:S(2)}, u32[]{:S(2)}) collective-permute-start(bf16[72,256]{1,0:T(8,128)(2,1)S(1)} %get-tuple-element.41), channel_id=1, source_target_pairs={{0,8},{16,24},{8,0},{24,16},{1,9},{17,25},{9,1},{25,17},{2,10},{18... | collective-permute-start | bytes 110600 | tf_op jit(solution)/shard_map/ppermute | solution.py:314
  6.1 2.1 %collective-permute-start.4 = (bf16[72,256]{1,0:T(8,128)(2,1)S(1)}, bf16[72,256]{1,0:T(8,128)(2,1)S(1)}, u32[]{:S(2)}, u32[]{:S(2)}) collective-permute-start(bf16[72,256]{1,0:T(8,128)(2,1)S(1)} %get-tuple-element.42), channel_id=1, source_target_pairs={{8,16},{16,8},{9,17},{17,9},{10,18},{18,10},{11,19},{19,11},{12,20... | collective-permute-start | bytes 110600 | tf_op jit(solution)/shard_map/ppermute | solution.py:313
  8.2 0.8 %copy.6.speed_ref = s32[6,2]{1,0:T(8,128)S(1)} copy(s32[6,2]{0,1:T(2,128)} %param.9) | data formatting | bytes 96 | tf_op args[4]
  8.9 0.0 copy-start.1
  8.9 0.7 %copy-done.1 = s32[4]{0:T(128)S(1)} copy-done((s32[4]{0:T(128)S(1)}, s32[4]{0:T(128)}, u32[]{:S(2)}) %copy-start.1) | copy-done | bytes 40
  9.6 1.9 %shard_map.55 = (bf16[4,768,256]{2,1,0:T(8,128)(2,1)S(1)}, bf16[6,4,384,128]{3,2,1,0:T(8,128)(2,1)S(1)}) custom-call(s32[1]{0:T(128)} %constant.0.clone.1.base_ref, s32[4]{0:T(128)S(1)} %copy-done.1, s32[6,2]{1,0:T(8,128)S(1)} %copy.6.speed_ref), custom_call_target="tpu_custom_call" | custom-call | flops 4000000000 | tf_op jit(solution)/shard_map/pallas_call | solution.py:264
  11.5 0.0 collective-permute-done.3.a_ref
  11.5 0.5 %collective-permute-done.4.b_ref = bf16[72,256]{1,0:T(8,128)(2,1)S(1)} collective-permute-done((bf16[72,256]{1,0:T(8,128)(2,1)S(1)}, bf16[72,256]{1,0:T(8,128)(2,1)S(1)}, u32[]{:S(2)}, u32[]{:S(2)}) %collective-permute-start.4) | collective-permute-done | bytes 36896 | tf_op jit(solution)/shard_map/ppermute | solution.py:313
  11.9 0.0 copy-done
  12.0 1.1 %collective-permute-start.9 = (bf16[144,256]{1,0:T(8,128)(2,1)S(1)}, bf16[144,256]{1,0:T(8,128)(2,1)S(1)}, u32[]{:S(2)}, u32[]{:S(2)}) collective-permute-start(bf16[144,256]{1,0:T(8,128)(2,1)S(1)} %shard_map.57.refs_1_), channel_id=1, source_target_pairs={{0,2},{1,3},{2,0},{3,1},{4,6},{5,7},{6,4},{7,5},{8,10},{9,11},{10,... | collective-permute-start | bytes 221192 | tf_op jit(solution)/shard_map/ppermute | solution.py:371
  13.1 2.3 %collective-permute-start.8 = (bf16[144,256]{1,0:T(8,128)(2,1)S(1)}, bf16[144,256]{1,0:T(8,128)(2,1)S(1)}, u32[]{:S(2)}, u32[]{:S(2)}) collective-permute-start(bf16[144,256]{1,0:T(8,128)(2,1)S(1)} %shard_map.57.refs_1_), channel_id=1, source_target_pairs={{0,3},{1,2},{2,1},{3,0},{4,7},{5,6},{6,5},{7,4},{8,11},{9,10},{10,... | collective-permute-start | bytes 221192 | tf_op jit(solution)/shard_map/ppermute | solution.py:371
  15.4 0.0 collective-permute-done.2.refs_1_
  15.4 0.3 collective-permute-start.7
  15.7 0.0 collective-permute-done.1.refs_0_
  15.7 3.2 %collective-permute-start.5 = (bf16[400,256]{1,0:T(8,128)(2,1)S(1)}, bf16[400,256]{1,0:T(8,128)(2,1)S(1)}, u32[]{:S(2)}, u32[]{:S(2)}) collective-permute-start(bf16[400,256]{1,0:T(8,128)(2,1)S(1)} %pad_maximum_fusion.2), channel_id=1, source_target_pairs={{0,4},{4,0},{1,5},{5,1},{2,6},{6,2},{3,7},{7,3},{8,12},{12,8},{9,1... | collective-permute-start | bytes 614408 | tf_op jit(solution)/shard_map/ppermute | solution.py:282
  18.9 0.0 collective-permute-done.refs_2_
  18.9 0.1 collective-permute-start.6
  19.0 0.5 %shard_map.58 = (bf16[2,192,256]{2,1,0:T(8,128)(2,1)S(1)}, bf16[2,384,128]{2,1,0:T(8,128)(2,1)S(1)}, f32[2,8,384]{2,1,0:T(8,128)S(1)}, bf16[2,192,256]{2,1,0:T(8,128)(2,1)S(1)}) custom-call(bf16[256,256]{1,0:T(8,128)(2,1)S(1)} %pad_maximum_fusion.3.own_ref.refs_0_, bf16[144,256]{1,0:T(8,128)(2,1)S(1)} %shard_map.57.refs_1_), custom_call_target="tpu_custom_call" | custom-call | flops 4000000000 | tf_op jit(solution)/shard_map/pallas_call | solution.py:264
  19.6 0.4 %collective-permute-done.5 = bf16[400,256]{1,0:T(8,128)(2,1)S(1)} collective-permute-done((bf16[400,256]{1,0:T(8,128)(2,1)S(1)}, bf16[400,256]{1,0:T(8,128)(2,1)S(1)}, u32[]{:S(2)}, u32[]{:S(2)}) %collective-permute-start.5) | collective-permute-done | bytes 204832 | tf_op jit(solution)/shard_map/ppermute | solution.py:282
  20.0 1.4 %shard_map.59.refs_16_ = f32[6,256,256]{2,1,0:T(8,128)S(1)} custom-call(bf16[2,192,256]{2,1,0:T(8,128)(2,1)S(1)} %get-tuple-element.44.refs_0_, bf16[2,192,256]{2,1,0:T(8,128)(2,1)S(1)} %get-tuple-element.45.refs_1_, bf16[2,384,128]{2,1,0:T(8,128)(2,1)S(1)} %get-tuple-element.46.refs_2_, f32[2,8,384]{2,1,0:T(8,128)S(1)} %get-tuple-element.47.refs_3_, ...), custom_call_target="tpu_custom_call" | custom-call | flops 2000000000 | tf_op jit(solution)/shard_map/pallas_call | solution.py:264
  21.4 0.0 collective-permute-done.9.refs_4_
  21.4 0.0 collective-permute-done.8.refs_5_
  21.4 0.0 collective-permute-done.7.refs_3_
  21.4 0.0 collective-permute-done.6.refs_12_
  21.5 1.9 %collective-permute-start.10 = (bf16[432,256]{1,0:T(8,128)(2,1)S(1)}, bf16[432,256]{1,0:T(8,128)(2,1)S(1)}, u32[]{:S(2)}, u32[]{:S(2)}) collective-permute-start(bf16[432,256]{1,0:T(8,128)(2,1)S(1)} %pad_maximum_fusion.1), channel_id=1, source_target_pairs={{0,4},{4,0},{1,5},{5,1},{2,6},{6,2},{3,7},{7,3},{8,12},{12,8},{9,1... | collective-permute-start | bytes 663560 | tf_op jit(solution)/shard_map/ppermute | solution.py:282
  23.4 0.8 %shard_map.60 = (bf16[2,192,256]{2,1,0:T(8,128)(2,1)S(1)}, bf16[2,384,128]{2,1,0:T(8,128)(2,1)S(1)}, f32[2,8,384]{2,1,0:T(8,128)S(1)}, bf16[2,192,256]{2,1,0:T(8...) custom-call(bf16[256,256]{1,0:T(8,128)(2,1)S(1)} %collective-permute, ...), custom_call_target="tpu_custom_call" | custom-call | flops 4000000000 | tf_op jit(solution)/shard_map/pallas_call | solution.py:264
  24.2 0.3 collective-permute-done.10.refs_13_
  24.5 4.1 %shard_map.61 = f32[6,128,256]{2,1,0:T(8,128)} custom-call(bf16[2,192,256]{2,1,0:T(8,128)(2,1)S(1)} %get-tuple-element.53.refs_0_, bf16[2,192,256]{2,1,0:T(8,128)(2,1)S(1)} %get-tuple-element.54.refs_1_, bf16[2,192,256]{2,1,0:T(8,128)(2,1)S(1)} %get-tuple-element.55.refs_2_, bf16[2,192,256]{2,1,0:T(8,128)(2,1)S(1)} %get-tuple-element.56.refs_3_, ...), custom_call_target="tpu_custom_call" | custom-call | flops 2000000000 | tf_op jit(solution)/shard_map/pallas_call | solution.py:264
  (9 shorter events, 0.2 us)
Async XLA Ops:
  1.1 14.3 %collective-permute-start.2 = (bf16[256,256]{1,0:T(8,128)(2,1)S(1)}, bf16[256,256]{1,0:T(8,128)(2,1)S(1)}, u32[]{:S(2)}, u32[]{:S(2)}) collective-permute-start(bf16[256,256]{1,0:T(8,128)(2,1)S(1)} %pad_maximum_fusion.3.own_ref.refs_0_), channel_id=1, source_target_pairs={{0,2},{1,3},{2,0},{3,1},{4,6},{5,7},{6,4},{7,5},{8,10},{9,11},{10,... | collective-permute-start | bytes 393224 | tf_op jit(solution)/shard_map/ppermute | solution.py:299
  3.4 12.3 %collective-permute-start.1 = (bf16[256,256]{1,0:T(8,128)(2,1)S(1)}, bf16[256,256]{1,0:T(8,128)(2,1)S(1)}, u32[]{:S(2)}, u32[]{:S(2)}) collective-permute-start(bf16[256,256]{1,0:T(8,128)(2,1)S(1)} %pad_maximum_fusion.3.own_ref.refs_0_), channel_id=1, source_target_pairs={{0,1},{1,0},{2,3},{3,2},{4,5},{5,4},{6,7},{7,6},{8,9},{9,8},{10,11... | collective-permute-start | bytes 393224 | tf_op jit(solution)/shard_map/ppermute | solution.py:299
  4.7 14.2 %collective-permute-start = (bf16[256,256]{1,0:T(8,128)(2,1)S(1)}, bf16[256,256]{1,0:T(8,128)(2,1)S(1)}, u32[]{:S(2)}, u32[]{:S(2)}) collective-permute-start(bf16[256,256]{1,0:T(8,128)(2,1)S(1)} %pad_maximum_fusion.3.own_ref.refs_0_), channel_id=1, source_target_pairs={{0,3},{1,2},{2,1},{3,0},{4,7},{5,6},{6,5},{7,4},{8,11},{9,10},{10,... | collective-permute-start | bytes 393224 | tf_op jit(solution)/shard_map/ppermute | solution.py:299
  4.8 6.7 %collective-permute-start.3 = (bf16[72,256]{1,0:T(8,128)(2,1)S(1)}, bf16[72,256]{1,0:T(8,128)(2,1)S(1)}, u32[]{:S(2)}, u32[]{:S(2)}) collective-permute-start(bf16[72,256]{1,0:T(8,128)(2,1)S(1)} %get-tuple-element.41), channel_id=1, source_target_pairs={{0,8},{16,24},{8,0},{24,16},{1,9},{17,25},{9,1},{25,17},{2,10},{18... | collective-permute-start | bytes 110600 | tf_op jit(solution)/shard_map/ppermute | solution.py:314
  6.1 5.9 %collective-permute-start.4 = (bf16[72,256]{1,0:T(8,128)(2,1)S(1)}, bf16[72,256]{1,0:T(8,128)(2,1)S(1)}, u32[]{:S(2)}, u32[]{:S(2)}) collective-permute-start(bf16[72,256]{1,0:T(8,128)(2,1)S(1)} %get-tuple-element.42), channel_id=1, source_target_pairs={{8,16},{16,8},{9,17},{17,9},{10,18},{18,10},{11,19},{19,11},{12,20... | collective-permute-start | bytes 110600 | tf_op jit(solution)/shard_map/ppermute | solution.py:313
  8.9 0.7 %copy-start.1 = (s32[4]{0:T(128)S(1)}, s32[4]{0:T(128)}, u32[]{:S(2)}) copy-start(s32[4]{0:T(128)} %times_ref.1) | copy-start | bytes 52
  9.6 2.4 %copy-start = (f32[1,9]{1,0:T(1,128)S(1)}, f32[1,9]{1,0:T(1,128)}, u32[]{:S(2)}) copy-start(f32[1,9]{1,0:T(1,128)} %taps_ref.1) | copy-start | bytes 112
  12.0 9.4 %collective-permute-start.9 = (bf16[144,256]{1,0:T(8,128)(2,1)S(1)}, bf16[144,256]{1,0:T(8,128)(2,1)S(1)}, u32[]{:S(2)}, u32[]{:S(2)}) collective-permute-start(bf16[144,256]{1,0:T(8,128)(2,1)S(1)} %shard_map.57.refs_1_), channel_id=1, source_target_pairs={{0,2},{1,3},{2,0},{3,1},{4,6},{5,7},{6,4},{7,5},{8,10},{9,11},{10,... | collective-permute-start | bytes 221192 | tf_op jit(solution)/shard_map/ppermute | solution.py:371
  13.1 8.3 %collective-permute-start.8 = (bf16[144,256]{1,0:T(8,128)(2,1)S(1)}, bf16[144,256]{1,0:T(8,128)(2,1)S(1)}, u32[]{:S(2)}, u32[]{:S(2)}) collective-permute-start(bf16[144,256]{1,0:T(8,128)(2,1)S(1)} %shard_map.57.refs_1_), channel_id=1, source_target_pairs={{0,3},{1,2},{2,1},{3,0},{4,7},{5,6},{6,5},{7,4},{8,11},{9,10},{10,... | collective-permute-start | bytes 221192 | tf_op jit(solution)/shard_map/ppermute | solution.py:371
  15.4 6.0 %collective-permute-start.7 = (bf16[144,256]{1,0:T(8,128)(2,1)S(1)}, bf16[144,256]{1,0:T(8,128)(2,1)S(1)}, u32[]{:S(2)}, u32[]{:S(2)}) collective-permute-start(bf16[144,256]{1,0:T(8,128)(2,1)S(1)} %shard_map.57.refs_1_), channel_id=1, source_target_pairs={{0,1},{1,0},{2,3},{3,2},{4,5},{5,4},{6,7},{7,6},{8,9},{9,8},{10,11... | collective-permute-start | bytes 221192 | tf_op jit(solution)/shard_map/ppermute | solution.py:371
  15.7 4.3 %collective-permute-start.5 = (bf16[400,256]{1,0:T(8,128)(2,1)S(1)}, bf16[400,256]{1,0:T(8,128)(2,1)S(1)}, u32[]{:S(2)}, u32[]{:S(2)}) collective-permute-start(bf16[400,256]{1,0:T(8,128)(2,1)S(1)} %pad_maximum_fusion.2), channel_id=1, source_target_pairs={{0,4},{4,0},{1,5},{5,1},{2,6},{6,2},{3,7},{7,3},{8,12},{12,8},{9,1... | collective-permute-start | bytes 614408 | tf_op jit(solution)/shard_map/ppermute | solution.py:282
  18.9 2.5 %collective-permute-start.6 = (bf16[768,256]{1,0:T(8,128)(2,1)S(1)}, bf16[768,256]{1,0:T(8,128)(2,1)S(1)}, u32[]{:S(2)}, u32[]{:S(2)}) collective-permute-start(bf16[768,256]{1,0:T(8,128)(2,1)S(1)} %pad_maximum_fusion), channel_id=1, source_target_pairs={{0,4},{4,0},{1,5},{5,1},{2,6},{6,2},{3,7},{7,3},{8,12},{12,8},{9,1... | collective-permute-start | bytes 1179656 | tf_op jit(solution)/shard_map/ppermute | solution.py:282
  21.5 3.0 %collective-permute-start.10 = (bf16[432,256]{1,0:T(8,128)(2,1)S(1)}, bf16[432,256]{1,0:T(8,128)(2,1)S(1)}, u32[]{:S(2)}, u32[]{:S(2)}) collective-permute-start(bf16[432,256]{1,0:T(8,128)(2,1)S(1)} %pad_maximum_fusion.1), channel_id=1, source_target_pairs={{0,4},{4,0},{1,5},{5,1},{2,6},{6,2},{3,7},{7,3},{8,12},{12,8},{9,1... | collective-permute-start | bytes 663560 | tf_op jit(solution)/shard_map/ppermute | solution.py:282

commit v7 on v6

--- a/solution.py
+++ b/solution.py
@@ -12,7 +12,7 @@
 RIM = REACH + PR
 GROUP = 4
 VMEM_LIMIT = 24 * 1024 * 1024
-STRIP_FLOPS = 10_000_000
+STRIP_FLOPS = 4_000_000_000
 SHIFT_FLOPS = 4_000_000_000
 BLUR_FLOPS = 4_000_000_000
 STACK_FLOPS = 2_000_000_000
@@ -186,6 +186,18 @@
         pieces = cut(select(col_base, kernels[i]))
         for n in range(0, all_cols, 16):
             bc_ref[i, n : n + 16, :] = turned(pieces, n)
+
+
+def edge_kernel(*refs):
+    out_ref = refs[-1]
+    last = jnp.where(lax.axis_index("ty") == 0, jnp.ones((1, 128), jnp.float32), 0.0)
+    first = (1.0 - last).astype(jnp.bfloat16)
+    last = last.astype(jnp.bfloat16)
+    at = 0
+    for ref in refs[:-1]:
+        rows, cols = ref.shape
+        out_ref[at : at + rows, :] = ref[:, :128] * first + ref[:, cols - 128 :] * last
+        at += rows
 
 
 def dot(a, b):
@@ -224,12 +236,12 @@
         for i in range(2):
             at = i * rows
             rim = 16 * i
+            right = [side_tiles[tile_at + at : tile_at + at + rows, :], side_halos[halo_at + rim : halo_at + rim + 128, :]]
             right = [
-                side_tiles[tile_at + at : tile_at + at + rows, :],
-                side_halos[halo_at + rim : halo_at + rim + 128, :],
+                x * side if x.shape[1] == 128 else x[:, :128] * after + x[:, cols - 128 :] * before
+                for x in right
             ]
             right = jnp.concatenate(right, 0)
-            right = right[:, :128] * after + right[:, cols - 128 :] * before
             half = jnp.concatenate([made[j][i], dot(brs[j][i], right).astype(jnp.bfloat16)], 1)
             image = dot(half, widen(bcs[j][i], wide // 128)) * scales[j][i, 0:1, :]
             image = jnp.concatenate([image[:upper], unused, image[upper:]], 0).astype(jnp.bfloat16)
@@ -361,7 +373,10 @@
             scratch=[pltpu.VMEM(shape.shape, jnp.float32), pltpu.SemaphoreType.DMA((hyps,))] if final else [],
         )
 
-    def beside(arrays):
+    def beside(arrays, narrow=False):
+        if narrow and ty == 2:
+            shape = bf16(sum(x.shape[0] for x in arrays), 128)
+            return side_swap(call(edge_kernel, [VMEM] * len(arrays), shape, *arrays, flops=STRIP_FLOPS))
         return side_swap(jnp.concatenate(arrays, 0))
 
     if epochs == slots:
@@ -381,7 +396,7 @@
         total, later, *rest = lax.optimization_barrier((total, later, *[halos[k] for k in taken]))
         rims = [rest[taken.index(k)] for k in range(1, epochs)]
         *blurs, made = blurred(others, rims)
-        return stack(list(range(1, epochs)), made, blurs, later, beside(rims), shifts, total, True)
+        return stack(list(range(1, epochs)), made, blurs, later, beside(rims, True), shifts, total, True)
 
     halos = [halo] + [
         lax.ppermute(halo, "ea", [(i, i ^ k) for i in range(epochs)]) for k in range(1, epochs)

time: 29 us -> 28.7 us (0.990)
  local copies, waits for them, and re-layouts: 1.44 us -> 0.12 us
  waiting for transfers between devices: 1.17 us -> 2.34 us
    ppermute x1, waiting for transfers between devices: 0.46 us -> 1.78 us  [shards(): rim_b = lax.ppermute(strip_b, 'tx', swap_b)]
    unnamed x5 -> x7, local copies, waits for them, and re-layouts: 1.43 us -> 0.11 us
    pallas_call x7 -> x8, Pallas kernels: 8.81 us -> 8.92 us  [call(): pl.pallas_call(kernel, out_shape=shapes, in_specs=specs, out_specs=out if...]
  transfers between devices with their start and end apart: 11 -> 11, of which waited for: 3 -> 3; matrix products, arithmetic and copies ran while one was open for 3% -> 1% of each run, Pallas kernels for 16% -> 16%
where the time goes in v7:
time: 28.7 us; the launch traced here: 28.6 us
  starting transfers between devices  15.9 us (55%)
  Pallas kernels  8.92 us (31%)
  waiting for transfers between devices  2.34 us (8%)
  other arithmetic  1.1 us (4%)
    pallas_call x8, Pallas kernels, call(): pl.pallas_call(kernel, out_shape=shapes, in_specs=specs, out_specs=out if...  8.92 us
    ppermute x3, starting transfers between devices, side_swap(): return lax.ppermute(x, 'ty', [(0, 1), (1, 0)])  5.2 us
    ppermute x3, starting transfers between devices, shards(): lax.ppermute(halo, 'ea', [(i, i ^ k) for i in range(epochs)])  3.68 us
    ppermute x3, starting transfers between devices, shards(): lax.ppermute(own, 'ea', [(i, i ^ k) for i in range(epochs)])  3.67 us
    ppermute x1, starting transfers between devices, shards(): rim_b = lax.ppermute(strip_b, 'tx', swap_b)  2.09 us
    ppermute x1, waiting for transfers between devices, shards(): rim_b = lax.ppermute(strip_b, 'tx', swap_b)  1.78 us
    ppermute x1, starting transfers between devices, shards(): rim_a = lax.ppermute(strip_a, 'tx', swap_a)  1.28 us
    another operation x1, other arithmetic  1.05 us
  transfers between devices with their start and end apart: 11, of which 3 were waited for; matrix products, arithmetic and copies ran while one was open for 1% of the time, Pallas kernels for 16%

profile of v7, /device:TPU:5, one launch (start us, length us, event | category | flops | bytes accessed | tf_op | source)
XLA Modules:
  0.0 28.6 jit_solution(2357307974989423844)
XLA Ops:
  0.0 1.1 %fusion = (bf16[128,256]{1,0:T(8,128)(2,1)S(1)}, bf16[128,256]{1,0:T(8,128)(2,1)S(1)}) fusion(f32[1,128,256]{2,1,0:T(8,128)} %param.5, f32[1,128,256]{2,1,0:T(8,128)} %param.6), kind=kLoop, calls=%fused_computation.4 | loop fusion | flops 98304 | bytes 393216 | tf_op jit(solution)/shard_map/convert
  1.1 0.0 copy-start.2
  1.1 0.0 copy-start
  1.1 2.4 %collective-permute-start.2 = (bf16[256,256]{1,0:T(8,128)(2,1)S(1)}, bf16[256,256]{1,0:T(8,128)(2,1)S(1)}, u32[]{:S(2)}, u32[]{:S(2)}) collective-permute-start(bf16[256,256]{1,0:T(8,128)(2,1)S(1)} %pad_maximum_fusion.2.own_ref.refs_0_), channel_id=1, source_target_pairs={{0,2},{1,3},{2,0},{3,1},{4,6},{5,7},{6,4},{7,5},{8,10},{9,11},{10,... | collective-permute-start | bytes 393224 | tf_op jit(solution)/shard_map/ppermute | solution.py:311
  3.5 1.3 %collective-permute-start.1 = (bf16[256,256]{1,0:T(8,128)(2,1)S(1)}, bf16[256,256]{1,0:T(8,128)(2,1)S(1)}, u32[]{:S(2)}, u32[]{:S(2)}) collective-permute-start(bf16[256,256]{1,0:T(8,128)(2,1)S(1)} %pad_maximum_fusion.2.own_ref.refs_0_), channel_id=1, source_target_pairs={{0,1},{1,0},{2,3},{3,2},{4,5},{5,4},{6,7},{7,6},{8,9},{9,8},{10,11... | collective-permute-start | bytes 393224 | tf_op jit(solution)/shard_map/ppermute | solution.py:311
  4.8 0.0 collective-permute-start
  4.8 1.3 %collective-permute-start.3 = (bf16[72,256]{1,0:T(8,128)(2,1)S(1)}, bf16[72,256]{1,0:T(8,128)(2,1)S(1)}, u32[]{:S(2)}, u32[]{:S(2)}) collective-permute-start(bf16[72,256]{1,0:T(8,128)(2,1)S(1)} %get-tuple-element.41), channel_id=1, source_target_pairs={{0,8},{16,24},{8,0},{24,16},{1,9},{17,25},{9,1},{25,17},{2,10},{18... | collective-permute-start | bytes 110600 | tf_op jit(solution)/shard_map/ppermute | solution.py:326
  6.1 2.1 %collective-permute-start.4 = (bf16[72,256]{1,0:T(8,128)(2,1)S(1)}, bf16[72,256]{1,0:T(8,128)(2,1)S(1)}, u32[]{:S(2)}, u32[]{:S(2)}) collective-permute-start(bf16[72,256]{1,0:T(8,128)(2,1)S(1)} %get-tuple-element.42), channel_id=1, source_target_pairs={{8,16},{16,8},{9,17},{17,9},{10,18},{18,10},{11,19},{19,11},{12,20... | collective-permute-start | bytes 110600 | tf_op jit(solution)/shard_map/ppermute | solution.py:325
  8.2 0.0 copy-done.2
  8.2 0.1 copy.6.speed_ref
  8.3 1.9 %shard_map.55 = (bf16[4,768,256]{2,1,0:T(8,128)(2,1)S(1)}, bf16[6,4,384,128]{3,2,1,0:T(8,128)(2,1)S(1)}) custom-call(s32[1]{0:T(128)} %constant.0.clone.1.base_ref, s32[4]{0:T(128)S(1)} %copy-done, s32[6,2]{1,0:T(8,128)S(1)} %copy.6.speed_ref), custom_call_target="tpu_custom_call" | custom-call | flops 4000000000 | tf_op jit(solution)/shard_map/pallas_call | solution.py:276
  10.2 0.0 collective-permute-done.3.a_ref
  10.2 1.8 %collective-permute-done.4.b_ref = bf16[72,256]{1,0:T(8,128)(2,1)S(1)} collective-permute-done((bf16[72,256]{1,0:T(8,128)(2,1)S(1)}, bf16[72,256]{1,0:T(8,128)(2,1)S(1)}, u32[]{:S(2)}, u32[]{:S(2)}) %collective-permute-start.4) | collective-permute-done | bytes 36896 | tf_op jit(solution)/shard_map/ppermute | solution.py:325
  12.0 1.1 %collective-permute-start.9 = (bf16[144,256]{1,0:T(8,128)(2,1)S(1)}, bf16[144,256]{1,0:T(8,128)(2,1)S(1)}, u32[]{:S(2)}, u32[]{:S(2)}) collective-permute-start(bf16[144,256]{1,0:T(8,128)(2,1)S(1)} %shard_map.57.refs_1_), channel_id=1, source_target_pairs={{0,2},{1,3},{2,0},{3,1},{4,6},{5,7},{6,4},{7,5},{8,10},{9,11},{10,... | collective-permute-start | bytes 221192 | tf_op jit(solution)/shard_map/ppermute | solution.py:386
  13.1 2.3 %collective-permute-start.8 = (bf16[144,256]{1,0:T(8,128)(2,1)S(1)}, bf16[144,256]{1,0:T(8,128)(2,1)S(1)}, u32[]{:S(2)}, u32[]{:S(2)}) collective-permute-start(bf16[144,256]{1,0:T(8,128)(2,1)S(1)} %shard_map.57.refs_1_), channel_id=1, source_target_pairs={{0,3},{1,2},{2,1},{3,0},{4,7},{5,6},{6,5},{7,4},{8,11},{9,10},{10,... | collective-permute-start | bytes 221192 | tf_op jit(solution)/shard_map/ppermute | solution.py:386
  15.4 0.0 collective-permute-done.2.refs_1_
  15.5 0.3 collective-permute-start.7
  15.7 0.0 collective-permute-done.1.refs_0_
  15.7 3.2 %collective-permute-start.5 = (bf16[400,256]{1,0:T(8,128)(2,1)S(1)}, bf16[400,256]{1,0:T(8,128)(2,1)S(1)}, u32[]{:S(2)}, u32[]{:S(2)}) collective-permute-start(bf16[400,256]{1,0:T(8,128)(2,1)S(1)} %pad_maximum_fusion.1), channel_id=1, source_target_pairs={{0,4},{4,0},{1,5},{5,1},{2,6},{6,2},{3,7},{7,3},{8,12},{12,8},{9,1... | collective-permute-start | bytes 614408 | tf_op jit(solution)/shard_map/ppermute | solution.py:294
  18.9 0.0 collective-permute-done.refs_2_
  19.0 0.1 collective-permute-start.6
  19.1 0.5 %shard_map.58 = (bf16[2,192,256]{2,1,0:T(8,128)(2,1)S(1)}, bf16[2,384,128]{2,1,0:T(8,128)(2,1)S(1)}, f32[2,8,384]{2,1,0:T(8,128)S(1)}, bf16[2,192,256]{2,1,0:T(8,128)(2,1)S(1)}) custom-call(bf16[256,256]{1,0:T(8,128)(2,1)S(1)} %pad_maximum_fusion.2.own_ref.refs_0_, bf16[144,256]{1,0:T(8,128)(2,1)S(1)} %shard_map.57.refs_1_), custom_call_target="tpu_custom_call" | custom-call | flops 4000000000 | tf_op jit(solution)/shard_map/pallas_call | solution.py:276
  19.6 0.4 %collective-permute-done.5 = bf16[400,256]{1,0:T(8,128)(2,1)S(1)} collective-permute-done((bf16[400,256]{1,0:T(8,128)(2,1)S(1)}, bf16[400,256]{1,0:T(8,128)(2,1)S(1)}, u32[]{:S(2)}, u32[]{:S(2)}) %collective-permute-start.5) | collective-permute-done | bytes 204832 | tf_op jit(solution)/shard_map/ppermute | solution.py:294
  20.0 1.4 %shard_map.59.refs_16_ = f32[6,256,256]{2,1,0:T(8,128)S(1)} custom-call(bf16[2,192,256]{2,1,0:T(8,128)(2,1)S(1)} %get-tuple-element.44.refs_0_, bf16[2,192,256]{2,1,0:T(8,128)(2,1)S(1)} %get-tuple-element.45.refs_1_, bf16[2,384,128]{2,1,0:T(8,128)(2,1)S(1)} %get-tuple-element.46.refs_2_, f32[2,8,384]{2,1,0:T(8,128)S(1)} %get-tuple-element.47.refs_3_, ...), custom_call_target="tpu_custom_call" | custom-call | flops 2000000000 | tf_op jit(solution)/shard_map/pallas_call | solution.py:276
  21.4 0.0 collective-permute-done.9.refs_4_.refs_1_
  21.4 0.0 collective-permute-done.8.refs_5_.refs_2_
  21.4 0.0 collective-permute-done.7.refs_3_.refs_0_
  21.5 0.0 collective-permute-done.6.refs_12_
  21.5 1.9 %collective-permute-start.10 = (bf16[432,128]{1,0:T(8,128)(2,1)S(1)}, bf16[432,128]{1,0:T(8,128)(2,1)S(1)}, u32[]{:S(2)}, u32[]{:S(2)}) collective-permute-start(bf16[432,128]{1,0:T(8,128)(2,1)S(1)} %shard_map.61), channel_id=1, source_target_pairs={{0,4},{4,0},{1,5},{5,1},{2,6},{6,2},{3,7},{7,3},{8,12},{12,8},{9,1... | collective-permute-start | bytes 331784 | tf_op jit(solution)/shard_map/ppermute | solution.py:294
  23.4 0.8 %shard_map.60 = (bf16[2,192,256]{2,1,0:T(8,128)(2,1)S(1)}, bf16[2,384,128]{2,1,0:T(8,128)(2,1)S(1)}, f32[2,8,384]{2,1,0:T(8,128)S(1)}, bf16[2,192,256]{2,1,0:T(8...) custom-call(bf16[256,256]{1,0:T(8,128)(2,1)S(1)} %collective-permute, ...), custom_call_target="tpu_custom_call" | custom-call | flops 4000000000 | tf_op jit(solution)/shard_map/pallas_call | solution.py:276
  24.3 0.1 collective-permute-done.10.refs_13_
  24.4 4.2 %shard_map.62 = f32[6,128,256]{2,1,0:T(8,128)} custom-call(bf16[2,192,256]{2,1,0:T(8,128)(2,1)S(1)} %get-tuple-element.53.refs_0_, bf16[2,192,256]{2,1,0:T(8,128)(2,1)S(1)} %get-tuple-element.54.refs_1_, bf16[2,192,256]{2,1,0:T(8,128)(2,1)S(1)} %get-tuple-element.55.refs_2_, bf16[2,192,256]{2,1,0:T(8,128)(2,1)S(1)} %get-tuple-element.56.refs_3_, ...), custom_call_target="tpu_custom_call" | custom-call | flops 2000000000 | tf_op jit(solution)/shard_map/pallas_call | solution.py:276
  (11 shorter events, 0.2 us)
Async XLA Ops:
  1.1 7.1 %copy-start.2 = (s32[6,2]{0,1:T(2,128)S(1)}, s32[6,2]{0,1:T(2,128)}, u32[]{:S(2)}) copy-start(s32[6,2]{0,1:T(2,128)} %param.9) | copy-start | bytes 148
  1.1 7.2 %copy-start = (s32[4]{0:T(128)S(1)}, s32[4]{0:T(128)}, u32[]{:S(2)}) copy-start(s32[4]{0:T(128)} %times_ref.1) | copy-start | bytes 52
  1.1 14.3 %collective-permute-start.2 = (bf16[256,256]{1,0:T(8,128)(2,1)S(1)}, bf16[256,256]{1,0:T(8,128)(2,1)S(1)}, u32[]{:S(2)}, u32[]{:S(2)}) collective-permute-start(bf16[256,256]{1,0:T(8,128)(2,1)S(1)} %pad_maximum_fusion.2.own_ref.refs_0_), channel_id=1, source_target_pairs={{0,2},{1,3},{2,0},{3,1},{4,6},{5,7},{6,4},{7,5},{8,10},{9,11},{10,... | collective-permute-start | bytes 393224 | tf_op jit(solution)/shard_map/ppermute | solution.py:311
  3.5 12.3 %collective-permute-start.1 = (bf16[256,256]{1,0:T(8,128)(2,1)S(1)}, bf16[256,256]{1,0:T(8,128)(2,1)S(1)}, u32[]{:S(2)}, u32[]{:S(2)}) collective-permute-start(bf16[256,256]{1,0:T(8,128)(2,1)S(1)} %pad_maximum_fusion.2.own_ref.refs_0_), channel_id=1, source_target_pairs={{0,1},{1,0},{2,3},{3,2},{4,5},{5,4},{6,7},{7,6},{8,9},{9,8},{10,11... | collective-permute-start | bytes 393224 | tf_op jit(solution)/shard_map/ppermute | solution.py:311
  4.8 14.2 %collective-permute-start = (bf16[256,256]{1,0:T(8,128)(2,1)S(1)}, bf16[256,256]{1,0:T(8,128)(2,1)S(1)}, u32[]{:S(2)}, u32[]{:S(2)}) collective-permute-start(bf16[256,256]{1,0:T(8,128)(2,1)S(1)} %pad_maximum_fusion.2.own_ref.refs_0_), channel_id=1, source_target_pairs={{0,3},{1,2},{2,1},{3,0},{4,7},{5,6},{6,5},{7,4},{8,11},{9,10},{10,... | collective-permute-start | bytes 393224 | tf_op jit(solution)/shard_map/ppermute | solution.py:311
  4.8 5.4 %collective-permute-start.3 = (bf16[72,256]{1,0:T(8,128)(2,1)S(1)}, bf16[72,256]{1,0:T(8,128)(2,1)S(1)}, u32[]{:S(2)}, u32[]{:S(2)}) collective-permute-start(bf16[72,256]{1,0:T(8,128)(2,1)S(1)} %get-tuple-element.41), channel_id=1, source_target_pairs={{0,8},{16,24},{8,0},{24,16},{1,9},{17,25},{9,1},{25,17},{2,10},{18... | collective-permute-start | bytes 110600 | tf_op jit(solution)/shard_map/ppermute | solution.py:326
  6.1 5.9 %collective-permute-start.4 = (bf16[72,256]{1,0:T(8,128)(2,1)S(1)}, bf16[72,256]{1,0:T(8,128)(2,1)S(1)}, u32[]{:S(2)}, u32[]{:S(2)}) collective-permute-start(bf16[72,256]{1,0:T(8,128)(2,1)S(1)} %get-tuple-element.42), channel_id=1, source_target_pairs={{8,16},{16,8},{9,17},{17,9},{10,18},{18,10},{11,19},{19,11},{12,20... | collective-permute-start | bytes 110600 | tf_op jit(solution)/shard_map/ppermute | solution.py:325
  8.3 3.7 %copy-start.1 = (f32[1,9]{1,0:T(1,128)S(1)}, f32[1,9]{1,0:T(1,128)}, u32[]{:S(2)}) copy-start(f32[1,9]{1,0:T(1,128)} %taps_ref.1) | copy-start | bytes 112
  12.0 9.4 %collective-permute-start.9 = (bf16[144,256]{1,0:T(8,128)(2,1)S(1)}, bf16[144,256]{1,0:T(8,128)(2,1)S(1)}, u32[]{:S(2)}, u32[]{:S(2)}) collective-permute-start(bf16[144,256]{1,0:T(8,128)(2,1)S(1)} %shard_map.57.refs_1_), channel_id=1, source_target_pairs={{0,2},{1,3},{2,0},{3,1},{4,6},{5,7},{6,4},{7,5},{8,10},{9,11},{10,... | collective-permute-start | bytes 221192 | tf_op jit(solution)/shard_map/ppermute | solution.py:386
  13.1 8.3 %collective-permute-start.8 = (bf16[144,256]{1,0:T(8,128)(2,1)S(1)}, bf16[144,256]{1,0:T(8,128)(2,1)S(1)}, u32[]{:S(2)}, u32[]{:S(2)}) collective-permute-start(bf16[144,256]{1,0:T(8,128)(2,1)S(1)} %shard_map.57.refs_1_), channel_id=1, source_target_pairs={{0,3},{1,2},{2,1},{3,0},{4,7},{5,6},{6,5},{7,4},{8,11},{9,10},{10,... | collective-permute-start | bytes 221192 | tf_op jit(solution)/shard_map/ppermute | solution.py:386
  15.5 6.0 %collective-permute-start.7 = (bf16[144,256]{1,0:T(8,128)(2,1)S(1)}, bf16[144,256]{1,0:T(8,128)(2,1)S(1)}, u32[]{:S(2)}, u32[]{:S(2)}) collective-permute-start(bf16[144,256]{1,0:T(8,128)(2,1)S(1)} %shard_map.57.refs_1_), channel_id=1, source_target_pairs={{0,1},{1,0},{2,3},{3,2},{4,5},{5,4},{6,7},{7,6},{8,9},{9,8},{10,11... | collective-permute-start | bytes 221192 | tf_op jit(solution)/shard_map/ppermute | solution.py:386
  15.7 4.3 %collective-permute-start.5 = (bf16[400,256]{1,0:T(8,128)(2,1)S(1)}, bf16[400,256]{1,0:T(8,128)(2,1)S(1)}, u32[]{:S(2)}, u32[]{:S(2)}) collective-permute-start(bf16[400,256]{1,0:T(8,128)(2,1)S(1)} %pad_maximum_fusion.1), channel_id=1, source_target_pairs={{0,4},{4,0},{1,5},{5,1},{2,6},{6,2},{3,7},{7,3},{8,12},{12,8},{9,1... | collective-permute-start | bytes 614408 | tf_op jit(solution)/shard_map/ppermute | solution.py:294
  19.0 2.5 %collective-permute-start.6 = (bf16[768,256]{1,0:T(8,128)(2,1)S(1)}, bf16[768,256]{1,0:T(8,128)(2,1)S(1)}, u32[]{:S(2)}, u32[]{:S(2)}) collective-permute-start(bf16[768,256]{1,0:T(8,128)(2,1)S(1)} %pad_maximum_fusion), channel_id=1, source_target_pairs={{0,4},{4,0},{1,5},{5,1},{2,6},{6,2},{3,7},{7,3},{8,12},{12,8},{9,1... | collective-permute-start | bytes 1179656 | tf_op jit(solution)/shard_map/ppermute | solution.py:294
  21.5 2.9 %collective-permute-start.10 = (bf16[432,128]{1,0:T(8,128)(2,1)S(1)}, bf16[432,128]{1,0:T(8,128)(2,1)S(1)}, u32[]{:S(2)}, u32[]{:S(2)}) collective-permute-start(bf16[432,128]{1,0:T(8,128)(2,1)S(1)} %shard_map.61), channel_id=1, source_target_pairs={{0,4},{4,0},{1,5},{5,1},{2,6},{6,2},{3,7},{7,3},{8,12},{12,8},{9,1... | collective-permute-start | bytes 331784 | tf_op jit(solution)/shard_map/ppermute | solution.py:294

commit v8 on v7

--- a/solution.py
+++ b/solution.py
@@ -385,7 +385,7 @@
         halos = [halo] + [
             lax.ppermute(halo, "ea", [(i, i ^ k) for i in range(epochs)]) for k in range(1, epochs)
         ]
-        side = beside([own, halo])
+        side = beside([own, halo], True)
         *blurs, made = blurred([own], [halo])
         total = stack([0], made, blurs, side[: own.shape[0]], side[own.shape[0] :], shifts, None, False)
         taken = [3, 1, 2]

time: 28.7 us -> 28.8 us (level)
    pallas_call x8 -> x9, Pallas kernels: 8.92 us -> 9 us  [call(): pl.pallas_call(kernel, out_shape=shapes, in_specs=specs, out_specs=out if...]
  transfers between devices with their start and end apart: 11 -> 11, of which waited for: 3 -> 3; matrix products, arithmetic and copies ran while one was open for 1% -> 0% of each run, Pallas kernels for 16% -> 17%
where the time goes in v8:
time: 28.8 us; the launch traced here: 28.6 us
  starting transfers between devices  16 us (56%)
  Pallas kernels  9 us (31%)
  waiting for transfers between devices  2.21 us (8%)
  other arithmetic  1.09 us (4%)
    pallas_call x9, Pallas kernels, call(): pl.pallas_call(kernel, out_shape=shapes, in_specs=specs, out_specs=out if...  9 us
    ppermute x3, starting transfers between devices, side_swap(): return lax.ppermute(x, 'ty', [(0, 1), (1, 0)])  5.31 us
    ppermute x3, starting transfers between devices, shards(): lax.ppermute(halo, 'ea', [(i, i ^ k) for i in range(epochs)])  3.68 us
    ppermute x3, starting transfers between devices, shards(): lax.ppermute(own, 'ea', [(i, i ^ k) for i in range(epochs)])  3.67 us
    ppermute x1, starting transfers between devices, shards(): rim_b = lax.ppermute(strip_b, 'tx', swap_b)  2.09 us
    ppermute x1, waiting for transfers between devices, shards(): rim_b = lax.ppermute(strip_b, 'tx', swap_b)  1.78 us
    ppermute x1, starting transfers between devices, shards(): rim_a = lax.ppermute(strip_a, 'tx', swap_a)  1.28 us
    another operation x1, other arithmetic  1.05 us
  transfers between devices with their start and end apart: 11, of which 3 were waited for; matrix products, arithmetic and copies ran while one was open for 0% of the time, Pallas kernels for 17%

profile of v8, /device:TPU:5, one launch (start us, length us, event | category | flops | bytes accessed | tf_op | source)
XLA Modules:
  0.0 28.6 jit_solution(6511840794993191080)
XLA Ops:
  0.0 1.1 %fusion = (bf16[128,256]{1,0:T(8,128)(2,1)S(1)}, bf16[128,256]{1,0:T(8,128)(2,1)S(1)}) fusion(f32[1,128,256]{2,1,0:T(8,128)} %param.5, f32[1,128,256]{2,1,0:T(8,128)} %param.6), kind=kLoop, calls=%fused_computation.3 | loop fusion | flops 98304 | bytes 393216 | tf_op jit(solution)/shard_map/convert
  1.1 0.0 copy-start.2
  1.1 0.0 copy-start
  1.1 2.4 %collective-permute-start.2 = (bf16[256,256]{1,0:T(8,128)(2,1)S(1)}, bf16[256,256]{1,0:T(8,128)(2,1)S(1)}, u32[]{:S(2)}, u32[]{:S(2)}) collective-permute-start(bf16[256,256]{1,0:T(8,128)(2,1)S(1)} %pad_maximum_fusion.1.own_ref.refs_0_), channel_id=1, source_target_pairs={{0,2},{1,3},{2,0},{3,1},{4,6},{5,7},{6,4},{7,5},{8,10},{9,11},{10,... | collective-permute-start | bytes 393224 | tf_op jit(solution)/shard_map/ppermute | solution.py:311
  3.5 1.3 %collective-permute-start.1 = (bf16[256,256]{1,0:T(8,128)(2,1)S(1)}, bf16[256,256]{1,0:T(8,128)(2,1)S(1)}, u32[]{:S(2)}, u32[]{:S(2)}) collective-permute-start(bf16[256,256]{1,0:T(8,128)(2,1)S(1)} %pad_maximum_fusion.1.own_ref.refs_0_), channel_id=1, source_target_pairs={{0,1},{1,0},{2,3},{3,2},{4,5},{5,4},{6,7},{7,6},{8,9},{9,8},{10,11... | collective-permute-start | bytes 393224 | tf_op jit(solution)/shard_map/ppermute | solution.py:311
  4.8 0.0 collective-permute-start
  4.8 1.3 %collective-permute-start.3 = (bf16[72,256]{1,0:T(8,128)(2,1)S(1)}, bf16[72,256]{1,0:T(8,128)(2,1)S(1)}, u32[]{:S(2)}, u32[]{:S(2)}) collective-permute-start(bf16[72,256]{1,0:T(8,128)(2,1)S(1)} %get-tuple-element.41), channel_id=1, source_target_pairs={{0,8},{16,24},{8,0},{24,16},{1,9},{17,25},{9,1},{25,17},{2,10},{18... | collective-permute-start | bytes 110600 | tf_op jit(solution)/shard_map/ppermute | solution.py:326
  6.1 2.1 %collective-permute-start.4 = (bf16[72,256]{1,0:T(8,128)(2,1)S(1)}, bf16[72,256]{1,0:T(8,128)(2,1)S(1)}, u32[]{:S(2)}, u32[]{:S(2)}) collective-permute-start(bf16[72,256]{1,0:T(8,128)(2,1)S(1)} %get-tuple-element.42), channel_id=1, source_target_pairs={{8,16},{16,8},{9,17},{17,9},{10,18},{18,10},{11,19},{19,11},{12,20... | collective-permute-start | bytes 110600 | tf_op jit(solution)/shard_map/ppermute | solution.py:325
  8.2 0.0 copy-done.2
  8.2 0.1 copy.6.speed_ref
  8.3 1.9 %shard_map.55 = (bf16[4,768,256]{2,1,0:T(8,128)(2,1)S(1)}, bf16[6,4,384,128]{3,2,1,0:T(8,128)(2,1)S(1)}) custom-call(s32[1]{0:T(128)} %constant.0.clone.1.base_ref, s32[4]{0:T(128)S(1)} %copy-done, s32[6,2]{1,0:T(8,128)S(1)} %copy.6.speed_ref), custom_call_target="tpu_custom_call" | custom-call | flops 4000000000 | tf_op jit(solution)/shard_map/pallas_call | solution.py:276
  10.2 0.0 collective-permute-done.3.a_ref
  10.2 1.8 %collective-permute-done.4.b_ref = bf16[72,256]{1,0:T(8,128)(2,1)S(1)} collective-permute-done((bf16[72,256]{1,0:T(8,128)(2,1)S(1)}, bf16[72,256]{1,0:T(8,128)(2,1)S(1)}, u32[]{:S(2)}, u32[]{:S(2)}) %collective-permute-start.4) | collective-permute-done | bytes 36896 | tf_op jit(solution)/shard_map/ppermute | solution.py:325
  12.0 1.1 %collective-permute-start.9 = (bf16[144,256]{1,0:T(8,128)(2,1)S(1)}, bf16[144,256]{1,0:T(8,128)(2,1)S(1)}, u32[]{:S(2)}, u32[]{:S(2)}) collective-permute-start(bf16[144,256]{1,0:T(8,128)(2,1)S(1)} %shard_map.57.refs_1_), channel_id=1, source_target_pairs={{0,2},{1,3},{2,0},{3,1},{4,6},{5,7},{6,4},{7,5},{8,10},{9,11},{10,... | collective-permute-start | bytes 221192 | tf_op jit(solution)/shard_map/ppermute | solution.py:386
  13.1 2.3 %collective-permute-start.8 = (bf16[144,256]{1,0:T(8,128)(2,1)S(1)}, bf16[144,256]{1,0:T(8,128)(2,1)S(1)}, u32[]{:S(2)}, u32[]{:S(2)}) collective-permute-start(bf16[144,256]{1,0:T(8,128)(2,1)S(1)} %shard_map.57.refs_1_), channel_id=1, source_target_pairs={{0,3},{1,2},{2,1},{3,0},{4,7},{5,6},{6,5},{7,4},{8,11},{9,10},{10,... | collective-permute-start | bytes 221192 | tf_op jit(solution)/shard_map/ppermute | solution.py:386
  15.5 0.0 collective-permute-done.2.refs_1_
  15.5 0.3 collective-permute-start.7
  15.7 0.0 collective-permute-done.1.refs_0_
  15.8 3.2 %collective-permute-start.5 = (bf16[400,128]{1,0:T(8,128)(2,1)S(1)}, bf16[400,128]{1,0:T(8,128)(2,1)S(1)}, u32[]{:S(2)}, u32[]{:S(2)}) collective-permute-start(bf16[400,128]{1,0:T(8,128)(2,1)S(1)} %shard_map.59), channel_id=1, source_target_pairs={{0,4},{4,0},{1,5},{5,1},{2,6},{6,2},{3,7},{7,3},{8,12},{12,8},{9,1... | collective-permute-start | bytes 307208 | tf_op jit(solution)/shard_map/ppermute | solution.py:294
  19.0 0.0 collective-permute-done.refs_2_
  19.0 0.1 collective-permute-start.6
  19.1 0.5 %shard_map.58 = (bf16[2,192,256]{2,1,0:T(8,128)(2,1)S(1)}, bf16[2,384,128]{2,1,0:T(8,128)(2,1)S(1)}, f32[2,8,384]{2,1,0:T(8,128)S(1)}, bf16[2,192,256]{2,1,0:T(8,128)(2,1)S(1)}) custom-call(bf16[256,256]{1,0:T(8,128)(2,1)S(1)} %pad_maximum_fusion.1.own_ref.refs_0_, bf16[144,256]{1,0:T(8,128)(2,1)S(1)} %shard_map.57.refs_1_), custom_call_target="tpu_custom_call" | custom-call | flops 4000000000 | tf_op jit(solution)/shard_map/pallas_call | solution.py:276
  19.6 0.3 %collective-permute-done.5 = bf16[400,128]{1,0:T(8,128)(2,1)S(1)} collective-permute-done((bf16[400,128]{1,0:T(8,128)(2,1)S(1)}, bf16[400,128]{1,0:T(8,128)(2,1)S(1)}, u32[]{:S(2)}, u32[]{:S(2)}) %collective-permute-start.5) | collective-permute-done | bytes 102432 | tf_op jit(solution)/shard_map/ppermute | solution.py:294
  19.9 1.4 %shard_map.60.refs_16_ = f32[6,256,256]{2,1,0:T(8,128)S(1)} custom-call(bf16[2,192,256]{2,1,0:T(8,128)(2,1)S(1)} %get-tuple-element.44.refs_0_, bf16[2,192,256]{2,1,0:T(8,128)(2,1)S(1)} %get-tuple-element.45.refs_1_, bf16[2,384,128]{2,1,0:T(8,128)(2,1)S(1)} %get-tuple-element.46.refs_2_, f32[2,8,384]{2,1,0:T(8,128)S(1)} %get-tuple-element.47.refs_3_, ...), custom_call_target="tpu_custom_call" | custom-call | flops 2000000000 | tf_op jit(solution)/shard_map/pallas_call | solution.py:276
  21.3 0.0 collective-permute-done.9.refs_4_.refs_1_
  21.3 0.0 collective-permute-done.8.refs_5_.refs_2_
  21.3 0.0 collective-permute-done.7.refs_3_.refs_0_
  21.3 0.0 collective-permute-done.6.refs_12_
  21.4 2.0 %collective-permute-start.10 = (bf16[432,128]{1,0:T(8,128)(2,1)S(1)}, bf16[432,128]{1,0:T(8,128)(2,1)S(1)}, u32[]{:S(2)}, u32[]{:S(2)}) collective-permute-start(bf16[432,128]{1,0:T(8,128)(2,1)S(1)} %shard_map.62), channel_id=1, source_target_pairs={{0,4},{4,0},{1,5},{5,1},{2,6},{6,2},{3,7},{7,3},{8,12},{12,8},{9,1... | collective-permute-start | bytes 331784 | tf_op jit(solution)/shard_map/ppermute | solution.py:294
  23.4 0.8 %shard_map.61 = (bf16[2,192,256]{2,1,0:T(8,128)(2,1)S(1)}, bf16[2,384,128]{2,1,0:T(8,128)(2,1)S(1)}, f32[2,8,384]{2,1,0:T(8,128)S(1)}, bf16[2,192,256]{2,1,0:T(8...) custom-call(bf16[256,256]{1,0:T(8,128)(2,1)S(1)} %collective-permute, ...), custom_call_target="tpu_custom_call" | custom-call | flops 4000000000 | tf_op jit(solution)/shard_map/pallas_call | solution.py:276
  24.3 0.1 collective-permute-done.10.refs_13_
  24.4 4.2 %shard_map.63 = f32[6,128,256]{2,1,0:T(8,128)} custom-call(bf16[2,192,256]{2,1,0:T(8,128)(2,1)S(1)} %get-tuple-element.53.refs_0_, bf16[2,192,256]{2,1,0:T(8,128)(2,1)S(1)} %get-tuple-element.54.refs_1_, bf16[2,192,256]{2,1,0:T(8,128)(2,1)S(1)} %get-tuple-element.55.refs_2_, bf16[2,192,256]{2,1,0:T(8,128)(2,1)S(1)} %get-tuple-element.56.refs_3_, ...), custom_call_target="tpu_custom_call" | custom-call | flops 2000000000 | tf_op jit(solution)/shard_map/pallas_call | solution.py:276
  (11 shorter events, 0.2 us)
Async XLA Ops:
  1.1 7.1 %copy-start.2 = (s32[6,2]{0,1:T(2,128)S(1)}, s32[6,2]{0,1:T(2,128)}, u32[]{:S(2)}) copy-start(s32[6,2]{0,1:T(2,128)} %param.9) | copy-start | bytes 148
  1.1 7.2 %copy-start = (s32[4]{0:T(128)S(1)}, s32[4]{0:T(128)}, u32[]{:S(2)}) copy-start(s32[4]{0:T(128)} %times_ref.1) | copy-start | bytes 52
  1.1 14.4 %collective-permute-start.2 = (bf16[256,256]{1,0:T(8,128)(2,1)S(1)}, bf16[256,256]{1,0:T(8,128)(2,1)S(1)}, u32[]{:S(2)}, u32[]{:S(2)}) collective-permute-start(bf16[256,256]{1,0:T(8,128)(2,1)S(1)} %pad_maximum_fusion.1.own_ref.refs_0_), channel_id=1, source_target_pairs={{0,2},{1,3},{2,0},{3,1},{4,6},{5,7},{6,4},{7,5},{8,10},{9,11},{10,... | collective-permute-start | bytes 393224 | tf_op jit(solution)/shard_map/ppermute | solution.py:311
  3.5 12.3 %collective-permute-start.1 = (bf16[256,256]{1,0:T(8,128)(2,1)S(1)}, bf16[256,256]{1,0:T(8,128)(2,1)S(1)}, u32[]{:S(2)}, u32[]{:S(2)}) collective-permute-start(bf16[256,256]{1,0:T(8,128)(2,1)S(1)} %pad_maximum_fusion.1.own_ref.refs_0_), channel_id=1, source_target_pairs={{0,1},{1,0},{2,3},{3,2},{4,5},{5,4},{6,7},{7,6},{8,9},{9,8},{10,11... | collective-permute-start | bytes 393224 | tf_op jit(solution)/shard_map/ppermute | solution.py:311
  4.8 14.2 %collective-permute-start = (bf16[256,256]{1,0:T(8,128)(2,1)S(1)}, bf16[256,256]{1,0:T(8,128)(2,1)S(1)}, u32[]{:S(2)}, u32[]{:S(2)}) collective-permute-start(bf16[256,256]{1,0:T(8,128)(2,1)S(1)} %pad_maximum_fusion.1.own_ref.refs_0_), channel_id=1, source_target_pairs={{0,3},{1,2},{2,1},{3,0},{4,7},{5,6},{6,5},{7,4},{8,11},{9,10},{10,... | collective-permute-start | bytes 393224 | tf_op jit(solution)/shard_map/ppermute | solution.py:311
  4.8 5.4 %collective-permute-start.3 = (bf16[72,256]{1,0:T(8,128)(2,1)S(1)}, bf16[72,256]{1,0:T(8,128)(2,1)S(1)}, u32[]{:S(2)}, u32[]{:S(2)}) collective-permute-start(bf16[72,256]{1,0:T(8,128)(2,1)S(1)} %get-tuple-element.41), channel_id=1, source_target_pairs={{0,8},{16,24},{8,0},{24,16},{1,9},{17,25},{9,1},{25,17},{2,10},{18... | collective-permute-start | bytes 110600 | tf_op jit(solution)/shard_map/ppermute | solution.py:326
  6.1 5.9 %collective-permute-start.4 = (bf16[72,256]{1,0:T(8,128)(2,1)S(1)}, bf16[72,256]{1,0:T(8,128)(2,1)S(1)}, u32[]{:S(2)}, u32[]{:S(2)}) collective-permute-start(bf16[72,256]{1,0:T(8,128)(2,1)S(1)} %get-tuple-element.42), channel_id=1, source_target_pairs={{8,16},{16,8},{9,17},{17,9},{10,18},{18,10},{11,19},{19,11},{12,20... | collective-permute-start | bytes 110600 | tf_op jit(solution)/shard_map/ppermute | solution.py:325
  8.3 3.7 %copy-start.1 = (f32[1,9]{1,0:T(1,128)S(1)}, f32[1,9]{1,0:T(1,128)}, u32[]{:S(2)}) copy-start(f32[1,9]{1,0:T(1,128)} %taps_ref.1) | copy-start | bytes 112
  12.0 9.3 %collective-permute-start.9 = (bf16[144,256]{1,0:T(8,128)(2,1)S(1)}, bf16[144,256]{1,0:T(8,128)(2,1)S(1)}, u32[]{:S(2)}, u32[]{:S(2)}) collective-permute-start(bf16[144,256]{1,0:T(8,128)(2,1)S(1)} %shard_map.57.refs_1_), channel_id=1, source_target_pairs={{0,2},{1,3},{2,0},{3,1},{4,6},{5,7},{6,4},{7,5},{8,10},{9,11},{10,... | collective-permute-start | bytes 221192 | tf_op jit(solution)/shard_map/ppermute | solution.py:386
  13.1 8.2 %collective-permute-start.8 = (bf16[144,256]{1,0:T(8,128)(2,1)S(1)}, bf16[144,256]{1,0:T(8,128)(2,1)S(1)}, u32[]{:S(2)}, u32[]{:S(2)}) collective-permute-start(bf16[144,256]{1,0:T(8,128)(2,1)S(1)} %shard_map.57.refs_1_), channel_id=1, source_target_pairs={{0,3},{1,2},{2,1},{3,0},{4,7},{5,6},{6,5},{7,4},{8,11},{9,10},{10,... | collective-permute-start | bytes 221192 | tf_op jit(solution)/shard_map/ppermute | solution.py:386
  15.5 5.9 %collective-permute-start.7 = (bf16[144,256]{1,0:T(8,128)(2,1)S(1)}, bf16[144,256]{1,0:T(8,128)(2,1)S(1)}, u32[]{:S(2)}, u32[]{:S(2)}) collective-permute-start(bf16[144,256]{1,0:T(8,128)(2,1)S(1)} %shard_map.57.refs_1_), channel_id=1, source_target_pairs={{0,1},{1,0},{2,3},{3,2},{4,5},{5,4},{6,7},{7,6},{8,9},{9,8},{10,11... | collective-permute-start | bytes 221192 | tf_op jit(solution)/shard_map/ppermute | solution.py:386
  15.8 4.2 %collective-permute-start.5 = (bf16[400,128]{1,0:T(8,128)(2,1)S(1)}, bf16[400,128]{1,0:T(8,128)(2,1)S(1)}, u32[]{:S(2)}, u32[]{:S(2)}) collective-permute-start(bf16[400,128]{1,0:T(8,128)(2,1)S(1)} %shard_map.59), channel_id=1, source_target_pairs={{0,4},{4,0},{1,5},{5,1},{2,6},{6,2},{3,7},{7,3},{8,12},{12,8},{9,1... | collective-permute-start | bytes 307208 | tf_op jit(solution)/shard_map/ppermute | solution.py:294
  19.0 2.4 %collective-permute-start.6 = (bf16[768,256]{1,0:T(8,128)(2,1)S(1)}, bf16[768,256]{1,0:T(8,128)(2,1)S(1)}, u32[]{:S(2)}, u32[]{:S(2)}) collective-permute-start(bf16[768,256]{1,0:T(8,128)(2,1)S(1)} %pad_maximum_fusion), channel_id=1, source_target_pairs={{0,4},{4,0},{1,5},{5,1},{2,6},{6,2},{3,7},{7,3},{8,12},{12,8},{9,1... | collective-permute-start | bytes 1179656 | tf_op jit(solution)/shard_map/ppermute | solution.py:294
  21.4 3.0 %collective-permute-start.10 = (bf16[432,128]{1,0:T(8,128)(2,1)S(1)}, bf16[432,128]{1,0:T(8,128)(2,1)S(1)}, u32[]{:S(2)}, u32[]{:S(2)}) collective-permute-start(bf16[432,128]{1,0:T(8,128)(2,1)S(1)} %shard_map.62), channel_id=1, source_target_pairs={{0,4},{4,0},{1,5},{5,1},{2,6},{6,2},{3,7},{7,3},{8,12},{12,8},{9,1... | collective-permute-start | bytes 331784 | tf_op jit(solution)/shard_map/ppermute | solution.py:294
